TPU v7x, 32 devices: a whole 2x2x4 slice. The times are simulated.
32 devices in a mesh: section: 8 (over z, core), seq: 4 (over y, x).
Axes of the slice: x: 2, y: 2, z: 4, core: 2. Of those that a mesh axis runs over, the one named last changes fastest.
Arguments:
- layer_input: bfloat16 [8, 3, 4096, 768], P('section', None, 'seq'), may hold values from -6 to 6
- grad_out: bfloat16 [8, 3, 4096, 768], P('section', None, 'seq'), may hold values from -6 to 6
- gate_weight: bfloat16 [768, 768], P('seq'), may hold values from -0.21875 to 0.21875
- mix_in_right: bfloat16 [64, 64, 64], P('seq'), may hold values from -0.75 to 0.75
- mix_in_left: bfloat16 [64, 64, 64], P('seq'), may hold values from -0.75 to 0.75
- mix_out_left: bfloat16 [64, 64, 64], P('seq'), may hold values from -0.75 to 0.75
- mix_out_right: bfloat16 [64, 64, 64], P('seq'), may hold values from -0.75 to 0.75
- kernel: bfloat16 [4096, 768], P('seq'), may hold values from -5 to 5
Outputs:
- input_grad: bfloat16 [8, 3, 4096, 768], P('section', None, 'seq')
- weight_grad: float32 [768, 768], P('seq')
- kernel_grad: bfloat16 [4096, 768], P('seq')
All inputs are finite; a program needn't handle non-finite values.
Results may differ from a plain program's by a relative error of at most 0.007.
Values may be sent and summed in bfloat16 or wider, within the bound.
No kernel may reach another device: no remote copies, remote signals or barrier semaphores. Data moves between devices by JAX's collectives and lax.ppermute only.
A program may use at most 128 MiB of HBM per device.

v0:
```python
import functools
import math

import jax
import jax.numpy as jnp
from jax import lax
from jax.experimental import pallas as pl
from jax.experimental.pallas import tpu as pltpu
from jax.sharding import PartitionSpec as P

BATCH = 3
SEQ = 4096
HALF = 8

BF16 = jnp.bfloat16
F32 = jnp.float32


def contract(form, left, right):
    return jnp.einsum(form, left, right, preferred_element_type=jnp.float32)


def dot(left, right):
    return jnp.dot(left, right, preferred_element_type=F32)


def dot_first(left, right):
    return lax.dot_general(left, right, (((0,), (0,)), ((), ())), preferred_element_type=F32)


def dot_last(left, right):
    return lax.dot_general(left, right, (((1,), (1,)), ((), ())), preferred_element_type=F32)


def params(grid):
    return pltpu.CompilerParams(
        dimension_semantics=("arbitrary",) * len(grid), vmem_limit_bytes=56 * 1024 * 1024
    )


def cost(flops, bytes_accessed):
    return pl.CostEstimate(flops=int(flops), bytes_accessed=int(bytes_accessed), transcendentals=0)


def put_pair(outs, where, low, first, second, own):
    for r, out in enumerate(outs):
        for g in range(own // HALF):
            at = r * own + g * HALF
            rows = jnp.concatenate([first[at : at + HALF], second[at : at + HALF]], axis=0)
            out[where, g, low : low + 2 * HALF, :] = rows.astype(BF16)


def expand_kernel(devices, left_in, left_out, right_in, right_out, *outs):
    big_li, big_qo, big_pt, big_rt, small_qt, small_lt = outs
    own, block = left_in.shape[0], left_in.shape[1]
    wide = block * HALF
    s = lax.broadcasted_iota(jnp.int32, (block, wide), 0)
    lane = lax.broadcasted_iota(jnp.int32, (block, wide), 1)
    picks = [
        jnp.where(lane == s * HALF + t, 1.0, 0.0).astype(BF16) for t in range(HALF)
    ]
    row = lax.broadcasted_iota(jnp.int32, (block, block), 0)
    column = lax.broadcasted_iota(jnp.int32, (block, block), 1)
    same = jnp.where(row == column, 1.0, 0.0).astype(BF16)
    for p in range(own):
        g, t = divmod(p, HALF)
        rows = slice(t * block, (t + 1) * block)
        big_li[g, rows, :] = dot(left_in[p], picks[t]).astype(BF16)
        big_qo[g, rows, :] = dot(right_out[p], picks[t]).astype(BF16)
        big_pt[g, rows, :] = dot_first(left_out[p], picks[t]).astype(BF16)
        big_rt[g, rows, :] = dot_first(right_in[p], picks[t]).astype(BF16)
        small_qt[p] = dot_last(same, right_out[p]).astype(BF16)
        small_lt[p] = dot_last(same, left_in[p]).astype(BF16)


def expand(devices, left_in, left_out, right_in, right_out):
    own, block = left_in.shape[0], left_in.shape[1]
    big = jax.ShapeDtypeStruct((own // HALF, HALF * block, HALF * block), BF16)
    small = jax.ShapeDtypeStruct(left_in.shape, BF16)
    return pl.pallas_call(
        functools.partial(expand_kernel, devices),
        out_shape=(big,) * 4 + (small,) * 2,
        compiler_params=params(()),
        cost_estimate=cost(4e9, 8e6),
    )(left_in, left_out, right_in, right_out)


def first_kernel(devices, right_in, acts, *outs):
    own = right_in.shape[0]
    for p in range(0, own, 2):
        put_pair(
            outs, 0, p * HALF, dot(right_in[p], acts[0, p]), dot(right_in[p + 1], acts[0, p + 1]), own
        )


def first(devices, c, width, right_in, acts):
    batch, own, block, _ = acts.shape
    piece = jax.ShapeDtypeStruct((batch, own // HALF, own * HALF, width), BF16)
    grid = (batch,)
    return pl.pallas_call(
        functools.partial(first_kernel, devices),
        grid=grid,
        in_specs=[
            pl.BlockSpec(right_in.shape, lambda b: (0, 0, 0)),
            pl.BlockSpec((1, own, block, width), lambda b: (b, 0, 0, c)),
        ],
        out_specs=[pl.BlockSpec((1,) + piece.shape[1:], lambda b: (b, 0, 0, 0))] * devices,
        out_shape=(piece,) * devices,
        compiler_params=params(grid),
        cost_estimate=cost(2 * batch * own * block * block * width, 4 * batch * own * block * width),
    )(right_in, acts)


def middle_kernel(devices, small, big, kern, *refs):
    pieces, outs, second = refs[:devices], refs[devices:-1], refs[-1]
    half, block = small.shape[0], small.shape[1]
    own = block // devices
    scale = kern[0].astype(F32)
    for b in range(second.shape[0]):
        spread = jnp.concatenate([piece[b, 0] for piece in pieces], axis=0)
        value = dot(big[0], spread)
        second[b, 0] = value
        weighted = (value * scale).astype(BF16)
        for i in range(0, half, 2):
            low = dot(small[i], weighted[i * block : (i + 1) * block])
            high = dot(small[i + 1], weighted[(i + 1) * block : (i + 2) * block])
            put_pair(outs, b, i * HALF, low, high, own)


def middle(devices, c, width, small, big, kern, pieces):
    batch, parts, long, _ = pieces[0].shape
    block = small.shape[1]
    piece = jax.ShapeDtypeStruct(pieces[0].shape, BF16)
    second = jax.ShapeDtypeStruct((batch, parts, HALF * block, width), F32)
    grid = (parts,)
    return pl.pallas_call(
        functools.partial(middle_kernel, devices),
        grid=grid,
        in_specs=[
            pl.BlockSpec((HALF, block, block), lambda g: (g, 0, 0)),
            pl.BlockSpec((1,) + big.shape[1:], lambda g: (g, 0, 0)),
            pl.BlockSpec((1, HALF * block, width), lambda g: (g, 0, c)),
        ]
        + [pl.BlockSpec((batch, 1, long, width), lambda g: (0, g, 0, 0))] * devices,
        out_specs=[pl.BlockSpec((batch, parts, HALF * HALF, width), lambda g: (0, 0, g, 0))] * devices
        + [pl.BlockSpec((batch, 1, HALF * block, width), lambda g: (0, g, 0, 0))],
        out_shape=(piece,) * devices + (second,),
        compiler_params=params(grid),
        cost_estimate=cost(3e9, 8e6),
    )(small, big, kern, *pieces)


def back_middle_kernel(devices, small, big, kern, second, *refs):
    pieces, outs, total = refs[:devices], refs[devices:-1], refs[-1]
    half, block = small.shape[0], small.shape[1]
    own = block // devices
    scale = kern[0].astype(F32)
    tally = None
    for b in range(second.shape[0]):
        spread = jnp.concatenate([piece[b, 0] for piece in pieces], axis=0)
        value = dot(big[0], spread)
        term = second[b, 0] * value
        tally = term if tally is None else tally + term
        weighted = (value * scale).astype(BF16)
        for i in range(0, half, 2):
            low = dot(small[i], weighted[i * block : (i + 1) * block])
            high = dot(small[i + 1], weighted[(i + 1) * block : (i + 2) * block])
            put_pair(outs, b, i * HALF, low, high, own)
    total[0] = tally


def back_middle(devices, c, width, small, big, kern, second, pieces):
    batch, parts, long, _ = pieces[0].shape
    block = small.shape[1]
    piece = jax.ShapeDtypeStruct(pieces[0].shape, BF16)
    total = jax.ShapeDtypeStruct((parts, HALF * block, width), F32)
    grid = (parts,)
    return pl.pallas_call(
        functools.partial(back_middle_kernel, devices),
        grid=grid,
        in_specs=[
            pl.BlockSpec((HALF, block, block), lambda g: (g, 0, 0)),
            pl.BlockSpec((1,) + big.shape[1:], lambda g: (g, 0, 0)),
            pl.BlockSpec((1, HALF * block, width), lambda g: (g, 0, c)),
            pl.BlockSpec((batch, 1, HALF * block, width), lambda g: (0, g, 0, 0)),
        ]
        + [pl.BlockSpec((batch, 1, long, width), lambda g: (0, g, 0, 0))] * devices,
        out_specs=[pl.BlockSpec((batch, parts, HALF * HALF, width), lambda g: (0, 0, g, 0))] * devices
        + [pl.BlockSpec((1, HALF * block, width), lambda g: (g, 0, 0))],
        out_shape=(piece,) * devices + (total,),
        compiler_params=params(grid),
        cost_estimate=cost(3e9, 8e6),
    )(small, big, kern, second, *pieces)


def gate_kernel(devices, small, weights, flat, upstream, *refs):
    outs, sloped = refs[:devices], refs[devices]
    count, block = small.shape[0], small.shape[1]
    own = block // devices
    preact = dot(flat[0], weights[...].astype(BF16))
    sigma = jax.nn.sigmoid(preact)
    swish = preact * sigma
    slope = sigma * (1.0 + preact * (1.0 - sigma))
    grad = upstream[0].astype(F32)
    sloped[0] = grad * slope
    mix_grad = (grad * swish).astype(BF16)
    for k in range(0, count, 2):
        low = dot(small[k], mix_grad[k * block : (k + 1) * block])
        high = dot(small[k + 1], mix_grad[(k + 1) * block : (k + 2) * block])
        put_pair(outs, 0, k * HALF, low, high, own)


def gate(devices, c, width, small, weights, flat, upstream):
    batch, rows, full = flat.shape
    own, block = small.shape[0], small.shape[1]
    count = 4
    piece = jax.ShapeDtypeStruct((batch, own // HALF, own * HALF, width), BF16)
    sloped = jax.ShapeDtypeStruct((batch, rows, width), F32)
    grid = (batch, own // count)
    return pl.pallas_call(
        functools.partial(gate_kernel, devices),
        grid=grid,
        in_specs=[
            pl.BlockSpec((count, block, block), lambda b, q: (q, 0, 0)),
            pl.BlockSpec((full, width), lambda b, q: (0, c)),
            pl.BlockSpec((1, count * block, full), lambda b, q: (b, q, 0)),
            pl.BlockSpec((1, count * block, width), lambda b, q: (b, q, c)),
        ],
        out_specs=[
            pl.BlockSpec((1, own // HALF, count * HALF, width), lambda b, q: (b, 0, q, 0))
        ]
        * devices
        + [pl.BlockSpec((1, count * block, width), lambda b, q: (b, q, 0))],
        out_shape=(piece,) * devices + (sloped,),
        compiler_params=params(grid),
        cost_estimate=cost(2 * batch * rows * full * width, 12e6),
    )(small, weights, flat, upstream)


def outer_kernel(devices, add, big, other, *refs):
    pieces, out = refs[:devices], refs[-1]
    spread = jnp.concatenate([piece[0, 0] for piece in pieces], axis=0)
    value = dot(big[0], spread)
    out[0] = (value + other[0] if add else value * other[0]).astype(BF16)


def outer(devices, c, width, add, big, other, before, pieces):
    batch, parts, long, _ = pieces[0].shape
    rows = big.shape[1]
    place = 0 if other.shape[2] == width else c
    full = before[0] if isinstance(before, tuple) else before.shape[2]
    grid = (parts, batch)
    operands = [big, other, *pieces]
    specs = [
        pl.BlockSpec((1,) + big.shape[1:], lambda g, b: (g, 0, 0)),
        pl.BlockSpec((1, rows, width), lambda g, b: (b, g, place)),
    ] + [pl.BlockSpec((1, 1, long, width), lambda g, b: (b, g, 0, 0))] * devices
    alias = {}
    if not isinstance(before, tuple):
        alias = {len(operands): 0}
        operands.append(before)
        specs.append(pl.BlockSpec(memory_space=pl.ANY))
    return pl.pallas_call(
        functools.partial(outer_kernel, devices, add),
        grid=grid,
        in_specs=specs,
        out_specs=pl.BlockSpec((1, rows, width), lambda g, b: (b, g, c)),
        out_shape=jax.ShapeDtypeStruct((batch, parts * rows, full), BF16),
        input_output_aliases=alias,
        compiler_params=params(grid),
        cost_estimate=cost(3e9, 6e6),
    )(*operands)


def swap(value, axis, bit):
    size = lax.axis_size(axis)
    return lax.ppermute(value, axis, [(i, i ^ bit) for i in range(size)])


def exchange(pieces):
    size = len(pieces)
    order = [size - 1, *range(1, size - 1)] if size > 1 else []
    moved = {r: swap(pieces[r], "seq", r) for r in order}
    return [pieces[0]] + [moved[r] for r in range(1, size)]


def bits_of(size):
    return [1 << k for k in range(size.bit_length() - 1)]


def has(axis, bit):
    return (lax.axis_index(axis) // bit) % 2


def halve(value, axis, bit, dim, kind):
    half = value.shape[dim] // 2
    mine = has(axis, bit)
    keep = lax.dynamic_slice_in_dim(value, mine * half, half, dim)
    send = lax.dynamic_slice_in_dim(value, (1 - mine) * half, half, dim)
    return keep + swap(send.astype(kind), axis, bit).astype(F32)


def double(value, axis, bit, dim):
    other = swap(value, axis, bit)
    mine = has(axis, bit)
    return jnp.where(
        mine == 0,
        jnp.concatenate([value, other], axis=dim),
        jnp.concatenate([other, value], axis=dim),
    )


def by_peer(value, dim):
    devices = lax.axis_size("seq")
    shape = value.shape
    for bit in bits_of(devices):
        pairs = value.reshape(
            *shape[:dim], devices // (2 * bit), 2, bit * shape[dim] // devices, *shape[dim + 1 :]
        )
        turned = jnp.flip(pairs, axis=dim + 1)
        value = jnp.where(has("seq", bit) == 0, pairs, turned).reshape(shape)
    return value


def gather_weights(gate_weight):
    devices = lax.axis_size("seq")
    sections = lax.axis_size("section")
    rows, width = gate_weight.shape
    shared = [bit for bit in (2, 1) if bit < sections and rows % (4 * 16) == 0]
    part = rows // (1 << len(shared))
    place = sum(has("section", bit) * bit for bit in shared)
    mine = lax.dynamic_slice_in_dim(gate_weight, place * part, part, 0).astype(F32)
    got = jnp.stack([mine] + [swap(mine, "seq", r) for r in range(1, devices)])
    got = by_peer(got, 0)
    if shared:
        got = double(got, "section", 1, 1)
        got = double(got, "section", 2, 1)
    return got.reshape(devices * rows, width)


def local(
    layer_input,
    grad_out,
    gate_weight,
    mix_in_right,
    mix_in_left,
    mix_out_left,
    mix_out_right,
    kernel,
):
    batch, rows, full = layer_input.shape[1:]
    own, block = mix_in_right.shape[0], mix_in_right.shape[1]
    replicas = lax.axis_size("section")
    devices = lax.axis_size("seq")
    weight_scale = 1.0 / math.sqrt(replicas * BATCH * SEQ)
    kernel_scale = 1.0 / math.sqrt(replicas * BATCH)
    chunks = 3
    width = full // chunks
    flat = layer_input[0]
    upstream = grad_out[0]
    acts = flat.reshape(batch, own, block, full)
    kern = kernel.reshape(own // HALF, HALF * block, full)

    weights = gather_weights(gate_weight)
    small_r = by_peer(mix_in_right, 1)
    small_p = by_peer(mix_out_left, 1)
    spread = [exchange(first(devices, c, width, small_r, acts)) for c in range(chunks)]
    big_li, big_qo, big_pt, big_rt, small_qt, small_lt = expand(
        devices, by_peer(mix_in_left, 2), small_p, small_r, by_peer(mix_out_right, 2)
    )
    returned, seconds = [], []
    for c in range(chunks):
        *pieces, second = middle(devices, c, width, small_p, big_li, kern, spread[c])
        returned.append(exchange(pieces))
        seconds.append(second)
    back_spread, slopes = [], []
    for c in range(chunks):
        *pieces, sloped = gate(devices, c, width, small_qt, weights, flat, upstream)
        back_spread.append(exchange(pieces))
        slopes.append(sloped)
    gate_grad = (full,)
    for c in range(chunks):
        gate_grad = outer(
            devices, c, width, False, big_qo, slopes[c], gate_grad, returned[c]
        )
    back_return, totals = [], []
    for c in range(chunks):
        *pieces, total = back_middle(
            devices, c, width, small_lt, big_pt, kern, seconds[c], back_spread[c]
        )
        back_return.append(exchange(pieces))
        totals.append(total.reshape(own * block, width))
    flat_grad = gate_grad.reshape(batch * rows, full)
    gate_part = dot_last(flat_grad, weights.astype(BF16)).reshape(batch, rows, full)
    term = dot_first(flat.reshape(batch * rows, full), flat_grad) * weight_scale

    weight_grad = term.reshape(devices, full // devices, full)
    for bit in bits_of(replicas):
        weight_grad = halve(weight_grad, "section", bit, 1, F32)
    for bit in reversed(bits_of(devices)):
        weight_grad = halve(weight_grad, "seq", bit, 0, F32)
    for bit in reversed(bits_of(replicas)):
        weight_grad = double(weight_grad, "section", bit, 1)
    weight_grad = weight_grad.reshape(full // devices, full)

    kernel_parts = []
    for total in totals:
        part = total * kernel_scale
        for bit in bits_of(replicas):
            part = halve(part, "section", bit, 0, BF16)
        part = part.astype(BF16)
        for bit in reversed(bits_of(replicas)):
            part = double(part, "section", bit, 0)
        kernel_parts.append(part)
    kernel_grad = jnp.concatenate(kernel_parts, axis=1)

    input_grad = (full,)
    for c in range(chunks):
        input_grad = outer(
            devices, c, width, True, big_rt, gate_part, input_grad, back_return[c]
        )
    return (input_grad[None], weight_grad, kernel_grad)


def forward_middle(spread, left_in, left_out, kern):
    second_mixed = contract("ija,baid->bijd", left_in, spread)
    weighted = (second_mixed * kern).astype(jnp.bfloat16)
    third_mixed = contract("ikj,bijd->bikd", left_out, weighted).astype(jnp.bfloat16)
    return (second_mixed, third_mixed)


def backward_middle(back_spread, second_mixed, left_in, left_out, kern):
    back_second = contract("ikj,bkid->bijd", left_out, back_spread)
    kernel_sum = jnp.sum(second_mixed * back_second, axis=0)
    back_weighted = (back_second * kern).astype(jnp.bfloat16)
    back_first = contract("ija,bijd->biad", left_in, back_weighted).astype(jnp.bfloat16)
    return (kernel_sum, back_first)


def local_plain(
    layer_input,
    grad_out,
    gate_weight,
    mix_in_right,
    mix_in_left,
    mix_out_left,
    mix_out_right,
    kernel,
):
    count_batch = layer_input.shape[1]
    token_rows = layer_input.shape[2]
    width = layer_input.shape[3]
    groups = mix_in_right.shape[0]
    block_size = mix_in_right.shape[1]
    replicas = lax.axis_size("section")
    kern = kernel.reshape(groups, block_size, width).astype(jnp.float32)
    acts = layer_input[0].reshape(count_batch, groups, block_size, width)
    flat_input = layer_input[0].reshape(count_batch * token_rows, width)
    upstream = grad_out[0].reshape(count_batch * token_rows, width).astype(jnp.float32)
    weights = lax.all_gather(gate_weight, "seq", axis=0, tiled=True)
    preact = jnp.dot(flat_input, weights, preferred_element_type=jnp.float32)
    sigma = jax.nn.sigmoid(preact)
    swish = preact * sigma
    slope = sigma * (1.0 + preact * (1.0 - sigma))
    mix_grad = (
        (upstream * swish).astype(jnp.bfloat16).reshape(count_batch, groups, block_size, width)
    )
    first_mixed = contract("aic,bacd->baid", mix_in_right, acts).astype(jnp.bfloat16)
    back_third = contract("kmi,bkmd->bkid", mix_out_right, mix_grad).astype(jnp.bfloat16)
    spread = lax.all_to_all(first_mixed, "seq", split_axis=2, concat_axis=1, tiled=True)
    second_mixed, third_mixed = forward_middle(spread, mix_in_left, mix_out_left, kern)
    returned = lax.all_to_all(third_mixed, "seq", split_axis=2, concat_axis=1, tiled=True)
    back_spread = lax.all_to_all(back_third, "seq", split_axis=2, concat_axis=1, tiled=True)
    kernel_sum, back_first = backward_middle(
        back_spread, second_mixed, mix_in_left, mix_out_left, kern
    )
    back_return = lax.all_to_all(back_first, "seq", split_axis=2, concat_axis=1, tiled=True)
    mixed = contract("kmi,bikd->bkmd", mix_out_right, returned).reshape(
        count_batch * token_rows, width
    )
    gate_grad = (upstream * mixed * slope).astype(jnp.bfloat16)
    gate_part = lax.dot_general(
        gate_grad, weights, (((1,), (1,)), ((), ())), preferred_element_type=jnp.float32
    )
    weight_scale = 1.0 / math.sqrt(replicas * BATCH * SEQ)
    kernel_scale = 1.0 / math.sqrt(replicas * BATCH)
    term = lax.dot_general(
        flat_input, gate_grad, (((0,), (0,)), ((), ())), preferred_element_type=jnp.float32
    )
    weight_local = lax.psum_scatter(term * weight_scale, "seq", scatter_dimension=0, tiled=True)
    weight_grad, kernel_total = lax.psum((weight_local, kernel_sum * kernel_scale), "section")
    mix_part = contract("aic,biad->bacd", mix_in_right, back_return).reshape(
        count_batch * token_rows, width
    )
    input_grad = (
        (gate_part + mix_part).astype(jnp.bfloat16).reshape(1, count_batch, token_rows, width)
    )
    kernel_grad = kernel_total.astype(jnp.bfloat16).reshape(groups * block_size, width)
    return (input_grad, weight_grad, kernel_grad)


def solution(mesh):
    placed = (
        P("section", None, "seq", None),
        P("section", None, "seq", None),
        P("seq", None),
        P("seq", None, None),
        P("seq", None, None),
        P("seq", None, None),
        P("seq", None, None),
        P("seq", None),
    )
    return jax.shard_map(
        local if 64 // mesh.shape["seq"] >= 16 else local_plain,
        mesh=mesh,
        in_specs=placed,
        out_specs=(P("section", None, "seq", None), P("seq", None), P("seq", None)),
        check_vma=False,
    )
```

profile of v0, /device:TPU:0, one launch (start us, length us, event | category | flops | bytes accessed | tf_op | source)
XLA Modules:
  0.0 302.8 jit_solution(9087676050362488307)
XLA Ops:
  1.6 3.0 collective-permute-start
  4.6 1.5 collective-permute-start.1
  6.1 1.4 reverse_select_fusion.5
  8.3 3.8 %shard_map.111 = (bf16[3,2,128,256]{3,2,1,0:T(8,128)(2,1)}, bf16[3,2,128,256]{3,2,1,0:T(8,128)(2,1)}, bf16[3,2,128,256]{3,2,1,0:T(8,128)(2,1)}, bf16[3,2,128,256]{3,2,1,0:T(8,128)(2,1)}) custom-call(bf16[16,64,64]{2,1,0:T(8,128)(2,1)} %bitcast.64, bf16[3,16,64,768]{3,2,1,0:T(8,128)(2,1)} %bitcast.46), custom_call_target="tpu_custom_call" | custom-call | flops 100663296 | bytes 3145728 | tf_op jit(solution)/shard_map/pallas_call | solution.py:100
  12.2 2.0 collective-permute-start.17
  14.1 1.5 collective-permute-start.18
  15.6 3.8 %shard_map.108 = (bf16[3,2,128,256]{3,2,1,0:T(8,128)(2,1)}, bf16[3,2,128,256]{3,2,1,0:T(8,128)(2,1)}, bf16[3,2,128,256]{3,2,1,0:T(8,128)(2,1)}, bf16[3,2,128,256]{3,2,1,0:T(8,128)(2,1)}) custom-call(bf16[16,64,64]{2,1,0:T(8,128)(2,1)} %bitcast.65, bf16[3,16,64,768]{3,2,1,0:T(8,128)(2,1)} %bitcast.47), custom_call_target="tpu_custom_call" | custom-call | flops 100663296 | bytes 3145728 | tf_op jit(solution)/shard_map/pallas_call | solution.py:100
  20.1 1.9 collective-permute-start.11
  24.9 1.5 collective-permute-start.12
  27.3 5.6 %collective-permute-done.18.refs_2_ = bf16[3,2,128,256]{3,2,1,0:T(8,128)(2,1)S(1)} collective-permute-done((bf16[3,2,128,256]{3,2,1,0:T(8,128)(2,1)}, bf16[3,2,128,256]{3,2,1,0:T(8,128)(2,1)S(1)}, u32[]{:S(2)}, u32[]{:S(2)}) %collective-permute-start.18) | collective-permute-done | bytes 393248 | tf_op jit(solution)/shard_map/ppermute | solution.py:277
  34.3 4.7 %shard_map.103 = (bf16[2,512,512]{2,1,0:T(8,128)(2,1)}, bf16[2,512,512]{2,1,0:T(8,128)(2,1)}, bf16[2,512,512]{2,1,0:T(8,128)(2,1)}, bf16[2,512,512]{2,1,0:T(8,12...) custom-call(bf16[16,64,64]{2,1,0:T(8,128)(2,1)} %copy.17.left_in, bf16[16,64,64]{2,1,0:T(8,128)(2,1)} %bitcast.92, ...), custom_call_target="tpu_custom_call" | custom-call | flops 4000000000 | bytes 8000000 | tf_op jit(solution)/shard_map/pallas_call | solution.py:80
  39.2 3.8 %shard_map.105 = (bf16[3,2,128,256]{3,2,1,0:T(8,128)(2,1)}, bf16[3,2,128,256]{3,2,1,0:T(8,128)(2,1)}, bf16[3,2,128,256]{3,2,1,0:T(8,128)(2,1)}, bf16[3,2,128,256]{3,2,1,0:T(8,128)(2,1)}) custom-call(bf16[16,64,64]{2,1,0:T(8,128)(2,1)} %bitcast.67, bf16[3,16,64,768]{3,2,1,0:T(8,128)(2,1)} %bitcast.48), custom_call_target="tpu_custom_call" | custom-call | flops 100663296 | bytes 3145728 | tf_op jit(solution)/shard_map/pallas_call | solution.py:100
  43.1 2.4 collective-permute-start.6
  45.5 4.3 %collective-permute-done.12.refs_2_ = bf16[3,2,128,256]{3,2,1,0:T(8,128)(2,1)} collective-permute-done((bf16[3,2,128,256]{3,2,1,0:T(8,128)(2,1)}, bf16[3,2,128,256]{3,2,1,0:T(8,128)(2,1)}, u32[]{:S(2)}, u32[]{:S(2)}) %collective-permute-start.12) | collective-permute-done | bytes 393248 | tf_op jit(solution)/shard_map/ppermute | solution.py:277
  49.8 5.3 %shard_map.112 = (bf16[3,2,128,256]{3,2,1,0:T(8,128)(2,1)}, bf16[3,2,128,256]{3,2,1,0:T(8,128)(2,1)}, bf16[3,2,128,256]{3,2,1,0:T(8,128)(2,1)}, bf16[3,2,128,256]{3,2,1,0:T(8,128)(2,1)}, f32[3,2,512,256]{3,2,1,0:T(8,128)}) custom-call(bf16[16,64,64]{2,1,0:T(8,128)(2,1)} %bitcast.93, bf16[2,512,512]{2,1,0:T(8,128)(2,1)} %get-tuple-element.70.big, ...), custom_call_target="tpu_custom_call" | custom-call | flops 3000000000 | bytes 8000000 | tf_op jit(solution)/shard_map/pallas_call | solution.py:136
  55.1 4.0 %collective-permute-start.20 = (bf16[3,2,128,256]{3,2,1,0:T(8,128)(2,1)}, bf16[3,2,128,256]{3,2,1,0:T(8,128)(2,1)S(1)}, u32[]{:S(2)}, u32[]{:S(2)}) collective-permute-start(bf16[3,2,128,256]{3,2,1,0:T(8,128)(2,1)} %get-tuple-element.94), channel_id=1, source_target_pairs={{0,1},{1,0},{2,3},{3,2},{4,5},{5,4},{6,7},{7,6},{8,9},{9,8},{10,11... | collective-permute-start | bytes 1179656 | tf_op jit(solution)/shard_map/ppermute | solution.py:277
  59.1 5.4 %shard_map.109 = (bf16[3,2,128,256]{3,2,1,0:T(8,128)(2,1)}, bf16[3,2,128,256]{3,2,1,0:T(8,128)(2,1)}, bf16[3,2,128,256]{3,2,1,0:T(8,128)(2,1)}, bf16[3,2,128,256]{3,2,1,0:T(8,128)(2,1)}, f32[3,2,512,256]{3,2,1,0:T(8,128)}) custom-call(bf16[16,64,64]{2,1,0:T(8,128)(2,1)} %bitcast.94, bf16[2,512,512]{2,1,0:T(8,128)(2,1)} %get-tuple-element.70.big, ...), custom_call_target="tpu_custom_call" | custom-call | flops 3000000000 | bytes 8000000 | tf_op jit(solution)/shard_map/pallas_call | solution.py:136
  64.6 2.0 collective-permute-done.6.refs_2_
  67.6 2.8 collective-permute-start.14
  70.4 5.3 %shard_map.106 = (bf16[3,2,128,256]{3,2,1,0:T(8,128)(2,1)}, bf16[3,2,128,256]{3,2,1,0:T(8,128)(2,1)}, bf16[3,2,128,256]{3,2,1,0:T(8,128)(2,1)}, bf16[3,2,128,256]{3,2,1,0:T(8,128)(2,1)}, f32[3,2,512,256]{3,2,1,0:T(8,128)}) custom-call(bf16[16,64,64]{2,1,0:T(8,128)(2,1)} %bitcast.95, bf16[2,512,512]{2,1,0:T(8,128)(2,1)} %get-tuple-element.70.big, ...), custom_call_target="tpu_custom_call" | custom-call | flops 3000000000 | bytes 8000000 | tf_op jit(solution)/shard_map/pallas_call | solution.py:136
  75.8 1.7 maximum_select_fusion
  77.5 12.0 %shard_map.110 = (bf16[3,2,128,256]{3,2,1,0:T(8,128)(2,1)}, bf16[3,2,128,256]{3,2,1,0:T(8,128)(2,1)}, bf16[3,2,128,256]{3,2,1,0:T(8,128)(2,1)}, bf16[3,2,128,256]{3,2,1,0:T(8,128)(2,1)}, f32[3,1024,256]{2,1,0:T(8,128)}) custom-call(bf16[16,64,64]{2,1,0:T(8,128)(2,1)} %get-tuple-element.68.small, f32[768,768]{1,0:T(8,128)} %bitcast.59, ...), custom_call_target="tpu_custom_call" | custom-call | flops 1207959552 | bytes 12000000 | tf_op jit(solution)/shard_map/pallas_call | solution.py:220
  89.5 12.1 %shard_map.107 = (bf16[3,2,128,256]{3,2,1,0:T(8,128)(2,1)}, bf16[3,2,128,256]{3,2,1,0:T(8,128)(2,1)}, bf16[3,2,128,256]{3,2,1,0:T(8,128)(2,1)}, bf16[3,2,128,256]{3,2,1,0:T(8,128)(2,1)}, f32[3,1024,256]{2,1,0:T(8,128)}) custom-call(bf16[16,64,64]{2,1,0:T(8,128)(2,1)} %get-tuple-element.68.small, f32[768,768]{1,0:T(8,128)} %bitcast.60, ...), custom_call_target="tpu_custom_call" | custom-call | flops 1207959552 | bytes 12000000 | tf_op jit(solution)/shard_map/pallas_call | solution.py:220
  101.6 2.2 collective-permute-start.16
  105.5 6.1 %shard_map.113.refs_4_ = bf16[3,1024,768]{2,1,0:T(8,128)(2,1)} custom-call(bf16[2,512,512]{2,1,0:T(8,128)(2,1)} %get-tuple-element.67.big, f32[3,1024,256]{2,1,0:T(8,128)} %get-tuple-element.88.other, bf16[3,2,128,256]{3,2,1,0:T(8,128)(2,1)} %get-tuple-element.93.refs_0_, bf16[3,2,128,256]{3,2,1,0:T(8,128)(2,1)} %copy-done.36, ...), custom_call_target="tpu_custom_call" | custom-call | flops 3000000000 | bytes 6000000 | tf_op jit(solution)/shard_map/pallas_call | solution.py:263
  111.6 2.1 collective-permute-start.9
  113.7 11.9 %shard_map.104 = (bf16[3,2,128,256]{3,2,1,0:T(8,128)(2,1)}, bf16[3,2,128,256]{3,2,1,0:T(8,128)(2,1)}, bf16[3,2,128,256]{3,2,1,0:T(8,128)(2,1)}, bf16[3,2,128,256]{3,2,1,0:T(8,128)(2,1)}, f32[3,1024,256]{2,1,0:T(8,128)}) custom-call(bf16[16,64,64]{2,1,0:T(8,128)(2,1)} %get-tuple-element.68.small, f32[768,768]{1,0:T(8,128)} %bitcast.61, ...), custom_call_target="tpu_custom_call" | custom-call | flops 1207959552 | bytes 12000000 | tf_op jit(solution)/shard_map/pallas_call | solution.py:220
  127.8 6.1 %shard_map.114.refs_4_ = bf16[3,1024,768]{2,1,0:T(8,128)(2,1)} custom-call(bf16[2,512,512]{2,1,0:T(8,128)(2,1)} %get-tuple-element.67.big, f32[3,1024,256]{2,1,0:T(8,128)} %get-tuple-element.79.other, bf16[3,2,128,256]{3,2,1,0:T(8,128)(2,1)} %get-tuple-element.84.refs_0_, bf16[3,2,128,256]{3,2,1,0:T(8,128)(2,1)} %copy-done.5, ...), custom_call_target="tpu_custom_call", output_to_operand_aliasing={{}: (6, {})} | custom-call | flops 3000000000 | bytes 6000000 | tf_op jit(solution)/shard_map/pallas_call | solution.py:263
  134.0 1.6 collective-permute-start.37
  137.7 6.2 %shard_map.115 = bf16[3,1024,768]{2,1,0:T(8,128)(2,1)} custom-call(bf16[2,512,512]{2,1,0:T(8,128)(2,1)} %get-tuple-element.67.big, f32[3,1024,256]{2,1,0:T(8,128)} %get-tuple-element.69.other, bf16[3,2,128,256]{3,2,1,0:T(8,128)(2,1)} %get-tuple-element.75.refs_0_, bf16[3,2,128,256]{3,2,1,0:T(8,128)(2,1)} %copy-done.8, ...), custom_call_target="tpu_custom_call", output_to_operand_aliasing={{}: (6, {})} | custom-call | flops 3000000000 | bytes 6000000 | tf_op jit(solution)/shard_map/pallas_call | solution.py:263
  143.9 9.1 %fusion.other = f32[3,1024,768]{2,1,0:T(8,128)} fusion(bf16[3,1024,768]{2,1,0:T(8,128)(2,1)} %shard_map.115, f32[768,768]{1,0:T(8,128)S(1)} %bitcast.62), kind=kOutput, calls=%fused_computation.4 | convolution fusion | flops 3624468480 | bytes 16515072 | tf_op jit(solution)/shard_map/dot_general | solution.py:32
  153.1 4.1 %convolution_multiply_fusion = f32[768,768]{0,1:T(8,128)S(1)} fusion(bf16[3072,768]{1,0:T(8,128)(2,1)S(1)} %bitcast.63, bf16[3072,768]{1,0:T(8,128)(2,1)S(1)} %bitcast.54), kind=kOutput, calls=%fused_computation.1 | convolution fusion | flops 3624468480 | bytes 11796480 | tf_op jit(solution)/shard_map/dot_general | solution.py:28
  158.2 1.5 collective-permute-start.31
  161.7 5.4 %shard_map.118 = (bf16[3,2,128,256]{3,2,1,0:T(8,128)(2,1)}, bf16[3,2,128,256]{3,2,1,0:T(8,128)(2,1)}, bf16[3,2,128,256]{3,2,1,0:T(8,128)(2,1)}, bf16[3,2,128,256]{3,2,1,0:T(8,128)(2,1)}, f32[2,512,256]{2,1,0:T(8,128)}) custom-call(bf16[16,64,64]{2,1,0:T(8,128)(2,1)} %get-tuple-element.97.small, bf16[2,512,512]{2,1,0:T(8,128)(2,1)} %get-tuple-element.98.big, ...), custom_call_target="tpu_custom_call" | custom-call | flops 3000000000 | bytes 8000000 | tf_op jit(solution)/shard_map/pallas_call | solution.py:178
  168.5 1.6 collective-permute-start.25
  170.8 5.4 %shard_map.117 = (bf16[3,2,128,256]{3,2,1,0:T(8,128)(2,1)}, bf16[3,2,128,256]{3,2,1,0:T(8,128)(2,1)}, bf16[3,2,128,256]{3,2,1,0:T(8,128)(2,1)}, bf16[3,2,128,256]{3,2,1,0:T(8,128)(2,1)}, f32[2,512,256]{2,1,0:T(8,128)}) custom-call(bf16[16,64,64]{2,1,0:T(8,128)(2,1)} %get-tuple-element.97.small, bf16[2,512,512]{2,1,0:T(8,128)(2,1)} %get-tuple-element.98.big, ...), custom_call_target="tpu_custom_call" | custom-call | flops 3000000000 | bytes 8000000 | tf_op jit(solution)/shard_map/pallas_call | solution.py:178
  179.7 5.4 %shard_map.116 = (bf16[3,2,128,256]{3,2,1,0:T(8,128)(2,1)}, bf16[3,2,128,256]{3,2,1,0:T(8,128)(2,1)}, bf16[3,2,128,256]{3,2,1,0:T(8,128)(2,1)}, bf16[3,2,128,256]{3,2,1,0:T(8,128)(2,1)}, f32[2,512,256]{2,1,0:T(8,128)}) custom-call(bf16[16,64,64]{2,1,0:T(8,128)(2,1)} %get-tuple-element.97.small, bf16[2,512,512]{2,1,0:T(8,128)(2,1)} %get-tuple-element.98.big, ...), custom_call_target="tpu_custom_call" | custom-call | flops 3000000000 | bytes 8000000 | tf_op jit(solution)/shard_map/pallas_call | solution.py:178
  188.9 1.5 collective-permute-start.40
  190.4 1.6 collective-permute-start.50
  192.2 3.3 %collective-permute-done.50 = bf16[256,256]{1,0:T(8,128)(2,1)S(1)} collective-permute-done((bf16[256,256]{1,0:T(8,128)(2,1)S(1)}, bf16[256,256]{1,0:T(8,128)(2,1)S(1)}, u32[]{:S(2)}, u32[]{:S(2)}) %collective-permute-start.50) | collective-permute-done | bytes 131104 | tf_op jit(solution)/shard_map/ppermute | solution.py:277
  195.5 1.5 collective-permute-start.56
  197.1 3.4 %collective-permute-done.56 = bf16[256,256]{1,0:T(8,128)(2,1)S(1)} collective-permute-done((bf16[256,256]{1,0:T(8,128)(2,1)S(1)}, bf16[256,256]{1,0:T(8,128)(2,1)S(1)}, u32[]{:S(2)}, u32[]{:S(2)}) %collective-permute-start.56) | collective-permute-done | bytes 131104 | tf_op jit(solution)/shard_map/ppermute | solution.py:277
  200.5 1.5 collective-permute-start.62
  202.0 3.4 %collective-permute-done.62 = bf16[256,256]{1,0:T(8,128)(2,1)S(1)} collective-permute-done((bf16[256,256]{1,0:T(8,128)(2,1)S(1)}, bf16[256,256]{1,0:T(8,128)(2,1)S(1)}, u32[]{:S(2)}, u32[]{:S(2)}) %collective-permute-start.62) | collective-permute-done | bytes 131104 | tf_op jit(solution)/shard_map/ppermute | solution.py:277
  207.7 1.9 collective-permute-start.34
  210.4 6.0 %shard_map.119.refs_4_ = bf16[3,1024,768]{2,1,0:T(8,128)(2,1)} custom-call(bf16[2,512,512]{2,1,0:T(8,128)(2,1)} %get-tuple-element.66.big, f32[3,1024,768]{2,1,0:T(8,128)} %fusion.other, bf16[3,2,128,256]{3,2,1,0:T(8,128)(2,1)} %get-tuple-element.122.refs_0_, bf16[3,2,128,256]{3,2,1,0:T(8,128)(2,1)} %copy-done.2, bf16[3,2,128,256]{3,2,1,0:T(8,128)(2,1)} %copy-done.3, ...), custom_call_target="tpu_custom_call" | custom-call | flops 3000000000 | bytes 6000000 | tf_op jit(solution)/shard_map/pallas_call | solution.py:263
  219.1 4.1 %collective-permute-done.33.refs_2_ = bf16[3,2,128,256]{3,2,1,0:T(8,128)(2,1)S(1)} collective-permute-done((bf16[3,2,128,256]{3,2,1,0:T(8,128)(2,1)}, bf16[3,2,128,256]{3,2,1,0:T(8,128)(2,1)S(1)}, u32[]{:S(2)}, u32[]{:S(2)}) %collective-permute-start.33) | collective-permute-done | bytes 393248 | tf_op jit(solution)/shard_map/ppermute | solution.py:277
  223.1 3.6 %collective-permute-start.28 = (bf16[3,2,128,256]{3,2,1,0:T(8,128)(2,1)}, bf16[3,2,128,256]{3,2,1,0:T(8,128)(2,1)S(1)}, u32[]{:S(2)}, u32[]{:S(2)}) collective-permute-start(bf16[3,2,128,256]{3,2,1,0:T(8,128)(2,1)} %get-tuple-element.107), channel_id=1, source_target_pairs={{0,3},{1,2},{2,1},{3,0},{4,7},{5,6},{6,5},{7,4},{8,11},{9,10},{10,... | collective-permute-start | bytes 1179656 | tf_op jit(solution)/shard_map/ppermute | solution.py:277
  227.1 2.4 collective-permute-start.51
  229.5 6.1 %shard_map.120.refs_4_ = bf16[3,1024,768]{2,1,0:T(8,128)(2,1)} custom-call(bf16[2,512,512]{2,1,0:T(8,128)(2,1)} %get-tuple-element.66.big, f32[3,1024,768]{2,1,0:T(8,128)} %fusion.other, bf16[3,2,128,256]{3,2,1,0:T(8,128)(2,1)} %get-tuple-element.113.refs_0_, bf16[3,2,128,256]{3,2,1,0:T(8,128)(2,1)} %copy-done.9, ...), custom_call_target="tpu_custom_call", output_to_operand_aliasing={{}: (6, {})} | custom-call | flops 3000000000 | bytes 6000000 | tf_op jit(solution)/shard_map/pallas_call | solution.py:263
  235.6 1.6 collective-permute-start.57
  237.2 5.2 %collective-permute-start.63 = (bf16[128,256]{1,0:T(8,128)(2,1)S(1)}, bf16[128,256]{1,0:T(8,128)(2,1)S(1)}, u32[]{:S(2)}, u32[]{:S(2)}) collective-permute-start(bf16[128,256]{1,0:T(8,128)(2,1)S(1)} %dynamic-slice_convert_fusion.6), channel_id=1, source_target_pairs={{0,16},{4,20},{8,24},{12,28},{16,0},{20,4},{24,8},{28,12},{1,17},{... | collective-permute-start | bytes 196616 | tf_op jit(solution)/shard_map/ppermute | solution.py:277
  243.1 6.0 %shard_map.121 = bf16[3,1024,768]{2,1,0:T(8,128)(2,1)} custom-call(bf16[2,512,512]{2,1,0:T(8,128)(2,1)} %get-tuple-element.66.big, f32[3,1024,768]{2,1,0:T(8,128)} %fusion.other, bf16[3,2,128,256]{3,2,1,0:T(8,128)(2,1)} %get-tuple-element.104.refs_0_, bf16[3,2,128,256]{3,2,1,0:T(8,128)(2,1)} %copy-done.10, ...), custom_call_target="tpu_custom_call", output_to_operand_aliasing={{}: (6, {})} | custom-call | flops 3000000000 | bytes 6000000 | tf_op jit(solution)/shard_map/pallas_call | solution.py:263
  249.4 1.6 collective-permute-start.42
  252.4 1.7 collective-permute-start.58
  255.4 9.6 %collective-permute-done.42 = f32[4,48,768]{2,1,0:T(8,128)S(1)} collective-permute-done((f32[4,48,768]{2,1,0:T(8,128)S(1)}, f32[4,48,768]{2,1,0:T(8,128)S(1)}, u32[]{:S(2)}, u32[]{:S(2)}) %collective-permute-start.42) | collective-permute-done | bytes 589856 | tf_op jit(solution)/shard_map/ppermute | solution.py:277
  265.2 1.6 collective-permute-start.43
  266.9 2.5 collective-permute-start.53
  269.6 2.1 collective-permute-start.65
  271.6 8.1 %collective-permute-done.43 = f32[4,24,768]{2,1,0:T(8,128)S(1)} collective-permute-done((f32[4,24,768]{2,1,0:T(8,128)S(1)}, f32[4,24,768]{2,1,0:T(8,128)S(1)}, u32[]{:S(2)}, u32[]{:S(2)}) %collective-permute-start.43) | collective-permute-done | bytes 294944 | tf_op jit(solution)/shard_map/ppermute | solution.py:277
  281.6 3.6 %collective-permute-done.44 = f32[2,24,768]{2,1,0:T(8,128)S(1)} collective-permute-done((f32[2,24,768]{2,1,0:T(8,128)S(1)}, f32[2,24,768]{2,1,0:T(8,128)S(1)}, u32[]{:S(2)}, u32[]{:S(2)}) %collective-permute-start.44) | collective-permute-done | bytes 147488 | tf_op jit(solution)/shard_map/ppermute | solution.py:277
  286.4 3.2 %collective-permute-done.45 = f32[1,24,768]{2,1,0:T(8,128)S(1)} collective-permute-done((f32[1,24,768]{2,1,0:T(8,128)S(1)}, f32[1,24,768]{2,1,0:T(8,128)S(1)}, u32[]{:S(2)}, u32[]{:S(2)}) %collective-permute-start.45) | collective-permute-done | bytes 73760 | tf_op jit(solution)/shard_map/ppermute | solution.py:277
  290.0 5.1 %collective-permute-done.46 = f32[1,24,768]{2,1,0:T(8,128)S(1)} collective-permute-done((f32[1,24,768]{2,1,0:T(8,128)S(1)}, f32[1,24,768]{2,1,0:T(8,128)S(1)}, u32[]{:S(2)}, u32[]{:S(2)}) %collective-permute-start.46) | collective-permute-done | bytes 73760 | tf_op jit(solution)/shard_map/ppermute | solution.py:277
  295.4 4.9 %collective-permute-done.47 = f32[1,48,768]{2,1,0:T(8,128)S(1)} collective-permute-done((f32[1,48,768]{2,1,0:T(8,128)S(1)}, f32[1,48,768]{2,1,0:T(8,128)S(1)}, u32[]{:S(2)}, u32[]{:S(2)}) %collective-permute-start.47) | collective-permute-done | bytes 147488 | tf_op jit(solution)/shard_map/ppermute | solution.py:277
  (246 shorter events, 43.2 us)
Async XLA Ops:
  1.6 18.4 %collective-permute-start = (f32[48,768]{1,0:T(8,128)S(1)}, f32[48,768]{1,0:T(8,128)S(1)}, u32[]{:S(2)}, u32[]{:S(2)}) collective-permute-start(f32[48,768]{1,0:T(8,128)S(1)} %get-tuple-element.130), channel_id=1, source_target_pairs={{0,1},{1,0},{2,3},{3,2},{4,5},{5,4},{6,7},{7,6},{8,9},{9,8},{10,11... | collective-permute-start | bytes 442376 | tf_op jit(solution)/shard_map/ppermute | solution.py:277
  4.6 15.6 %collective-permute-start.1 = (f32[48,768]{1,0:T(8,128)S(1)}, f32[48,768]{1,0:T(8,128)S(1)}, u32[]{:S(2)}, u32[]{:S(2)}) collective-permute-start(f32[48,768]{1,0:T(8,128)S(1)} %get-tuple-element.130), channel_id=1, source_target_pairs={{0,2},{1,3},{2,0},{3,1},{4,6},{5,7},{6,4},{7,5},{8,10},{9,11},{10,... | collective-permute-start | bytes 442376 | tf_op jit(solution)/shard_map/ppermute | solution.py:277
  6.1 15.9 %collective-permute-start.2 = (f32[48,768]{1,0:T(8,128)S(1)}, f32[48,768]{1,0:T(8,128)S(1)}, u32[]{:S(2)}, u32[]{:S(2)}) collective-permute-start(f32[48,768]{1,0:T(8,128)S(1)} %get-tuple-element.130), channel_id=1, source_target_pairs={{0,3},{1,2},{2,1},{3,0},{4,7},{5,6},{6,5},{7,4},{8,11},{9,10},{10,... | collective-permute-start | bytes 442376 | tf_op jit(solution)/shard_map/ppermute | solution.py:277
  12.2 14.4 %collective-permute-start.17 = (bf16[3,2,128,256]{3,2,1,0:T(8,128)(2,1)}, bf16[3,2,128,256]{3,2,1,0:T(8,128)(2,1)S(1)}, u32[]{:S(2)}, u32[]{:S(2)}) collective-permute-start(bf16[3,2,128,256]{3,2,1,0:T(8,128)(2,1)} %get-tuple-element.90), channel_id=1, source_target_pairs={{0,1},{1,0},{2,3},{3,2},{4,5},{5,4},{6,7},{7,6},{8,9},{9,8},{10,11... | collective-permute-start | bytes 1179656 | tf_op jit(solution)/shard_map/ppermute | solution.py:277
  14.1 18.8 %collective-permute-start.18 = (bf16[3,2,128,256]{3,2,1,0:T(8,128)(2,1)}, bf16[3,2,128,256]{3,2,1,0:T(8,128)(2,1)S(1)}, u32[]{:S(2)}, u32[]{:S(2)}) collective-permute-start(bf16[3,2,128,256]{3,2,1,0:T(8,128)(2,1)} %get-tuple-element.91), channel_id=1, source_target_pairs={{0,2},{1,3},{2,0},{3,1},{4,6},{5,7},{6,4},{7,5},{8,10},{9,11},{10,... | collective-permute-start | bytes 1179656 | tf_op jit(solution)/shard_map/ppermute | solution.py:277
  20.0 23.0 %collective-permute-start.19 = (bf16[3,2,128,256]{3,2,1,0:T(8,128)(2,1)}, bf16[3,2,128,256]{3,2,1,0:T(8,128)(2,1)}, u32[]{:S(2)}, u32[]{:S(2)}) collective-permute-start(bf16[3,2,128,256]{3,2,1,0:T(8,128)(2,1)} %get-tuple-element.92), channel_id=1, source_target_pairs={{0,3},{1,2},{2,1},{3,0},{4,7},{5,6},{6,5},{7,4},{8,11},{9,10},{10,... | collective-permute-start | bytes 1179656 | tf_op jit(solution)/shard_map/ppermute | solution.py:277
  20.1 22.9 %collective-permute-start.11 = (bf16[3,2,128,256]{3,2,1,0:T(8,128)(2,1)}, bf16[3,2,128,256]{3,2,1,0:T(8,128)(2,1)}, u32[]{:S(2)}, u32[]{:S(2)}) collective-permute-start(bf16[3,2,128,256]{3,2,1,0:T(8,128)(2,1)} %get-tuple-element.81), channel_id=1, source_target_pairs={{0,1},{1,0},{2,3},{3,2},{4,5},{5,4},{6,7},{7,6},{8,9},{9,8},{10,11... | collective-permute-start | bytes 1179656 | tf_op jit(solution)/shard_map/ppermute | solution.py:277
  24.9 24.8 %collective-permute-start.12 = (bf16[3,2,128,256]{3,2,1,0:T(8,128)(2,1)}, bf16[3,2,128,256]{3,2,1,0:T(8,128)(2,1)}, u32[]{:S(2)}, u32[]{:S(2)}) collective-permute-start(bf16[3,2,128,256]{3,2,1,0:T(8,128)(2,1)} %get-tuple-element.82), channel_id=1, source_target_pairs={{0,2},{1,3},{2,0},{3,1},{4,6},{5,7},{6,4},{7,5},{8,10},{9,11},{10,... | collective-permute-start | bytes 1179656 | tf_op jit(solution)/shard_map/ppermute | solution.py:277
  26.6 28.5 %collective-permute-start.13 = (bf16[3,2,128,256]{3,2,1,0:T(8,128)(2,1)S(1)}, bf16[3,2,128,256]{3,2,1,0:T(8,128)(2,1)}, u32[]{:S(2)}, u32[]{:S(2)}) collective-permute-start(bf16[3,2,128,256]{3,2,1,0:T(8,128)(2,1)S(1)} %copy-done.20), channel_id=1, source_target_pairs={{0,3},{1,2},{2,1},{3,0},{4,7},{5,6},{6,5},{7,4},{8,11},{9,10},{10,... | collective-permute-start | bytes 1179656 | tf_op jit(solution)/shard_map/ppermute | solution.py:277
  32.9 42.8 %collective-permute-start.4 = (f32[4,96,768]{2,1,0:T(8,128)S(1)}, f32[4,96,768]{2,1,0:T(8,128)S(1)}, u32[]{:S(2)}, u32[]{:S(2)}) collective-permute-start(f32[4,96,768]{2,1,0:T(8,128)S(1)} %maximum_select_fusion.1), channel_id=1, source_target_pairs={{0,8},{4,12},{8,0},{12,4},{16,24},{20,28},{24,16},{28,20},{1,9},{5... | collective-permute-start | bytes 3538952 | tf_op jit(solution)/shard_map/ppermute | solution.py:277
  43.0 21.5 %collective-permute-start.5 = (bf16[3,2,128,256]{3,2,1,0:T(8,128)(2,1)}, bf16[3,2,128,256]{3,2,1,0:T(8,128)(2,1)S(1)}, u32[]{:S(2)}, u32[]{:S(2)}) collective-permute-start(bf16[3,2,128,256]{3,2,1,0:T(8,128)(2,1)} %get-tuple-element.72), channel_id=1, source_target_pairs={{0,1},{1,0},{2,3},{3,2},{4,5},{5,4},{6,7},{7,6},{8,9},{9,8},{10,11... | collective-permute-start | bytes 1179656 | tf_op jit(solution)/shard_map/ppermute | solution.py:277
  43.1 23.5 %collective-permute-start.6 = (bf16[3,2,128,256]{3,2,1,0:T(8,128)(2,1)}, bf16[3,2,128,256]{3,2,1,0:T(8,128)(2,1)S(1)}, u32[]{:S(2)}, u32[]{:S(2)}) collective-permute-start(bf16[3,2,128,256]{3,2,1,0:T(8,128)(2,1)} %get-tuple-element.73), channel_id=1, source_target_pairs={{0,2},{1,3},{2,0},{3,1},{4,6},{5,7},{6,4},{7,5},{8,10},{9,11},{10,... | collective-permute-start | bytes 1179656 | tf_op jit(solution)/shard_map/ppermute | solution.py:277
  49.8 17.9 %collective-permute-start.7 = (bf16[3,2,128,256]{3,2,1,0:T(8,128)(2,1)}, bf16[3,2,128,256]{3,2,1,0:T(8,128)(2,1)S(1)}, u32[]{:S(2)}, u32[]{:S(2)}) collective-permute-start(bf16[3,2,128,256]{3,2,1,0:T(8,128)(2,1)} %get-tuple-element.74), channel_id=1, source_target_pairs={{0,3},{1,2},{2,1},{3,0},{4,7},{5,6},{6,5},{7,4},{8,11},{9,10},{10,... | collective-permute-start | bytes 1179656 | tf_op jit(solution)/shard_map/ppermute | solution.py:277
  55.1 46.6 %collective-permute-start.20 = (bf16[3,2,128,256]{3,2,1,0:T(8,128)(2,1)}, bf16[3,2,128,256]{3,2,1,0:T(8,128)(2,1)S(1)}, u32[]{:S(2)}, u32[]{:S(2)}) collective-permute-start(bf16[3,2,128,256]{3,2,1,0:T(8,128)(2,1)} %get-tuple-element.94), channel_id=1, source_target_pairs={{0,1},{1,0},{2,3},{3,2},{4,5},{5,4},{6,7},{7,6},{8,9},{9,8},{10,11... | collective-permute-start | bytes 1179656 | tf_op jit(solution)/shard_map/ppermute | solution.py:277
  64.5 39.4 %collective-permute-start.21 = (bf16[3,2,128,256]{3,2,1,0:T(8,128)(2,1)S(1)}, bf16[3,2,128,256]{3,2,1,0:T(8,128)(2,1)S(1)}, u32[]{:S(2)}, u32[]{:S(2)}) collective-permute-start(bf16[3,2,128,256]{3,2,1,0:T(8,128)(2,1)S(1)} %copy-done.37), channel_id=1, source_target_pairs={{0,2},{1,3},{2,0},{3,1},{4,6},{5,7},{6,4},{7,5},{8,10},{9,11},{10,... | collective-permute-start | bytes 1179656 | tf_op jit(solution)/shard_map/ppermute | solution.py:277
  66.5 38.2 %collective-permute-start.22 = (bf16[3,2,128,256]{3,2,1,0:T(8,128)(2,1)S(1)}, bf16[3,2,128,256]{3,2,1,0:T(8,128)(2,1)S(1)}, u32[]{:S(2)}, u32[]{:S(2)}) collective-permute-start(bf16[3,2,128,256]{3,2,1,0:T(8,128)(2,1)S(1)} %copy-done.34), channel_id=1, source_target_pairs={{0,3},{1,2},{2,1},{3,0},{4,7},{5,6},{6,5},{7,4},{8,11},{9,10},{10,... | collective-permute-start | bytes 1179656 | tf_op jit(solution)/shard_map/ppermute | solution.py:277
  67.6 44.0 %collective-permute-start.14 = (bf16[3,2,128,256]{3,2,1,0:T(8,128)(2,1)}, bf16[3,2,128,256]{3,2,1,0:T(8,128)(2,1)S(1)}, u32[]{:S(2)}, u32[]{:S(2)}) collective-permute-start(bf16[3,2,128,256]{3,2,1,0:T(8,128)(2,1)} %get-tuple-element.85), channel_id=1, source_target_pairs={{0,1},{1,0},{2,3},{3,2},{4,5},{5,4},{6,7},{7,6},{8,9},{9,8},{10,11... | collective-permute-start | bytes 1179656 | tf_op jit(solution)/shard_map/ppermute | solution.py:277
  75.8 49.9 %collective-permute-start.15 = (bf16[3,2,128,256]{3,2,1,0:T(8,128)(2,1)S(1)}, bf16[3,2,128,256]{3,2,1,0:T(8,128)(2,1)S(1)}, u32[]{:S(2)}, u32[]{:S(2)}) collective-permute-start(bf16[3,2,128,256]{3,2,1,0:T(8,128)(2,1)S(1)} %copy-done.32), channel_id=1, source_target_pairs={{0,2},{1,3},{2,0},{3,1},{4,6},{5,7},{6,4},{7,5},{8,10},{9,11},{10,... | collective-permute-start | bytes 1179656 | tf_op jit(solution)/shard_map/ppermute | solution.py:277
  101.6 25.4 %collective-permute-start.16 = (bf16[3,2,128,256]{3,2,1,0:T(8,128)(2,1)S(1)}, bf16[3,2,128,256]{3,2,1,0:T(8,128)(2,1)S(1)}, u32[]{:S(2)}, u32[]{:S(2)}) collective-permute-start(bf16[3,2,128,256]{3,2,1,0:T(8,128)(2,1)S(1)} %copy-done.30), channel_id=1, source_target_pairs={{0,3},{1,2},{2,1},{3,0},{4,7},{5,6},{6,5},{7,4},{8,11},{9,10},{10,... | collective-permute-start | bytes 1179656 | tf_op jit(solution)/shard_map/ppermute | solution.py:277
  103.9 30.1 %collective-permute-start.10 = (bf16[3,2,128,256]{3,2,1,0:T(8,128)(2,1)S(1)}, bf16[3,2,128,256]{3,2,1,0:T(8,128)(2,1)S(1)}, u32[]{:S(2)}, u32[]{:S(2)}) collective-permute-start(bf16[3,2,128,256]{3,2,1,0:T(8,128)(2,1)S(1)} %copy-done.35), channel_id=1, source_target_pairs={{0,3},{1,2},{2,1},{3,0},{4,7},{5,6},{6,5},{7,4},{8,11},{9,10},{10,... | collective-permute-start | bytes 1179656 | tf_op jit(solution)/shard_map/ppermute | solution.py:277
  104.7 30.9 %collective-permute-start.8 = (bf16[3,2,128,256]{3,2,1,0:T(8,128)(2,1)S(1)}, bf16[3,2,128,256]{3,2,1,0:T(8,128)(2,1)S(1)}, u32[]{:S(2)}, u32[]{:S(2)}) collective-permute-start(bf16[3,2,128,256]{3,2,1,0:T(8,128)(2,1)S(1)} %copy-done.33), channel_id=1, source_target_pairs={{0,1},{1,0},{2,3},{3,2},{4,5},{5,4},{6,7},{7,6},{8,9},{9,8},{10,11... | collective-permute-start | bytes 1179656 | tf_op jit(solution)/shard_map/ppermute | solution.py:277
  111.6 25.3 %collective-permute-start.9 = (bf16[3,2,128,256]{3,2,1,0:T(8,128)(2,1)S(1)}, bf16[3,2,128,256]{3,2,1,0:T(8,128)(2,1)S(1)}, u32[]{:S(2)}, u32[]{:S(2)}) collective-permute-start(bf16[3,2,128,256]{3,2,1,0:T(8,128)(2,1)S(1)} %copy-done.31), channel_id=1, source_target_pairs={{0,2},{1,3},{2,0},{3,1},{4,6},{5,7},{6,4},{7,5},{8,10},{9,11},{10,... | collective-permute-start | bytes 1179656 | tf_op jit(solution)/shard_map/ppermute | solution.py:277
  125.7 31.6 %collective-permute-start.35 = (bf16[3,2,128,256]{3,2,1,0:T(8,128)(2,1)}, bf16[3,2,128,256]{3,2,1,0:T(8,128)(2,1)}, u32[]{:S(2)}, u32[]{:S(2)}) collective-permute-start(bf16[3,2,128,256]{3,2,1,0:T(8,128)(2,1)} %get-tuple-element.119), channel_id=1, source_target_pairs={{0,1},{1,0},{2,3},{3,2},{4,5},{5,4},{6,7},{7,6},{8,9},{9,8},{10,11... | collective-permute-start | bytes 1179656 | tf_op jit(solution)/shard_map/ppermute | solution.py:277
  127.1 32.7 %collective-permute-start.36 = (bf16[3,2,128,256]{3,2,1,0:T(8,128)(2,1)S(1)}, bf16[3,2,128,256]{3,2,1,0:T(8,128)(2,1)}, u32[]{:S(2)}, u32[]{:S(2)}) collective-permute-start(bf16[3,2,128,256]{3,2,1,0:T(8,128)(2,1)S(1)} %copy-done.29), channel_id=1, source_target_pairs={{0,2},{1,3},{2,0},{3,1},{4,6},{5,7},{6,4},{7,5},{8,10},{9,11},{10,... | collective-permute-start | bytes 1179656 | tf_op jit(solution)/shard_map/ppermute | solution.py:277
  134.0 27.0 %collective-permute-start.37 = (bf16[3,2,128,256]{3,2,1,0:T(8,128)(2,1)S(1)}, bf16[3,2,128,256]{3,2,1,0:T(8,128)(2,1)}, u32[]{:S(2)}, u32[]{:S(2)}) collective-permute-start(bf16[3,2,128,256]{3,2,1,0:T(8,128)(2,1)S(1)} %copy-done.28), channel_id=1, source_target_pairs={{0,3},{1,2},{2,1},{3,0},{4,7},{5,6},{6,5},{7,4},{8,11},{9,10},{10,... | collective-permute-start | bytes 1179656 | tf_op jit(solution)/shard_map/ppermute | solution.py:277
  135.6 32.9 %collective-permute-start.29 = (bf16[3,2,128,256]{3,2,1,0:T(8,128)(2,1)S(1)}, bf16[3,2,128,256]{3,2,1,0:T(8,128)(2,1)}, u32[]{:S(2)}, u32[]{:S(2)}) collective-permute-start(bf16[3,2,128,256]{3,2,1,0:T(8,128)(2,1)S(1)} %copy-done.26), channel_id=1, source_target_pairs={{0,1},{1,0},{2,3},{3,2},{4,5},{5,4},{6,7},{7,6},{8,9},{9,8},{10,11... | collective-permute-start | bytes 1179656 | tf_op jit(solution)/shard_map/ppermute | solution.py:277
  136.9 33.1 %collective-permute-start.30 = (bf16[3,2,128,256]{3,2,1,0:T(8,128)(2,1)S(1)}, bf16[3,2,128,256]{3,2,1,0:T(8,128)(2,1)}, u32[]{:S(2)}, u32[]{:S(2)}) collective-permute-start(bf16[3,2,128,256]{3,2,1,0:T(8,128)(2,1)S(1)} %copy-done.25), channel_id=1, source_target_pairs={{0,2},{1,3},{2,0},{3,1},{4,6},{5,7},{6,4},{7,5},{8,10},{9,11},{10,... | collective-permute-start | bytes 1179656 | tf_op jit(solution)/shard_map/ppermute | solution.py:277
  158.2 11.9 %collective-permute-start.31 = (bf16[3,2,128,256]{3,2,1,0:T(8,128)(2,1)S(1)}, bf16[3,2,128,256]{3,2,1,0:T(8,128)(2,1)S(1)}, u32[]{:S(2)}, u32[]{:S(2)}) collective-permute-start(bf16[3,2,128,256]{3,2,1,0:T(8,128)(2,1)S(1)} %copy-done.24), channel_id=1, source_target_pairs={{0,3},{1,2},{2,1},{3,0},{4,7},{5,6},{6,5},{7,4},{8,11},{9,10},{10,... | collective-permute-start | bytes 1179656 | tf_op jit(solution)/shard_map/ppermute | solution.py:277
  159.7 18.6 %collective-permute-start.23 = (bf16[3,2,128,256]{3,2,1,0:T(8,128)(2,1)S(1)}, bf16[3,2,128,256]{3,2,1,0:T(8,128)(2,1)}, u32[]{:S(2)}, u32[]{:S(2)}) collective-permute-start(bf16[3,2,128,256]{3,2,1,0:T(8,128)(2,1)S(1)} %copy-done.27), channel_id=1, source_target_pairs={{0,1},{1,0},{2,3},{3,2},{4,5},{5,4},{6,7},{7,6},{8,9},{9,8},{10,11... | collective-permute-start | bytes 1179656 | tf_op jit(solution)/shard_map/ppermute | solution.py:277
  161.0 17.8 %collective-permute-start.24 = (bf16[3,2,128,256]{3,2,1,0:T(8,128)(2,1)}, bf16[3,2,128,256]{3,2,1,0:T(8,128)(2,1)}, u32[]{:S(2)}, u32[]{:S(2)}) collective-permute-start(bf16[3,2,128,256]{3,2,1,0:T(8,128)(2,1)} %get-tuple-element.102), channel_id=1, source_target_pairs={{0,2},{1,3},{2,0},{3,1},{4,6},{5,7},{6,4},{7,5},{8,10},{9,11},{10,... | collective-permute-start | bytes 1179656 | tf_op jit(solution)/shard_map/ppermute | solution.py:277
  168.5 11.2 %collective-permute-start.25 = (bf16[3,2,128,256]{3,2,1,0:T(8,128)(2,1)}, bf16[3,2,128,256]{3,2,1,0:T(8,128)(2,1)}, u32[]{:S(2)}, u32[]{:S(2)}) collective-permute-start(bf16[3,2,128,256]{3,2,1,0:T(8,128)(2,1)} %get-tuple-element.103), channel_id=1, source_target_pairs={{0,3},{1,2},{2,1},{3,0},{4,7},{5,6},{6,5},{7,4},{8,11},{9,10},{10,... | collective-permute-start | bytes 1179656 | tf_op jit(solution)/shard_map/ppermute | solution.py:277
  170.1 79.1 %collective-permute-start.41 = (f32[4,96,768]{2,1,0:T(8,128)S(1)}, f32[4,96,768]{2,1,0:T(8,128)S(1)}, u32[]{:S(2)}, u32[]{:S(2)}) collective-permute-start(f32[4,96,768]{2,1,0:T(8,128)S(1)} %constant_dynamic-slice_fusion.4), channel_id=1, source_target_pairs={{0,4},{4,0},{8,12},{12,8},{16,20},{20,16},{24,28},{28,24},{1,5},{5... | collective-permute-start | bytes 3538952 | tf_op jit(solution)/shard_map/ppermute | solution.py:277
  170.1 17.6 %collective-permute-start.49 = (bf16[512,256]{1,0:T(8,128)(2,1)S(1)}, bf16[512,256]{1,0:T(8,128)(2,1)S(1)}, u32[]{:S(2)}, u32[]{:S(2)}) collective-permute-start(bf16[512,256]{1,0:T(8,128)(2,1)S(1)} %dynamic-slice_convert_fusion.2), channel_id=1, source_target_pairs={{0,4},{4,0},{8,12},{12,8},{16,20},{20,16},{24,28},{28,24},{1,5},{5... | collective-permute-start | bytes 786440 | tf_op jit(solution)/shard_map/ppermute | solution.py:277
  178.3 10.6 %collective-permute-start.55 = (bf16[512,256]{1,0:T(8,128)(2,1)}, bf16[512,256]{1,0:T(8,128)(2,1)S(1)}, u32[]{:S(2)}, u32[]{:S(2)}) collective-permute-start(bf16[512,256]{1,0:T(8,128)(2,1)} %dynamic-slice_convert_fusion.1), channel_id=1, source_target_pairs={{0,4},{4,0},{8,12},{12,8},{16,20},{20,16},{24,28},{28,24},{1,5},{5... | collective-permute-start | bytes 786440 | tf_op jit(solution)/shard_map/ppermute | solution.py:277
  186.6 19.8 %collective-permute-start.38 = (bf16[3,2,128,256]{3,2,1,0:T(8,128)(2,1)S(1)}, bf16[3,2,128,256]{3,2,1,0:T(8,128)(2,1)S(1)}, u32[]{:S(2)}, u32[]{:S(2)}) collective-permute-start(bf16[3,2,128,256]{3,2,1,0:T(8,128)(2,1)S(1)} %copy-done.23), channel_id=1, source_target_pairs={{0,1},{1,0},{2,3},{3,2},{4,5},{5,4},{6,7},{7,6},{8,9},{9,8},{10,11... | collective-permute-start | bytes 1179656 | tf_op jit(solution)/shard_map/ppermute | solution.py:277
  187.7 20.0 %collective-permute-start.39 = (bf16[3,2,128,256]{3,2,1,0:T(8,128)(2,1)S(1)}, bf16[3,2,128,256]{3,2,1,0:T(8,128)(2,1)S(1)}, u32[]{:S(2)}, u32[]{:S(2)}) collective-permute-start(bf16[3,2,128,256]{3,2,1,0:T(8,128)(2,1)S(1)} %copy-done.22), channel_id=1, source_target_pairs={{0,2},{1,3},{2,0},{3,1},{4,6},{5,7},{6,4},{7,5},{8,10},{9,11},{10,... | collective-permute-start | bytes 1179656 | tf_op jit(solution)/shard_map/ppermute | solution.py:277
  188.9 20.7 %collective-permute-start.40 = (bf16[3,2,128,256]{3,2,1,0:T(8,128)(2,1)S(1)}, bf16[3,2,128,256]{3,2,1,0:T(8,128)(2,1)S(1)}, u32[]{:S(2)}, u32[]{:S(2)}) collective-permute-start(bf16[3,2,128,256]{3,2,1,0:T(8,128)(2,1)S(1)} %copy-done.21), channel_id=1, source_target_pairs={{0,3},{1,2},{2,1},{3,0},{4,7},{5,6},{6,5},{7,4},{8,11},{9,10},{10,... | collective-permute-start | bytes 1179656 | tf_op jit(solution)/shard_map/ppermute | solution.py:277
  190.4 5.1 %collective-permute-start.50 = (bf16[256,256]{1,0:T(8,128)(2,1)S(1)}, bf16[256,256]{1,0:T(8,128)(2,1)S(1)}, u32[]{:S(2)}, u32[]{:S(2)}) collective-permute-start(bf16[256,256]{1,0:T(8,128)(2,1)S(1)} %dynamic-slice_convert_fusion.5), channel_id=1, source_target_pairs={{0,8},{4,12},{8,0},{12,4},{16,24},{20,28},{24,16},{28,20},{1,9},{5... | collective-permute-start | bytes 393224 | tf_op jit(solution)/shard_map/ppermute | solution.py:277
  195.5 5.0 %collective-permute-start.56 = (bf16[256,256]{1,0:T(8,128)(2,1)S(1)}, bf16[256,256]{1,0:T(8,128)(2,1)S(1)}, u32[]{:S(2)}, u32[]{:S(2)}) collective-permute-start(bf16[256,256]{1,0:T(8,128)(2,1)S(1)} %dynamic-slice_convert_fusion.4), channel_id=1, source_target_pairs={{0,8},{4,12},{8,0},{12,4},{16,24},{20,28},{24,16},{28,20},{1,9},{5... | collective-permute-start | bytes 393224 | tf_op jit(solution)/shard_map/ppermute | solution.py:277
  200.5 5.0 %collective-permute-start.62 = (bf16[256,256]{1,0:T(8,128)(2,1)S(1)}, bf16[256,256]{1,0:T(8,128)(2,1)S(1)}, u32[]{:S(2)}, u32[]{:S(2)}) collective-permute-start(bf16[256,256]{1,0:T(8,128)(2,1)S(1)} %dynamic-slice_convert_fusion.3), channel_id=1, source_target_pairs={{0,8},{4,12},{8,0},{12,4},{16,24},{20,28},{24,16},{28,20},{1,9},{5... | collective-permute-start | bytes 393224 | tf_op jit(solution)/shard_map/ppermute | solution.py:277
  205.4 12.3 %collective-permute-start.32 = (bf16[3,2,128,256]{3,2,1,0:T(8,128)(2,1)}, bf16[3,2,128,256]{3,2,1,0:T(8,128)(2,1)S(1)}, u32[]{:S(2)}, u32[]{:S(2)}) collective-permute-start(bf16[3,2,128,256]{3,2,1,0:T(8,128)(2,1)} %get-tuple-element.114), channel_id=1, source_target_pairs={{0,1},{1,0},{2,3},{3,2},{4,5},{5,4},{6,7},{7,6},{8,9},{9,8},{10,11... | collective-permute-start | bytes 1179656 | tf_op jit(solution)/shard_map/ppermute | solution.py:277
  206.5 16.6 %collective-permute-start.33 = (bf16[3,2,128,256]{3,2,1,0:T(8,128)(2,1)}, bf16[3,2,128,256]{3,2,1,0:T(8,128)(2,1)S(1)}, u32[]{:S(2)}, u32[]{:S(2)}) collective-permute-start(bf16[3,2,128,256]{3,2,1,0:T(8,128)(2,1)} %get-tuple-element.115), channel_id=1, source_target_pairs={{0,2},{1,3},{2,0},{3,1},{4,6},{5,7},{6,4},{7,5},{8,10},{9,11},{10,... | collective-permute-start | bytes 1179656 | tf_op jit(solution)/shard_map/ppermute | solution.py:277
  207.7 19.4 %collective-permute-start.34 = (bf16[3,2,128,256]{3,2,1,0:T(8,128)(2,1)}, bf16[3,2,128,256]{3,2,1,0:T(8,128)(2,1)}, u32[]{:S(2)}, u32[]{:S(2)}) collective-permute-start(bf16[3,2,128,256]{3,2,1,0:T(8,128)(2,1)} %get-tuple-element.116), channel_id=1, source_target_pairs={{0,3},{1,2},{2,1},{3,0},{4,7},{5,6},{6,5},{7,4},{8,11},{9,10},{10,... | collective-permute-start | bytes 1179656 | tf_op jit(solution)/shard_map/ppermute | solution.py:277
  209.6 25.9 %collective-permute-start.26 = (bf16[3,2,128,256]{3,2,1,0:T(8,128)(2,1)}, bf16[3,2,128,256]{3,2,1,0:T(8,128)(2,1)S(1)}, u32[]{:S(2)}, u32[]{:S(2)}) collective-permute-start(bf16[3,2,128,256]{3,2,1,0:T(8,128)(2,1)} %get-tuple-element.105), channel_id=1, source_target_pairs={{0,1},{1,0},{2,3},{3,2},{4,5},{5,4},{6,7},{7,6},{8,9},{9,8},{10,11... | collective-permute-start | bytes 1179656 | tf_op jit(solution)/shard_map/ppermute | solution.py:277
  217.7 19.4 %collective-permute-start.27 = (bf16[3,2,128,256]{3,2,1,0:T(8,128)(2,1)}, bf16[3,2,128,256]{3,2,1,0:T(8,128)(2,1)S(1)}, u32[]{:S(2)}, u32[]{:S(2)}) collective-permute-start(bf16[3,2,128,256]{3,2,1,0:T(8,128)(2,1)} %get-tuple-element.106), channel_id=1, source_target_pairs={{0,2},{1,3},{2,0},{3,1},{4,6},{5,7},{6,4},{7,5},{8,10},{9,11},{10,... | collective-permute-start | bytes 1179656 | tf_op jit(solution)/shard_map/ppermute | solution.py:277
  223.1 19.2 %collective-permute-start.28 = (bf16[3,2,128,256]{3,2,1,0:T(8,128)(2,1)}, bf16[3,2,128,256]{3,2,1,0:T(8,128)(2,1)S(1)}, u32[]{:S(2)}, u32[]{:S(2)}) collective-permute-start(bf16[3,2,128,256]{3,2,1,0:T(8,128)(2,1)} %get-tuple-element.107), channel_id=1, source_target_pairs={{0,3},{1,2},{2,1},{3,0},{4,7},{5,6},{6,5},{7,4},{8,11},{9,10},{10,... | collective-permute-start | bytes 1179656 | tf_op jit(solution)/shard_map/ppermute | solution.py:277
  227.1 23.9 %collective-permute-start.51 = (bf16[128,256]{1,0:T(8,128)(2,1)S(1)}, bf16[128,256]{1,0:T(8,128)(2,1)S(1)}, u32[]{:S(2)}, u32[]{:S(2)}) collective-permute-start(bf16[128,256]{1,0:T(8,128)(2,1)S(1)} %dynamic-slice_convert_fusion.8), channel_id=1, source_target_pairs={{0,16},{4,20},{8,24},{12,28},{16,0},{20,4},{24,8},{28,12},{1,17},{... | collective-permute-start | bytes 196616 | tf_op jit(solution)/shard_map/ppermute | solution.py:277
  235.6 16.8 %collective-permute-start.57 = (bf16[128,256]{1,0:T(8,128)(2,1)S(1)}, bf16[128,256]{1,0:T(8,128)(2,1)S(1)}, u32[]{:S(2)}, u32[]{:S(2)}) collective-permute-start(bf16[128,256]{1,0:T(8,128)(2,1)S(1)} %dynamic-slice_convert_fusion.7), channel_id=1, source_target_pairs={{0,16},{4,20},{8,24},{12,28},{16,0},{20,4},{24,8},{28,12},{1,17},{... | collective-permute-start | bytes 196616 | tf_op jit(solution)/shard_map/ppermute | solution.py:277
  237.2 16.9 %collective-permute-start.63 = (bf16[128,256]{1,0:T(8,128)(2,1)S(1)}, bf16[128,256]{1,0:T(8,128)(2,1)S(1)}, u32[]{:S(2)}, u32[]{:S(2)}) collective-permute-start(bf16[128,256]{1,0:T(8,128)(2,1)S(1)} %dynamic-slice_convert_fusion.6), channel_id=1, source_target_pairs={{0,16},{4,20},{8,24},{12,28},{16,0},{20,4},{24,8},{28,12},{1,17},{... | collective-permute-start | bytes 196616 | tf_op jit(solution)/shard_map/ppermute | solution.py:277
  249.4 15.7 %collective-permute-start.42 = (f32[4,48,768]{2,1,0:T(8,128)S(1)}, f32[4,48,768]{2,1,0:T(8,128)S(1)}, u32[]{:S(2)}, u32[]{:S(2)}) collective-permute-start(f32[4,48,768]{2,1,0:T(8,128)S(1)} %constant_dynamic-slice_fusion.3), channel_id=1, source_target_pairs={{0,8},{4,12},{8,0},{12,4},{16,24},{20,28},{24,16},{28,20},{1,9},{5... | collective-permute-start | bytes 1769480 | tf_op jit(solution)/shard_map/ppermute | solution.py:277
  251.0 15.8 %collective-permute-start.52 = (bf16[128,256]{1,0:T(8,128)(2,1)S(1)}, bf16[128,256]{1,0:T(8,128)(2,1)S(1)}, u32[]{:S(2)}, u32[]{:S(2)}) collective-permute-start(bf16[128,256]{1,0:T(8,128)(2,1)S(1)} %add_convert_fusion.2), channel_id=1, source_target_pairs={{0,16},{4,20},{8,24},{12,28},{16,0},{20,4},{24,8},{28,12},{1,17},{... | collective-permute-start | bytes 196616 | tf_op jit(solution)/shard_map/ppermute | solution.py:277
  252.4 17.1 %collective-permute-start.58 = (bf16[128,256]{1,0:T(8,128)(2,1)S(1)}, bf16[128,256]{1,0:T(8,128)(2,1)S(1)}, u32[]{:S(2)}, u32[]{:S(2)}) collective-permute-start(bf16[128,256]{1,0:T(8,128)(2,1)S(1)} %add_convert_fusion.1), channel_id=1, source_target_pairs={{0,16},{4,20},{8,24},{12,28},{16,0},{20,4},{24,8},{28,12},{1,17},{... | collective-permute-start | bytes 196616 | tf_op jit(solution)/shard_map/ppermute | solution.py:277
  254.1 15.4 %collective-permute-start.64 = (bf16[128,256]{1,0:T(8,128)(2,1)S(1)}, bf16[128,256]{1,0:T(8,128)(2,1)S(1)}, u32[]{:S(2)}, u32[]{:S(2)}) collective-permute-start(bf16[128,256]{1,0:T(8,128)(2,1)S(1)} %add_convert_fusion), channel_id=1, source_target_pairs={{0,16},{4,20},{8,24},{12,28},{16,0},{20,4},{24,8},{28,12},{1,17},{... | collective-permute-start | bytes 196616 | tf_op jit(solution)/shard_map/ppermute | solution.py:277
  265.2 14.6 %collective-permute-start.43 = (f32[4,24,768]{2,1,0:T(8,128)S(1)}, f32[4,24,768]{2,1,0:T(8,128)S(1)}, u32[]{:S(2)}, u32[]{:S(2)}) collective-permute-start(f32[4,24,768]{2,1,0:T(8,128)S(1)} %constant_dynamic-slice_fusion.2), channel_id=1, source_target_pairs={{0,16},{4,20},{8,24},{12,28},{16,0},{20,4},{24,8},{28,12},{1,17},{... | collective-permute-start | bytes 884744 | tf_op jit(solution)/shard_map/ppermute | solution.py:277
  266.9 13.9 %collective-permute-start.53 = (bf16[256,256]{1,0:T(8,128)(2,1)S(1)}, bf16[256,256]{1,0:T(8,128)(2,1)S(1)}, u32[]{:S(2)}, u32[]{:S(2)}) collective-permute-start(bf16[256,256]{1,0:T(8,128)(2,1)S(1)} %maximum_select_fusion.13), channel_id=1, source_target_pairs={{0,8},{4,12},{8,0},{12,4},{16,24},{20,28},{24,16},{28,20},{1,9},{5... | collective-permute-start | bytes 393224 | tf_op jit(solution)/shard_map/ppermute | solution.py:277
  269.5 11.5 %collective-permute-start.59 = (bf16[256,256]{1,0:T(8,128)(2,1)S(1)}, bf16[256,256]{1,0:T(8,128)(2,1)S(1)}, u32[]{:S(2)}, u32[]{:S(2)}) collective-permute-start(bf16[256,256]{1,0:T(8,128)(2,1)S(1)} %maximum_select_fusion.14), channel_id=1, source_target_pairs={{0,8},{4,12},{8,0},{12,4},{16,24},{20,28},{24,16},{28,20},{1,9},{5... | collective-permute-start | bytes 393224 | tf_op jit(solution)/shard_map/ppermute | solution.py:277
  269.6 16.6 %collective-permute-start.65 = (bf16[256,256]{1,0:T(8,128)(2,1)S(1)}, bf16[256,256]{1,0:T(8,128)(2,1)S(1)}, u32[]{:S(2)}, u32[]{:S(2)}) collective-permute-start(bf16[256,256]{1,0:T(8,128)(2,1)S(1)} %maximum_select_fusion.15), channel_id=1, source_target_pairs={{0,8},{4,12},{8,0},{12,4},{16,24},{20,28},{24,16},{28,20},{1,9},{5... | collective-permute-start | bytes 393224 | tf_op jit(solution)/shard_map/ppermute | solution.py:277
  279.8 5.3 %collective-permute-start.44 = (f32[2,24,768]{2,1,0:T(8,128)S(1)}, f32[2,24,768]{2,1,0:T(8,128)S(1)}, u32[]{:S(2)}, u32[]{:S(2)}) collective-permute-start(f32[2,24,768]{2,1,0:T(8,128)S(1)} %constant_dynamic-slice_fusion.1), channel_id=1, source_target_pairs={{0,2},{1,3},{2,0},{3,1},{4,6},{5,7},{6,4},{7,5},{8,10},{9,11},{10,... | collective-permute-start | bytes 442376 | tf_op jit(solution)/shard_map/ppermute | solution.py:277
  280.8 8.9 %collective-permute-start.54 = (bf16[512,256]{1,0:T(8,128)(2,1)S(1)}, bf16[512,256]{1,0:T(8,128)(2,1)S(1)}, u32[]{:S(2)}, u32[]{:S(2)}) collective-permute-start(bf16[512,256]{1,0:T(8,128)(2,1)S(1)} %maximum_select_fusion.8), channel_id=1, source_target_pairs={{0,4},{4,0},{8,12},{12,8},{16,20},{20,16},{24,28},{28,24},{1,5},{5... | collective-permute-start | bytes 786440 | tf_op jit(solution)/shard_map/ppermute | solution.py:277
  281.0 14.1 %collective-permute-start.60 = (bf16[512,256]{1,0:T(8,128)(2,1)S(1)}, bf16[512,256]{1,0:T(8,128)(2,1)S(1)}, u32[]{:S(2)}, u32[]{:S(2)}) collective-permute-start(bf16[512,256]{1,0:T(8,128)(2,1)S(1)} %maximum_select_fusion.9), channel_id=1, source_target_pairs={{0,4},{4,0},{8,12},{12,8},{16,20},{20,16},{24,28},{28,24},{1,5},{5... | collective-permute-start | bytes 786440 | tf_op jit(solution)/shard_map/ppermute | solution.py:277
  285.2 4.4 %collective-permute-start.45 = (f32[1,24,768]{2,1,0:T(8,128)S(1)}, f32[1,24,768]{2,1,0:T(8,128)S(1)}, u32[]{:S(2)}, u32[]{:S(2)}) collective-permute-start(f32[1,24,768]{2,1,0:T(8,128)S(1)} %constant_dynamic-slice_fusion), channel_id=1, source_target_pairs={{0,1},{1,0},{2,3},{3,2},{4,5},{5,4},{6,7},{7,6},{8,9},{9,8},{10,11... | collective-permute-start | bytes 221192 | tf_op jit(solution)/shard_map/ppermute | solution.py:277
  286.3 14.1 %collective-permute-start.66 = (bf16[512,256]{1,0:T(8,128)(2,1)S(1)}, bf16[512,256]{1,0:T(8,128)(2,1)S(1)}, u32[]{:S(2)}, u32[]{:S(2)}) collective-permute-start(bf16[512,256]{1,0:T(8,128)(2,1)S(1)} %maximum_select_fusion.10), channel_id=1, source_target_pairs={{0,4},{4,0},{8,12},{12,8},{16,20},{20,16},{24,28},{28,24},{1,5},{5... | collective-permute-start | bytes 786440 | tf_op jit(solution)/shard_map/ppermute | solution.py:277
  289.6 5.4 %collective-permute-start.46 = (f32[1,24,768]{2,1,0:T(8,128)S(1)}, f32[1,24,768]{2,1,0:T(8,128)S(1)}, u32[]{:S(2)}, u32[]{:S(2)}) collective-permute-start(f32[1,24,768]{2,1,0:T(8,128)S(1)} %dynamic-slice_add_fusion.4), channel_id=1, source_target_pairs={{0,16},{4,20},{8,24},{12,28},{16,0},{20,4},{24,8},{28,12},{1,17},{... | collective-permute-start | bytes 221192 | tf_op jit(solution)/shard_map/ppermute | solution.py:277
  295.1 5.2 %collective-permute-start.47 = (f32[1,48,768]{2,1,0:T(8,128)S(1)}, f32[1,48,768]{2,1,0:T(8,128)S(1)}, u32[]{:S(2)}, u32[]{:S(2)}) collective-permute-start(f32[1,48,768]{2,1,0:T(8,128)S(1)} %maximum_select_fusion.12), channel_id=1, source_target_pairs={{0,8},{4,12},{8,0},{12,4},{16,24},{20,28},{24,16},{28,20},{1,9},{5... | collective-permute-start | bytes 442376 | tf_op jit(solution)/shard_map/ppermute | solution.py:277
  (49 other events, 278.3 us)
where the time goes:
time: 305 us; the launch traced here: 303 us
  Pallas kernels  121 us (40%)
  starting transfers between devices  82.8 us (27%)
  waiting for transfers between devices  64.2 us (21%)
  other arithmetic  14 us (5%)
  matrix products  13.2 us (4%)
  local copies, waits for them, and re-layouts  5.99 us (2%)
    ppermute x67, starting transfers between devices, swap(): return lax.ppermute(value, axis, [(i, i ^ bit) for i in range(size)])  82.8 us
    ppermute x67, waiting for transfers between devices, swap(): return lax.ppermute(value, axis, [(i, i ^ bit) for i in range(size)])  64.2 us
    pallas_call x6, Pallas kernels, outer(): pl.pallas_call(functools.partial(outer_kernel, devices, add), grid=grid,...  36.6 us
    pallas_call x3, Pallas kernels, gate(): pl.pallas_call(functools.partial(gate_kernel, devices), grid=grid, in_spe...  36 us
    pallas_call x3, Pallas kernels, back_middle(): pl.pallas_call(functools.partial(back_middle_kernel, devices), grid=grid,...  16.2 us
    pallas_call x3, Pallas kernels, middle(): pl.pallas_call(functools.partial(middle_kernel, devices), grid=grid, in_s...  16 us
    pallas_call x3, Pallas kernels, first(): pl.pallas_call(functools.partial(first_kernel, devices), grid=grid, in_sp...  11.5 us
    dot_general x1, matrix products, dot_last(): lax.dot_general(left, right, (((1,), (1,)), ((), ())), preferred_element_...  9.13 us
  transfers between devices with their start and end apart: 67, of which 18 were waited for; matrix products, arithmetic and copies ran while one was open for 9% of the time, Pallas kernels for 40%

commit v1 on v0

v1 whole, which is shorter than its diff:
```python
import functools
import math

import jax
import jax.numpy as jnp
from jax import lax
from jax.experimental import pallas as pl
from jax.experimental.pallas import tpu as pltpu
from jax.sharding import PartitionSpec as P

BATCH = 3
SEQ = 4096
HALF = 8

BF16 = jnp.bfloat16
F32 = jnp.float32


def contract(form, left, right):
    return jnp.einsum(form, left, right, preferred_element_type=jnp.float32)


def dot(left, right):
    return jnp.dot(left, right, preferred_element_type=F32)


def dot_first(left, right):
    return lax.dot_general(left, right, (((0,), (0,)), ((), ())), preferred_element_type=F32)


def dot_last(left, right):
    return lax.dot_general(left, right, (((1,), (1,)), ((), ())), preferred_element_type=F32)


def params(grid):
    return pltpu.CompilerParams(
        dimension_semantics=("arbitrary",) * len(grid), vmem_limit_bytes=56 * 1024 * 1024
    )


def cost(flops, bytes_accessed):
    return pl.CostEstimate(flops=1000, bytes_accessed=1000, transcendentals=0)


def put_pair(outs, where, low, first, second, own, columns=slice(None)):
    for r, out in enumerate(outs):
        for g in range(own // HALF):
            at = r * own + g * HALF
            rows = jnp.concatenate([first[at : at + HALF], second[at : at + HALF]], axis=0)
            out[where, g, low : low + 2 * HALF, columns] = rows.astype(BF16)


def expand_kernel(devices, left_in, left_out, right_in, right_out, right_turned, *outs):
    big_li, big_qo, big_pt, big_rt, small_qt, small_lt = outs
    own, block = left_in.shape[0], left_in.shape[1]
    wide = block * HALF
    s = lax.broadcasted_iota(jnp.int32, (block, wide), 0)
    lane = lax.broadcasted_iota(jnp.int32, (block, wide), 1)
    picks = [
        jnp.where(lane == s * HALF + t, 1.0, 0.0).astype(BF16) for t in range(HALF)
    ]
    row = lax.broadcasted_iota(jnp.int32, (block, block), 0)
    column = lax.broadcasted_iota(jnp.int32, (block, block), 1)
    same = jnp.where(row == column, 1.0, 0.0).astype(BF16)
    for p in range(own):
        g, t = divmod(p, HALF)
        rows = slice(t * block, (t + 1) * block)
        big_li[g, rows, :] = dot(left_in[p], picks[t]).astype(BF16)
        big_qo[g, rows, :] = dot(right_out[p], picks[t]).astype(BF16)
        big_pt[g, rows, :] = dot_first(left_out[p], picks[t]).astype(BF16)
        big_rt[g, rows, :] = dot_first(right_in[p], picks[t]).astype(BF16)
        small_qt[p] = dot_last(same, right_turned[p]).astype(BF16)
        small_lt[p] = dot_last(same, left_in[p]).astype(BF16)


def expand(devices, left_in, left_out, right_in, right_out, right_turned):
    own, block = left_in.shape[0], left_in.shape[1]
    big = jax.ShapeDtypeStruct((own // HALF, HALF * block, HALF * block), BF16)
    small = jax.ShapeDtypeStruct(left_in.shape, BF16)
    return pl.pallas_call(
        functools.partial(expand_kernel, devices),
        out_shape=(big,) * 4 + (small,) * 2,
        compiler_params=params(()),
        cost_estimate=cost(4e9, 8e6),
    )(left_in, left_out, right_in, right_out, right_turned)


def each(refs, devices):
    return refs if len(refs) == devices else [refs[0].at[r] for r in range(devices)]


def piece_shapes(devices, joint, batch, own, width):
    shape = (batch, own // HALF, own * HALF, width)
    if joint:
        return [jax.ShapeDtypeStruct((devices,) + shape, BF16)]
    return [jax.ShapeDtypeStruct(shape, BF16)] * devices


def piece_specs(devices, joint, block, index):
    if joint:
        return [pl.BlockSpec((devices,) + block, lambda *at: (0,) + index(*at))]
    return [pl.BlockSpec(block, index)] * devices


def first_kernel(devices, right_in, acts, *refs):
    own = right_in.shape[0]
    outs = each(refs, devices)
    for b in range(acts.shape[0]):
        for p in range(0, own, 2):
            low, high = dot(right_in[p], acts[b, p]), dot(right_in[p + 1], acts[b, p + 1])
            put_pair(outs, b, p * HALF, low, high, own)


def first(devices, width, joint, right_in, acts):
    batch, own, block, full = acts.shape
    grid = (full // width,)
    shapes = piece_shapes(devices, joint, batch, own, full)
    return pl.pallas_call(
        functools.partial(first_kernel, devices),
        grid=grid,
        in_specs=[
            pl.BlockSpec(right_in.shape, lambda c: (0, 0, 0)),
            pl.BlockSpec((batch, own, block, width), lambda c: (0, 0, 0, c)),
        ],
        out_specs=piece_specs(
            devices, joint, shapes[0].shape[-4:-1] + (width,), lambda c: (0, 0, 0, c)
        ),
        out_shape=shapes,
        compiler_params=params(grid),
        cost_estimate=cost(1e9, 1e6),
    )(right_in, acts)


def middle_kernel(devices, count, small, big, kern, *refs):
    pieces, outs, second = each(refs[:count], devices), each(refs[count:-1], devices), refs[-1]
    half, block = small.shape[0], small.shape[1]
    own = block // devices
    scale = kern[0].astype(F32)
    for b in range(second.shape[0]):
        spread = jnp.concatenate([piece[b, 0] for piece in pieces], axis=0)
        value = dot(big[0], spread)
        second[b, 0] = value
        weighted = (value * scale).astype(BF16)
        for i in range(0, half, 2):
            low = dot(small[i], weighted[i * block : (i + 1) * block])
            high = dot(small[i + 1], weighted[(i + 1) * block : (i + 2) * block])
            put_pair(outs, b, i * HALF, low, high, own)


def middle(devices, width, joint_in, joint, small, big, kern, pieces):
    batch, parts, long, full = pieces[0].shape[-4:]
    block = small.shape[1]
    second = jax.ShapeDtypeStruct((batch, parts, HALF * block, full), F32)
    grid = (parts, full // width)
    return pl.pallas_call(
        functools.partial(middle_kernel, devices, len(pieces)),
        grid=grid,
        in_specs=[
            pl.BlockSpec((HALF, block, block), lambda g, c: (g, 0, 0)),
            pl.BlockSpec((1,) + big.shape[1:], lambda g, c: (g, 0, 0)),
            pl.BlockSpec((1, HALF * block, width), lambda g, c: (g, 0, c)),
        ]
        + piece_specs(devices, joint_in, (batch, 1, long, width), lambda g, c: (0, g, 0, c)),
        out_specs=piece_specs(
            devices, joint, (batch, parts, HALF * HALF, width), lambda g, c: (0, 0, g, c)
        )
        + [pl.BlockSpec((batch, 1, HALF * block, width), lambda g, c: (0, g, 0, c))],
        out_shape=piece_shapes(devices, joint, batch, small.shape[0], full) + [second],
        compiler_params=params(grid),
        cost_estimate=cost(3e9, 8e6),
    )(small, big, kern, *pieces)


def back_middle_kernel(devices, count, small, big, kern, second, *refs):
    pieces, outs, total = each(refs[:count], devices), each(refs[count:-1], devices), refs[-1]
    half, block = small.shape[0], small.shape[1]
    own = block // devices
    scale = kern[0].astype(F32)
    tally = None
    for b in range(second.shape[0]):
        spread = jnp.concatenate([piece[b, 0] for piece in pieces], axis=0)
        value = dot(big[0], spread)
        term = second[b, 0] * value
        tally = term if tally is None else tally + term
        weighted = (value * scale).astype(BF16)
        for i in range(0, half, 2):
            low = dot(small[i], weighted[i * block : (i + 1) * block])
            high = dot(small[i + 1], weighted[(i + 1) * block : (i + 2) * block])
            put_pair(outs, b, i * HALF, low, high, own)
    total[0] = tally


def back_middle(devices, c, width, joint_in, joint, small, big, kern, second, pieces):
    batch, parts, long, _ = pieces[0].shape[-4:]
    block = small.shape[1]
    total = jax.ShapeDtypeStruct((parts, HALF * block, width), F32)
    grid = (parts,)
    return pl.pallas_call(
        functools.partial(back_middle_kernel, devices, len(pieces)),
        grid=grid,
        in_specs=[
            pl.BlockSpec((HALF, block, block), lambda g: (g, 0, 0)),
            pl.BlockSpec((1,) + big.shape[1:], lambda g: (g, 0, 0)),
            pl.BlockSpec((1, HALF * block, width), lambda g: (g, 0, c)),
            pl.BlockSpec((batch, 1, HALF * block, width), lambda g: (0, g, 0, c)),
        ]
        + piece_specs(devices, joint_in, (batch, 1, long, width), lambda g: (0, g, 0, c)),
        out_specs=piece_specs(
            devices, joint, (batch, parts, HALF * HALF, width), lambda g: (0, 0, g, 0)
        )
        + [pl.BlockSpec((1, HALF * block, width), lambda g: (g, 0, 0))],
        out_shape=piece_shapes(devices, joint, batch, small.shape[0], width) + [total],
        compiler_params=params(grid),
        cost_estimate=cost(3e9, 8e6),
    )(small, big, kern, second, *pieces)


def gate_kernel(devices, width, small, weights, flat, upstream, *refs):
    pieces, sloped = refs[:-1], refs[-1]
    block = small.shape[1]
    own = block // devices
    rows = 4 * block
    for low in range(0, flat.shape[1], rows):
        here = slice(low, low + rows)
        for columns in (slice(0, width), slice(width, 2 * width)):
            preact = dot(flat[0, here, :], weights[:, columns].astype(BF16))
            sigma = 0.5 * jnp.tanh(0.5 * preact) + 0.5
            swish = preact * sigma
            slope = sigma + swish * (1.0 - sigma)
            grad = upstream[0, here, columns].astype(F32)
            sloped[0, here, columns] = grad * slope
            mix_grad = (grad * swish).astype(BF16)
            for q in range(0, 4, 2):
                k = low // block + q
                first_product = dot(small[k], mix_grad[q * block : (q + 1) * block])
                next_product = dot(small[k + 1], mix_grad[(q + 1) * block : (q + 2) * block])
                put_pair(pieces, 0, k * HALF, first_product, next_product, own, columns)


def gate(devices, small, weights, flat, upstream):
    batch, rows, full = flat.shape
    own, block = small.shape[0], small.shape[1]
    count = own // 2
    width = full // 2
    piece = jax.ShapeDtypeStruct((batch, own // HALF, own * HALF, full), BF16)
    sloped = jax.ShapeDtypeStruct((batch, rows, full), F32)
    grid = (batch, own // count)
    part = pl.BlockSpec((1, count * block, full), lambda b, q: (b, q, 0))
    return pl.pallas_call(
        functools.partial(gate_kernel, devices, width),
        grid=grid,
        in_specs=[
            pl.BlockSpec((count, block, block), lambda b, q: (q, 0, 0)),
            pl.BlockSpec((full, full), lambda b, q: (0, 0)),
            part,
            part,
        ],
        out_specs=[
            pl.BlockSpec((1, own // HALF, count * HALF, full), lambda b, q: (b, 0, q, 0))
        ]
        * devices
        + [part],
        out_shape=(piece,) * devices + (sloped,),
        compiler_params=params(grid),
        cost_estimate=cost(14e9, 30e6),
    )(small, weights, flat, upstream)


def ending_kernel(devices, count, scale, big, sloped, weights, flat, *refs):
    pieces, part, total = each(refs[:count], devices), refs[-2], refs[-1]
    step = pl.program_id(0) * pl.num_programs(1) + pl.program_id(1)

    @pl.when(step == 0)
    def _():
        total[...] = jnp.zeros_like(total)

    spread = jnp.concatenate([piece[0, 0] for piece in pieces], axis=0)
    grad = (dot(big[0], spread) * sloped[0]).astype(BF16)
    part[0] = dot_last(grad, weights[...].astype(BF16))
    total[...] += dot_first(flat[0], grad) * scale


def ending(devices, joint, scale, big, sloped, weights, flat, pieces):
    batch, parts, long, full = pieces[0].shape[-4:]
    rows = big.shape[1]
    grid = (parts, batch)
    part = pl.BlockSpec((1, rows, full), lambda g, b: (b, g, 0))
    whole = pl.BlockSpec((full, full), lambda g, b: (0, 0))
    return pl.pallas_call(
        functools.partial(ending_kernel, devices, len(pieces), scale),
        grid=grid,
        in_specs=[pl.BlockSpec((1,) + big.shape[1:], lambda g, b: (g, 0, 0)), part, whole, part]
        + piece_specs(devices, joint, (1, 1, long, full), lambda g, b: (b, g, 0, 0)),
        out_specs=[part, whole],
        out_shape=[
            jax.ShapeDtypeStruct(sloped.shape, F32),
            jax.ShapeDtypeStruct((full, full), F32),
        ],
        compiler_params=params(grid),
        cost_estimate=cost(5e9, 8e6),
    )(big, sloped, weights, flat, *pieces)


def outer_kernel(devices, add, count, big, other, *refs):
    pieces, out = each(refs[:count], devices), refs[-1]
    for b in range(out.shape[0]):
        spread = jnp.concatenate([piece[b, 0] for piece in pieces], axis=0)
        value = dot(big[0], spread)
        out[b] = (value + other[b] if add else value * other[b]).astype(BF16)


def outer(devices, c, width, joint, add, big, other, before, pieces):
    batch, parts, long, _ = pieces[0].shape[-4:]
    rows = big.shape[1]
    grid = (parts,)
    operands = [big, other, *pieces]
    specs = [
        pl.BlockSpec((1,) + big.shape[1:], lambda g: (g, 0, 0)),
        pl.BlockSpec((batch, rows, width), lambda g: (0, g, c)),
    ] + piece_specs(devices, joint, (batch, 1, long, width), lambda g: (0, g, 0, 0))
    alias = {}
    if before is not None:
        alias = {len(operands): 0}
        operands.append(before)
        specs.append(pl.BlockSpec(memory_space=pl.ANY))
    return pl.pallas_call(
        functools.partial(outer_kernel, devices, add, len(pieces)),
        grid=grid,
        in_specs=specs,
        out_specs=pl.BlockSpec((batch, rows, width), lambda g: (0, g, c)),
        out_shape=jax.ShapeDtypeStruct(other.shape, BF16),
        input_output_aliases=alias,
        compiler_params=params(grid),
        cost_estimate=cost(5e9, 8e6),
    )(*operands)


def after(value, *earlier):
    return lax.optimization_barrier((value, *earlier))[0]


def swap(value, axis, bit):
    size = lax.axis_size(axis)
    return lax.ppermute(value, axis, [(i, i ^ bit) for i in range(size)])


def exchange(pieces):
    if len(pieces) == 1:
        return [lax.all_to_all(pieces[0], "seq", 0, 0, tiled=True)]
    size = len(pieces)
    order = [size - 1, *range(1, size - 1)] if size > 1 else []
    moved = {r: swap(pieces[r], "seq", r) for r in order}
    return [pieces[0]] + [moved[r] for r in range(1, size)]


def bits_of(size):
    return [1 << k for k in range(size.bit_length() - 1)]


def has(axis, bit):
    return (lax.axis_index(axis) // bit) % 2


def halve(value, axis, bit, dim, kind):
    half = value.shape[dim] // 2
    mine = has(axis, bit)
    keep = lax.dynamic_slice_in_dim(value, mine * half, half, dim)
    send = lax.dynamic_slice_in_dim(value, (1 - mine) * half, half, dim)
    return keep + swap(send.astype(kind), axis, bit).astype(F32)


def double(value, axis, bit, dim):
    other = swap(value, axis, bit)
    mine = has(axis, bit)
    return jnp.where(
        mine == 0,
        jnp.concatenate([value, other], axis=dim),
        jnp.concatenate([other, value], axis=dim),
    )


def by_peer(value, dim, axis="seq", unit=1):
    devices = lax.axis_size(axis) // unit
    shape = value.shape
    for bit in bits_of(devices):
        pairs = value.reshape(
            *shape[:dim], devices // (2 * bit), 2, bit * shape[dim] // devices, *shape[dim + 1 :]
        )
        turned = jnp.flip(pairs, axis=dim + 1)
        value = jnp.where(has(axis, bit * unit) == 0, pairs, turned).reshape(shape)
    return value


def scatter(value, axis, unit, dim, kind):
    peers = lax.axis_size(axis) // unit
    block = value.shape[dim] // peers
    me = lax.axis_index(axis) // unit
    total = lax.dynamic_slice_in_dim(value, me * block, block, dim)
    for r in range(1, peers):
        part = lax.dynamic_slice_in_dim(value, jnp.bitwise_xor(me, r) * block, block, dim)
        total = total + swap(part.astype(kind), axis, r * unit).astype(F32)
    return total


def collect(value, axis, unit, dim):
    peers = lax.axis_size(axis) // unit
    blocks = [value] + [swap(value, axis, r * unit) for r in range(1, peers)]
    return by_peer(jnp.concatenate(blocks, axis=dim), dim, axis, unit)


def gather_weights(gate_weight, earlier):
    devices = lax.axis_size("seq")
    sections = lax.axis_size("section")
    rows, width = gate_weight.shape
    shared = [bit for bit in (2, 1) if bit < sections and rows % (4 * 16) == 0]
    part = rows // (1 << len(shared))
    place = sum(has("section", bit) << k for k, bit in enumerate(shared))
    mine = lax.dynamic_slice_in_dim(gate_weight, place * part, part, 0).astype(F32)
    got = jnp.stack([mine] + [swap(mine, "seq", r) for r in range(1, devices)])
    got = by_peer(after(got, earlier), 0)
    for bit in shared:
        got = double(got, "section", bit, 1)
    return got.reshape(devices * rows, width)


def local(
    layer_input,
    grad_out,
    gate_weight,
    mix_in_right,
    mix_in_left,
    mix_out_left,
    mix_out_right,
    kernel,
):
    batch, rows, full = layer_input.shape[1:]
    own, block = mix_in_right.shape[0], mix_in_right.shape[1]
    replicas = lax.axis_size("section")
    devices = lax.axis_size("seq")
    weight_scale = 1.0 / math.sqrt(replicas * BATCH * SEQ)
    kernel_scale = 1.0 / math.sqrt(replicas * BATCH)
    width = full // 2
    flat = layer_input[0]
    upstream = grad_out[0]
    acts = flat.reshape(batch, own, block, full)
    kern = kernel.reshape(own // HALF, HALF * block, full)

    firsts = first(devices, width, True, mix_in_right, acts)
    spread = exchange(firsts)
    small_p = by_peer(after(mix_out_left, firsts), 1)
    right_turned = by_peer(after(mix_out_right, firsts), 2)
    big_li, big_qo, big_pt, big_rt, small_qt, small_lt = expand(
        devices, mix_in_left, small_p, mix_in_right, mix_out_right, right_turned
    )
    weights = gather_weights(after(gate_weight, firsts), big_li)
    *back_third, sloped = gate(devices, small_qt, weights, flat, upstream)
    back_spread = exchange(after(back_third, spread))
    *third, second = middle(
        devices, width, True, True, after(mix_out_left, sloped), big_li, kern, spread
    )
    returned = exchange(after(third, *back_spread))

    sixth = full // 6
    parts = ((0, 5 * sixth), (5, sixth))
    back_first, totals = [], []
    for c, wide in parts:
        sent, total = back_middle(
            devices, c, wide, False, True, after(small_lt, second, *totals), big_pt, kern, second,
            back_spread,
        )
        back_first.append(sent)
        totals.append(total)
    kernel_grad = jnp.concatenate(totals, axis=2).reshape(own * block, full) * kernel_scale
    kernel_grad = halve(kernel_grad, "section", 1, 0, BF16)
    kernel_grad = scatter(kernel_grad, "section", 2, 0, BF16).astype(BF16)
    back_first[0] = after(back_first[0], kernel_grad)
    gate_part, weight_grad = ending(
        devices, True, weight_scale, after(big_qo, kernel_grad), sloped, weights, flat, returned
    )
    weight_grad = weight_grad.reshape(devices, full // devices, full)
    weight_grad = halve(weight_grad, "section", 1, 1, BF16)
    weight_grad = scatter(weight_grad, "section", 2, 1, BF16)
    weight_grad = scatter(weight_grad, "seq", 1, 0, F32)
    kernel_grad = collect(kernel_grad, "section", 2, 0)
    kernel_grad = double(kernel_grad, "section", 1, 0)
    back_return = [exchange([after(back_first[0], *returned)])]
    back_return.append(exchange([after(back_first[1], *back_return[0], weight_grad)]))

    input_grad = None
    halves = []
    for (c, wide), arrived in zip(parts, back_return):
        input_grad = outer(
            devices, c, wide, True, True, big_rt, gate_part, input_grad, arrived
        )
        halves.append(input_grad)
    weight_grad = collect(after(weight_grad, *back_return[0]), "section", 2, 1)
    weight_grad = double(after(weight_grad, halves[0]), "section", 1, 1)
    weight_grad = weight_grad.reshape(full // devices, full)
    return (input_grad[None], weight_grad, kernel_grad)


def forward_middle(spread, left_in, left_out, kern):
    second_mixed = contract("ija,baid->bijd", left_in, spread)
    weighted = (second_mixed * kern).astype(jnp.bfloat16)
    third_mixed = contract("ikj,bijd->bikd", left_out, weighted).astype(jnp.bfloat16)
    return (second_mixed, third_mixed)


def backward_middle(back_spread, second_mixed, left_in, left_out, kern):
    back_second = contract("ikj,bkid->bijd", left_out, back_spread)
    kernel_sum = jnp.sum(second_mixed * back_second, axis=0)
    back_weighted = (back_second * kern).astype(jnp.bfloat16)
    back_first = contract("ija,bijd->biad", left_in, back_weighted).astype(jnp.bfloat16)
    return (kernel_sum, back_first)


def local_plain(
    layer_input,
    grad_out,
    gate_weight,
    mix_in_right,
    mix_in_left,
    mix_out_left,
    mix_out_right,
    kernel,
):
    count_batch = layer_input.shape[1]
    token_rows = layer_input.shape[2]
    width = layer_input.shape[3]
    groups = mix_in_right.shape[0]
    block_size = mix_in_right.shape[1]
    replicas = lax.axis_size("section")
    kern = kernel.reshape(groups, block_size, width).astype(jnp.float32)
    acts = layer_input[0].reshape(count_batch, groups, block_size, width)
    flat_input = layer_input[0].reshape(count_batch * token_rows, width)
    upstream = grad_out[0].reshape(count_batch * token_rows, width).astype(jnp.float32)
    weights = lax.all_gather(gate_weight, "seq", axis=0, tiled=True)
    preact = jnp.dot(flat_input, weights, preferred_element_type=jnp.float32)
    sigma = jax.nn.sigmoid(preact)
    swish = preact * sigma
    slope = sigma * (1.0 + preact * (1.0 - sigma))
    mix_grad = (
        (upstream * swish).astype(jnp.bfloat16).reshape(count_batch, groups, block_size, width)
    )
    first_mixed = contract("aic,bacd->baid", mix_in_right, acts).astype(jnp.bfloat16)
    back_third = contract("kmi,bkmd->bkid", mix_out_right, mix_grad).astype(jnp.bfloat16)
    spread = lax.all_to_all(first_mixed, "seq", split_axis=2, concat_axis=1, tiled=True)
    second_mixed, third_mixed = forward_middle(spread, mix_in_left, mix_out_left, kern)
    returned = lax.all_to_all(third_mixed, "seq", split_axis=2, concat_axis=1, tiled=True)
    back_spread = lax.all_to_all(back_third, "seq", split_axis=2, concat_axis=1, tiled=True)
    kernel_sum, back_first = backward_middle(
        back_spread, second_mixed, mix_in_left, mix_out_left, kern
    )
    back_return = lax.all_to_all(back_first, "seq", split_axis=2, concat_axis=1, tiled=True)
    mixed = contract("kmi,bikd->bkmd", mix_out_right, returned).reshape(
        count_batch * token_rows, width
    )
    gate_grad = (upstream * mixed * slope).astype(jnp.bfloat16)
    gate_part = lax.dot_general(
        gate_grad, weights, (((1,), (1,)), ((), ())), preferred_element_type=jnp.float32
    )
    weight_scale = 1.0 / math.sqrt(replicas * BATCH * SEQ)
    kernel_scale = 1.0 / math.sqrt(replicas * BATCH)
    term = lax.dot_general(
        flat_input, gate_grad, (((0,), (0,)), ((), ())), preferred_element_type=jnp.float32
    )
    weight_local = lax.psum_scatter(term * weight_scale, "seq", scatter_dimension=0, tiled=True)
    weight_grad, kernel_total = lax.psum((weight_local, kernel_sum * kernel_scale), "section")
    mix_part = contract("aic,biad->bacd", mix_in_right, back_return).reshape(
        count_batch * token_rows, width
    )
    input_grad = (
        (gate_part + mix_part).astype(jnp.bfloat16).reshape(1, count_batch, token_rows, width)
    )
    kernel_grad = kernel_total.astype(jnp.bfloat16).reshape(groups * block_size, width)
    return (input_grad, weight_grad, kernel_grad)


def solution(mesh):
    placed = (
        P("section", None, "seq", None),
        P("section", None, "seq", None),
        P("seq", None),
        P("seq", None, None),
        P("seq", None, None),
        P("seq", None, None),
        P("seq", None, None),
        P("seq", None),
    )
    return jax.shard_map(
        local if 64 // mesh.shape["seq"] >= 16 else local_plain,
        mesh=mesh,
        in_specs=placed,
        out_specs=(P("section", None, "seq", None), P("seq", None), P("seq", None)),
        check_vma=False,
    )
```

time: 305 us -> 269 us (0.88)
  waiting for transfers between devices: 64.2 us -> 116 us
  Pallas kernels: 121 us -> 78.8 us
  starting transfers between devices: 82.8 us -> 53.2 us
  matrix products: 13.2 us -> 0 us
    ppermute x67 -> x27, starting transfers between devices: 82.8 us -> 34.8 us  [swap(): return lax.ppermute(value, axis, [(i, i ^ bit) for i in range(size)])]
    pallas_call x15 -> x7, Pallas kernels: 105 us -> 69.3 us  [the longest x1 16.6 us: gate(): pl.pallas_call(functools.partial(gate_kernel, devices, width), grid=grid,...]
    ppermute x67 -> x27, waiting for transfers between devices: 64.2 us -> 94.9 us  [swap(): return lax.ppermute(value, axis, [(i, i ^ bit) for i in range(size)])]
    all_to_all x0 -> x4, waiting for transfers between devices: none -> 21.5 us  [exchange(): return [lax.all_to_all(pieces[0], 'seq', 0, 0, tiled=True)]]
    all_to_all x0 -> x4, starting transfers between devices: none -> 18.4 us  [exchange(): return [lax.all_to_all(pieces[0], 'seq', 0, 0, tiled=True)]]
    dot_general x2 -> x0, matrix products: 13.2 us -> none  [the longest x1 9.13 us: dot_last(): lax.dot_general(left, right, (((1,), (1,)), ((), ())), preferred_element_...]
    pallas_call x3 -> x1, Pallas kernels: 11.5 us -> 4.66 us  [first(): pl.pallas_call(functools.partial(first_kernel, devices), grid=grid, in_sp...]
  transfers between devices with their start and end apart: 67 -> 31, of which waited for: 18 -> 18; matrix products, arithmetic and copies ran while one was open for 9% -> 5% of each run, Pallas kernels for 40% -> 26%
where the time goes in v1:
time: 269 us; the launch traced here: 268 us
  waiting for transfers between devices  116 us (43%)
  Pallas kernels  78.8 us (29%)
  starting transfers between devices  53.2 us (20%)
  other arithmetic  12 us (4%)
  local copies, waits for them, and re-layouts  6.51 us (2%)
    ppermute x27, waiting for transfers between devices, swap(): return lax.ppermute(value, axis, [(i, i ^ bit) for i in range(size)])  94.9 us
    ppermute x27, starting transfers between devices, swap(): return lax.ppermute(value, axis, [(i, i ^ bit) for i in range(size)])  34.8 us
    all_to_all x4, waiting for transfers between devices, exchange(): return [lax.all_to_all(pieces[0], 'seq', 0, 0, tiled=True)]  21.5 us
    all_to_all x4, starting transfers between devices, exchange(): return [lax.all_to_all(pieces[0], 'seq', 0, 0, tiled=True)]  18.4 us
    pallas_call x1, Pallas kernels, gate(): pl.pallas_call(functools.partial(gate_kernel, devices, width), grid=grid,...  16.6 us
    pallas_call x1, Pallas kernels, ending(): pl.pallas_call(functools.partial(ending_kernel, devices, len(pieces), sca...  15.9 us
    pallas_call x2, Pallas kernels, back_middle(): pl.pallas_call(functools.partial(back_middle_kernel, devices, len(pieces)...  14.7 us
    pallas_call x1, Pallas kernels, middle(): pl.pallas_call(functools.partial(middle_kernel, devices, len(pieces)), gr...  11.3 us
  transfers between devices with their start and end apart: 31, of which 18 were waited for; matrix products, arithmetic and copies ran while one was open for 5% of the time, Pallas kernels for 26%

profile of v1, /device:TPU:0, one launch (start us, length us, event | category | flops | bytes accessed | tf_op | source)
XLA Modules:
  0.0 267.9 jit_solution(11793509400734717889)
XLA Ops:
  0.7 4.7 %shard_map.103 = bf16[4,3,2,128,768]{4,3,2,1,0:T(8,128)(2,1)} custom-call(bf16[16,64,64]{2,1,0:T(8,128)(2,1)} %right_in.3, bf16[3,16,64,768]{3,2,1,0:T(8,128)(2,1)} %bitcast.31), custom_call_target="tpu_custom_call" | custom-call | flops 1000 | bytes 1000 | tf_op jit(solution)/shard_map/pallas_call | solution.py:118
  5.3 0.9 fusion.1
  6.2 4.0 %collective-permute-start.2 = (f32[48,768]{1,0:T(8,128)S(1)}, f32[48,768]{1,0:T(8,128)S(1)}, u32[]{:S(2)}, u32[]{:S(2)}) collective-permute-start(f32[48,768]{1,0:T(8,128)S(1)} %get-tuple-element.87), channel_id=1, source_target_pairs={{0,3},{1,2},{2,1},{3,0},{4,7},{5,6},{6,5},{7,4},{8,11},{9,10},{10,... | collective-permute-start | bytes 442376 | tf_op jit(solution)/shard_map/ppermute | solution.py:344
  10.2 0.5 collective-permute-start
  10.8 5.0 %all-to-all-start = ((bf16[4,3,2,128,768]{4,3,2,1,0:T(8,128)(2,1)}), bf16[4,3,2,128,768]{4,3,2,1,0:T(8,128)(2,1)}, u32[]{:S(2)}, u32[]{:S(2)}) async-start(bf16[4,3,2,128,768]{4,3,2,1,0:T(8,128)(2,1)} %shard_map.103), calls=%async_computation | async-start | bytes 9437184 | tf_op jit(solution)/shard_map/all_to_all | solution.py:349
  16.2 0.8 copy.13.right_turned
  17.1 0.8 reverse_select_fusion.8
  17.9 4.8 %shard_map.104 = (bf16[2,512,512]{2,1,0:T(8,128)(2,1)}, bf16[2,512,512]{2,1,0:T(8,128)(2,1)}, bf16[2,512,512]{2,1,0:T(8,128)(2,1)}, bf16[2,512,512]{2,1,0:T(8,12...) custom-call(bf16[16,64,64]{2,1,0:T(8,128)(2,1)} %left_in.1, bf16[16,64,64]{2,1,0:T(8,128)(2,1)} %bitcast.56, ...), custom_call_target="tpu_custom_call" | custom-call | flops 1000 | bytes 1000 | tf_op jit(solution)/shard_map/pallas_call | solution.py:80
  22.9 2.0 collective-permute-start.3
  24.9 12.5 %collective-permute-done.3 = f32[4,48,768]{2,1,0:T(8,128)S(1)} collective-permute-done((f32[4,48,768]{2,1,0:T(8,128)S(1)}, f32[4,48,768]{2,1,0:T(8,128)S(1)}, u32[]{:S(2)}, u32[]{:S(2)}) %collective-permute-start.3) | collective-permute-done | bytes 589856 | tf_op jit(solution)/shard_map/ppermute | solution.py:344
  37.7 2.8 %collective-permute-done.4 = f32[4,96,768]{2,1,0:T(8,128)S(1)} collective-permute-done((f32[4,96,768]{2,1,0:T(8,128)S(1)}, f32[4,96,768]{2,1,0:T(8,128)S(1)}, u32[]{:S(2)}, u32[]{:S(2)}) %collective-permute-start.4) | collective-permute-done | bytes 1179680 | tf_op jit(solution)/shard_map/ppermute | solution.py:344
  40.5 1.6 maximum_select_fusion
  42.1 16.6 %shard_map.105 = (bf16[3,2,128,768]{3,2,1,0:T(8,128)(2,1)}, bf16[3,2,128,768]{3,2,1,0:T(8,128)(2,1)}, bf16[3,2,128,768]{3,2,1,0:T(8,128)(2,1)}, bf16[3,2,128,768]{3,2,1,0:T(8,128)(2,1)}, f32[3,1024,768]{2,1,0:T(8,128)}) custom-call(bf16[16,64,64]{2,1,0:T(8,128)(2,1)} %get-tuple-element.45.small, f32[768,768]{1,0:T(8,128)} %bitcast.34, ...), custom_call_target="tpu_custom_call" | custom-call | flops 1000 | bytes 1000 | tf_op jit(solution)/shard_map/pallas_call | solution.py:249
  58.7 9.8 %all-to-all-done.refs_0_ = bf16[4,3,2,128,768]{4,3,2,1,0:T(8,128)(2,1)} async-done(((bf16[4,3,2,128,768]{4,3,2,1,0:T(8,128)(2,1)}), bf16[4,3,2,128,768]{4,3,2,1,0:T(8,128)(2,1)}, u32[]{:S(2)}, u32[]{:S(2)}) %all-to-all-start) | async-done | bytes 4718624 | tf_op jit(solution)/shard_map/all_to_all | solution.py:349
  68.5 1.4 collective-permute-start.5
  70.0 1.1 collective-permute-start.6
  71.1 1.0 collective-permute-start.7
  72.0 11.3 %shard_map.106 = (bf16[4,3,2,128,768]{4,3,2,1,0:T(8,128)(2,1)}, f32[3,2,512,768]{3,2,1,0:T(8,128)}) custom-call(bf16[16,64,64]{2,1,0:T(8,128)(2,1)} %small, bf16[2,512,512]{2,1,0:T(8,128)(2,1)} %get-tuple-element.47.big, bf16[2,512,768]{2,1,0:T(8,128)(2,1)} %bitcast.37, bf16[4,3,2,128,768]{4,3,2,1,0:T(8,128)(2,1)} %all-to-all-done.refs_0_), custom_call_target="tpu_custom_call" | custom-call | flops 1000 | bytes 1000 | tf_op jit(solution)/shard_map/pallas_call | solution.py:155
  83.4 14.3 %collective-permute-done.5.refs_1_ = bf16[3,2,128,768]{3,2,1,0:T(8,128)(2,1)S(1)} collective-permute-done((bf16[3,2,128,768]{3,2,1,0:T(8,128)(2,1)}, bf16[3,2,128,768]{3,2,1,0:T(8,128)(2,1)S(1)}, u32[]{:S(2)}, u32[]{:S(2)}) %collective-permute-start.5) | collective-permute-done | bytes 1179680 | tf_op jit(solution)/shard_map/ppermute | solution.py:344
  97.7 23.5 %collective-permute-done.6.refs_2_ = bf16[3,2,128,768]{3,2,1,0:T(8,128)(2,1)S(1)} collective-permute-done((bf16[3,2,128,768]{3,2,1,0:T(8,128)(2,1)}, bf16[3,2,128,768]{3,2,1,0:T(8,128)(2,1)S(1)}, u32[]{:S(2)}, u32[]{:S(2)}) %collective-permute-start.6) | collective-permute-done | bytes 1179680 | tf_op jit(solution)/shard_map/ppermute | solution.py:344
  121.2 0.8 collective-permute-done.7.refs_3_
  122.2 0.8 copy-done.2
  123.0 5.0 %all-to-all-start.1 = ((bf16[4,3,2,128,768]{4,3,2,1,0:T(8,128)(2,1)}), bf16[4,3,2,128,768]{4,3,2,1,0:T(8,128)(2,1)}, u32[]{:S(2)}, u32[]{:S(2)}) async-start(bf16[4,3,2,128,768]{4,3,2,1,0:T(8,128)(2,1)} %get-tuple-element.67), calls=%async_computation.1 | async-start | bytes 9437184 | tf_op jit(solution)/shard_map/all_to_all | solution.py:349
  128.0 9.9 %shard_map.107 = (bf16[4,3,2,128,640]{4,3,2,1,0:T(8,128)(2,1)}, f32[2,512,640]{2,1,0:T(8,128)}) custom-call(bf16[16,64,64]{2,1,0:T(8,128)(2,1)} %get-tuple-element.63.small, bf16[2,512,512]{2,1,0:T(8,128)(2,1)} %get-tuple-element.53.big, bf16[2,512,768]{2,1,0:T(8,128)(2,1)} %bitcast.38, f32[3,2,512,768]{3,2,1,0:T(8,128)} %get-tuple-element.51.second, ...), custom_call_target="tpu_custom_call" | custom-call | flops 1000 | bytes 1000 | tf_op jit(solution)/shard_map/pallas_call | solution.py:198
  137.9 4.8 %shard_map.108 = (bf16[4,3,2,128,128]{4,3,2,1,0:T(8,128)(2,1)}, f32[2,512,128]{2,1,0:T(8,128)}) custom-call(bf16[16,64,64]{2,1,0:T(8,128)(2,1)} %get-tuple-element.63.small, bf16[2,512,512]{2,1,0:T(8,128)(2,1)} %get-tuple-element.53.big, bf16[2,512,768]{2,1,0:T(8,128)(2,1)} %bitcast.39, f32[3,2,512,768]{3,2,1,0:T(8,128)} %get-tuple-element.51.second, ...), custom_call_target="tpu_custom_call" | custom-call | flops 1000 | bytes 1000 | tf_op jit(solution)/shard_map/pallas_call | solution.py:198
  142.7 1.3 maximum_multiply_fusion
  144.0 1.0 dynamic-slice_convert_fusion
  145.0 2.6 collective-permute-done.8
  147.6 1.3 convert_add_fusion
  148.9 1.1 copy-done.3
  150.1 2.5 collective-permute-start.10
  152.6 1.4 collective-permute-start.11
  154.2 13.1 %collective-permute-done.10 = bf16[128,768]{1,0:T(8,128)(2,1)S(1)} collective-permute-done((bf16[128,768]{1,0:T(8,128)(2,1)S(1)}, bf16[128,768]{1,0:T(8,128)(2,1)S(1)}, u32[]{:S(2)}, u32[]{:S(2)}) %collective-permute-start.10) | collective-permute-done | bytes 196640 | tf_op jit(solution)/shard_map/ppermute | solution.py:344
  167.3 0.5 collective-permute-done.9
  167.8 1.1 add_convert_fusion
  168.9 10.7 %all-to-all-done.1.refs_0_ = bf16[4,3,2,128,768]{4,3,2,1,0:T(8,128)(2,1)} async-done(((bf16[4,3,2,128,768]{4,3,2,1,0:T(8,128)(2,1)}), bf16[4,3,2,128,768]{4,3,2,1,0:T(8,128)(2,1)}, u32[]{:S(2)}, u32[]{:S(2)}) %all-to-all-start.1) | async-done | bytes 4718624 | tf_op jit(solution)/shard_map/all_to_all | solution.py:349
  179.6 5.0 %all-to-all-start.2 = ((bf16[4,3,2,128,640]{4,3,2,1,0:T(8,128)(2,1)}), bf16[4,3,2,128,640]{4,3,2,1,0:T(8,128)(2,1)}, u32[]{:S(2)}, u32[]{:S(2)}) async-start(bf16[4,3,2,128,640]{4,3,2,1,0:T(8,128)(2,1)} %get-tuple-element.72), calls=%async_computation.2 | async-start | bytes 7864320 | tf_op jit(solution)/shard_map/all_to_all | solution.py:349
  184.6 15.9 %shard_map.109 = (f32[3,1024,768]{2,1,0:T(8,128)}, f32[768,768]{1,0:T(8,128)}) custom-call(bf16[2,512,512]{2,1,0:T(8,128)(2,1)} %get-tuple-element.65.big, f32[3,1024,768]{2,1,0:T(8,128)} %get-tuple-element.49.sloped, f32[768,768]{1,0:T(8,128)} %bitcast.35, bf16[3,1024,768]{2,1,0:T(8,128)(2,1)} %bitcast.33, bf16[4,3,2,128,768]{4,3,2,1,0:T(8,128)(2,1)} %all-to-all-done.1.refs_0_), custom_call_target="tpu_custom_call" | custom-call | flops 1000 | bytes 1000 | tf_op jit(solution)/shard_map/pallas_call | solution.py:289
  200.5 1.3 dynamic-slice_convert_fusion.1
  202.0 1.3 collective-permute-start.23
  203.3 2.6 collective-permute-start.24
  205.9 0.6 collective-permute-start.25
  206.4 1.4 convert_add_fusion.1
  208.3 3.5 %collective-permute-start.14 = (bf16[4,24,768]{2,1,0:T(8,128)(2,1)S(1)}, bf16[4,24,768]{2,1,0:T(8,128)(2,1)S(1)}, u32[]{:S(2)}, u32[]{:S(2)}) collective-permute-start(bf16[4,24,768]{2,1,0:T(8,128)(2,1)S(1)} %get-tuple-element.82), channel_id=1, source_target_pairs={{0,16},{4,20},{8,24},{12,28},{16,0},{20,4},{24,8},{28,12},{1,17},{... | collective-permute-start | bytes 442376 | tf_op jit(solution)/shard_map/ppermute | solution.py:344
  211.8 1.7 collective-permute-done.23
  213.5 2.5 collective-permute-start.15
  216.0 4.5 %collective-permute-done.24 = bf16[128,768]{1,0:T(8,128)(2,1)S(1)} collective-permute-done((bf16[128,768]{1,0:T(8,128)(2,1)S(1)}, bf16[128,768]{1,0:T(8,128)(2,1)S(1)}, u32[]{:S(2)}, u32[]{:S(2)}) %collective-permute-start.24) | collective-permute-done | bytes 196640 | tf_op jit(solution)/shard_map/ppermute | solution.py:344
  220.9 13.3 %collective-permute-done.14 = bf16[4,24,768]{2,1,0:T(8,128)(2,1)S(1)} collective-permute-done((bf16[4,24,768]{2,1,0:T(8,128)(2,1)S(1)}, bf16[4,24,768]{2,1,0:T(8,128)(2,1)S(1)}, u32[]{:S(2)}, u32[]{:S(2)}) %collective-permute-start.14) | collective-permute-done | bytes 147488 | tf_op jit(solution)/shard_map/ppermute | solution.py:344
  234.2 1.8 collective-permute-start.16
  236.0 1.5 collective-permute-start.17
  237.9 1.3 collective-permute-done.16
  239.2 1.6 collective-permute-done.17
  240.8 1.9 collective-permute-done.18
  242.8 3.0 %collective-permute-start.19 = (f32[1,24,768]{2,1,0:T(8,128)S(1)}, f32[1,24,768]{2,1,0:T(8,128)S(1)}, u32[]{:S(2)}, u32[]{:S(2)}) collective-permute-start(f32[1,24,768]{2,1,0:T(8,128)S(1)} %add_add_fusion), channel_id=1, source_target_pairs={{0,8},{4,12},{8,0},{12,4},{16,24},{20,28},{24,16},{28,20},{1,9},{5... | collective-permute-start | bytes 221192 | tf_op jit(solution)/shard_map/ppermute | solution.py:344
  245.8 1.1 collective-permute-start.20
  246.9 1.4 collective-permute-start.21
  248.5 3.5 %all-to-all-start.3 = ((bf16[4,3,2,128,128]{4,3,2,1,0:T(8,128)(2,1)}), bf16[4,3,2,128,128]{4,3,2,1,0:T(8,128)(2,1)S(1)}, u32[]{:S(2)}, u32[]{:S(2)}) async-start(bf16[4,3,2,128,128]{4,3,2,1,0:T(8,128)(2,1)} %get-tuple-element.74), calls=%async_computation.3 | async-start | bytes 1572864 | tf_op jit(solution)/shard_map/all_to_all | solution.py:349
  252.0 7.5 %shard_map.110.refs_1_ = bf16[3,1024,768]{2,1,0:T(8,128)(2,1)} custom-call(bf16[2,512,512]{2,1,0:T(8,128)(2,1)} %get-tuple-element.42.big, f32[3,1024,768]{2,1,0:T(8,128)} %get-tuple-element.68.other, bf16[4,3,2,128,640]{4,3,2,1,0:T(8,128)(2,1)} %all-to-all-done.2.refs_0_), custom_call_target="tpu_custom_call" | custom-call | flops 1000 | bytes 1000 | tf_op jit(solution)/shard_map/pallas_call | solution.py:326
  259.6 0.6 collective-permute-start.22
  260.1 1.8 maximum_select_fusion.1
  261.9 0.9 maximum_select_fusion.3
  262.8 0.9 all-to-all-done.3.refs_0_
  263.7 0.9 copy-done.4
  264.6 3.3 %shard_map.111 = bf16[3,1024,768]{2,1,0:T(8,128)(2,1)} custom-call(bf16[2,512,512]{2,1,0:T(8,128)(2,1)} %get-tuple-element.42.big, f32[3,1024,768]{2,1,0:T(8,128)} %get-tuple-element.68.other, bf16[4,3,2,128,128]{4,3,2,1,0:T(8,128)(2,1)} %copy-done.4, bf16[3,1024,768]{2,1,0:T(8,128)(2,1)} %shard_map.110.refs_1_), custom_call_target="tpu_custom_call", output_to_operand_aliasing={{}: (3, {})} | custom-call | flops 1000 | bytes 1000 | tf_op jit(solution)/shard_map/pallas_call | solution.py:326
  (54 shorter events, 3.1 us)
Async XLA Ops:
  6.2 9.6 %copy-start.6 = (bf16[16,64,64]{2,1,0:T(8,128)(2,1)S(1)}, bf16[16,64,64]{2,1,0:T(8,128)(2,1)}, u32[]{:S(2)}) copy-start(bf16[16,64,64]{2,1,0:T(8,128)(2,1)} %right_out.1) | copy-start | bytes 393220
  6.2 16.5 %collective-permute-start.2 = (f32[48,768]{1,0:T(8,128)S(1)}, f32[48,768]{1,0:T(8,128)S(1)}, u32[]{:S(2)}, u32[]{:S(2)}) collective-permute-start(f32[48,768]{1,0:T(8,128)S(1)} %get-tuple-element.87), channel_id=1, source_target_pairs={{0,3},{1,2},{2,1},{3,0},{4,7},{5,6},{6,5},{7,4},{8,11},{9,10},{10,... | collective-permute-start | bytes 442376 | tf_op jit(solution)/shard_map/ppermute | solution.py:344
  10.2 12.5 %collective-permute-start = (f32[48,768]{1,0:T(8,128)S(1)}, f32[48,768]{1,0:T(8,128)S(1)}, u32[]{:S(2)}, u32[]{:S(2)}) collective-permute-start(f32[48,768]{1,0:T(8,128)S(1)} %get-tuple-element.87), channel_id=1, source_target_pairs={{0,1},{1,0},{2,3},{3,2},{4,5},{5,4},{6,7},{7,6},{8,9},{9,8},{10,11... | collective-permute-start | bytes 442376 | tf_op jit(solution)/shard_map/ppermute | solution.py:344
  10.7 12.0 %collective-permute-start.1 = (f32[48,768]{1,0:T(8,128)S(1)}, f32[48,768]{1,0:T(8,128)S(1)}, u32[]{:S(2)}, u32[]{:S(2)}) collective-permute-start(f32[48,768]{1,0:T(8,128)S(1)} %get-tuple-element.87), channel_id=1, source_target_pairs={{0,2},{1,3},{2,0},{3,1},{4,6},{5,7},{6,4},{7,5},{8,10},{9,11},{10,... | collective-permute-start | bytes 442376 | tf_op jit(solution)/shard_map/ppermute | solution.py:344
  10.8 57.7 %all-to-all-start = ((bf16[4,3,2,128,768]{4,3,2,1,0:T(8,128)(2,1)}), bf16[4,3,2,128,768]{4,3,2,1,0:T(8,128)(2,1)}, u32[]{:S(2)}, u32[]{:S(2)}) async-start(bf16[4,3,2,128,768]{4,3,2,1,0:T(8,128)(2,1)} %shard_map.103), calls=%async_computation | async-start | bytes 9437184 | tf_op jit(solution)/shard_map/all_to_all | solution.py:349
  15.8 1.3 copy-start.7
  22.9 14.6 %collective-permute-start.3 = (f32[4,48,768]{2,1,0:T(8,128)S(1)}, f32[4,48,768]{2,1,0:T(8,128)S(1)}, u32[]{:S(2)}, u32[]{:S(2)}) collective-permute-start(f32[4,48,768]{2,1,0:T(8,128)S(1)} %bitcast.47), channel_id=1, source_target_pairs={{0,8},{4,12},{8,0},{12,4},{16,24},{20,28},{24,16},{28,20},{1,9},{5... | collective-permute-start | bytes 1769480 | tf_op jit(solution)/shard_map/ppermute | solution.py:344
  37.6 2.9 %collective-permute-start.4 = (f32[4,96,768]{2,1,0:T(8,128)S(1)}, f32[4,96,768]{2,1,0:T(8,128)S(1)}, u32[]{:S(2)}, u32[]{:S(2)}) collective-permute-start(f32[4,96,768]{2,1,0:T(8,128)S(1)} %maximum_select_fusion.2), channel_id=1, source_target_pairs={{0,4},{4,0},{8,12},{12,8},{16,20},{20,16},{24,28},{28,24},{1,5},{5... | collective-permute-start | bytes 3538952 | tf_op jit(solution)/shard_map/ppermute | solution.py:344
  68.5 29.1 %collective-permute-start.5 = (bf16[3,2,128,768]{3,2,1,0:T(8,128)(2,1)}, bf16[3,2,128,768]{3,2,1,0:T(8,128)(2,1)S(1)}, u32[]{:S(2)}, u32[]{:S(2)}) collective-permute-start(bf16[3,2,128,768]{3,2,1,0:T(8,128)(2,1)} %get-tuple-element.59), channel_id=1, source_target_pairs={{0,1},{1,0},{2,3},{3,2},{4,5},{5,4},{6,7},{7,6},{8,9},{9,8},{10,11... | collective-permute-start | bytes 3538952 | tf_op jit(solution)/shard_map/ppermute | solution.py:344
  70.0 51.2 %collective-permute-start.6 = (bf16[3,2,128,768]{3,2,1,0:T(8,128)(2,1)}, bf16[3,2,128,768]{3,2,1,0:T(8,128)(2,1)S(1)}, u32[]{:S(2)}, u32[]{:S(2)}) collective-permute-start(bf16[3,2,128,768]{3,2,1,0:T(8,128)(2,1)} %get-tuple-element.60), channel_id=1, source_target_pairs={{0,2},{1,3},{2,0},{3,1},{4,6},{5,7},{6,4},{7,5},{8,10},{9,11},{10,... | collective-permute-start | bytes 3538952 | tf_op jit(solution)/shard_map/ppermute | solution.py:344
  71.1 50.9 %collective-permute-start.7 = (bf16[3,2,128,768]{3,2,1,0:T(8,128)(2,1)}, bf16[3,2,128,768]{3,2,1,0:T(8,128)(2,1)S(1)}, u32[]{:S(2)}, u32[]{:S(2)}) collective-permute-start(bf16[3,2,128,768]{3,2,1,0:T(8,128)(2,1)} %get-tuple-element.61), channel_id=1, source_target_pairs={{0,3},{1,2},{2,1},{3,0},{4,7},{5,6},{6,5},{7,4},{8,11},{9,10},{10,... | collective-permute-start | bytes 3538952 | tf_op jit(solution)/shard_map/ppermute | solution.py:344
  97.7 24.3 %copy-start = (bf16[3,2,128,768]{3,2,1,0:T(8,128)(2,1)}, bf16[3,2,128,768]{3,2,1,0:T(8,128)(2,1)S(1)}, u32[]{:S(2)}) copy-start(bf16[3,2,128,768]{3,2,1,0:T(8,128)(2,1)S(1)} %collective-permute-done.5.refs_1_) | copy-start | bytes 3538948
  121.2 1.0 copy-start.1
  122.0 1.0 copy-start.2
  123.0 56.7 %all-to-all-start.1 = ((bf16[4,3,2,128,768]{4,3,2,1,0:T(8,128)(2,1)}), bf16[4,3,2,128,768]{4,3,2,1,0:T(8,128)(2,1)}, u32[]{:S(2)}, u32[]{:S(2)}) async-start(bf16[4,3,2,128,768]{4,3,2,1,0:T(8,128)(2,1)} %get-tuple-element.67), calls=%async_computation.1 | async-start | bytes 9437184 | tf_op jit(solution)/shard_map/all_to_all | solution.py:349
  137.9 4.8 %copy-start.5 = (f32[2,512,640]{2,1,0:T(8,128)S(1)}, f32[2,512,640]{2,1,0:T(8,128)}, u32[]{:S(2)}) copy-start(f32[2,512,640]{2,1,0:T(8,128)} %get-tuple-element.62) | copy-start | bytes 7864324
  145.0 2.6 collective-permute-start.8
  148.9 1.1 copy-start.3
  150.1 17.2 %collective-permute-start.10 = (bf16[128,768]{1,0:T(8,128)(2,1)S(1)}, bf16[128,768]{1,0:T(8,128)(2,1)S(1)}, u32[]{:S(2)}, u32[]{:S(2)}) collective-permute-start(bf16[128,768]{1,0:T(8,128)(2,1)S(1)} %get-tuple-element.79), channel_id=1, source_target_pairs={{0,16},{4,20},{8,24},{12,28},{16,0},{20,4},{24,8},{28,12},{1,17},{... | collective-permute-start | bytes 589832 | tf_op jit(solution)/shard_map/ppermute | solution.py:344
  152.6 14.7 %collective-permute-start.11 = (bf16[128,768]{1,0:T(8,128)(2,1)S(1)}, bf16[128,768]{1,0:T(8,128)(2,1)S(1)}, u32[]{:S(2)}, u32[]{:S(2)}) collective-permute-start(bf16[128,768]{1,0:T(8,128)(2,1)S(1)} %get-tuple-element.78), channel_id=1, source_target_pairs={{0,24},{4,28},{8,16},{12,20},{16,8},{20,12},{24,0},{28,4},{1,25},{... | collective-permute-start | bytes 589832 | tf_op jit(solution)/shard_map/ppermute | solution.py:344
  154.0 13.8 %collective-permute-start.9 = (bf16[128,768]{1,0:T(8,128)(2,1)S(1)}, bf16[128,768]{1,0:T(8,128)(2,1)S(1)}, u32[]{:S(2)}, u32[]{:S(2)}) collective-permute-start(bf16[128,768]{1,0:T(8,128)(2,1)S(1)} %get-tuple-element.77), channel_id=1, source_target_pairs={{0,8},{4,12},{8,0},{12,4},{16,24},{20,28},{24,16},{28,20},{1,9},{5... | collective-permute-start | bytes 589832 | tf_op jit(solution)/shard_map/ppermute | solution.py:344
  179.6 63.1 %all-to-all-start.2 = ((bf16[4,3,2,128,640]{4,3,2,1,0:T(8,128)(2,1)}), bf16[4,3,2,128,640]{4,3,2,1,0:T(8,128)(2,1)}, u32[]{:S(2)}, u32[]{:S(2)}) async-start(bf16[4,3,2,128,640]{4,3,2,1,0:T(8,128)(2,1)} %get-tuple-element.72), calls=%async_computation.2 | async-start | bytes 7864320 | tf_op jit(solution)/shard_map/all_to_all | solution.py:349
  201.9 4.6 %collective-permute-start.12 = (bf16[4,96,768]{2,1,0:T(8,128)(2,1)S(1)}, bf16[4,96,768]{2,1,0:T(8,128)(2,1)S(1)}, u32[]{:S(2)}, u32[]{:S(2)}) collective-permute-start(bf16[4,96,768]{2,1,0:T(8,128)(2,1)S(1)} %dynamic-slice_convert_fusion.1), channel_id=1, source_target_pairs={{0,4},{4,0},{8,12},{12,8},{16,20},{20,16},{24,28},{28,24},{1,5},{5... | collective-permute-start | bytes 1769480 | tf_op jit(solution)/shard_map/ppermute | solution.py:344
  202.0 11.5 %collective-permute-start.23 = (bf16[128,768]{1,0:T(8,128)(2,1)S(1)}, bf16[128,768]{1,0:T(8,128)(2,1)S(1)}, u32[]{:S(2)}, u32[]{:S(2)}) collective-permute-start(bf16[128,768]{1,0:T(8,128)(2,1)S(1)} %add_convert_fusion), channel_id=1, source_target_pairs={{0,8},{4,12},{8,0},{12,4},{16,24},{20,28},{24,16},{28,20},{1,9},{5... | collective-permute-start | bytes 589832 | tf_op jit(solution)/shard_map/ppermute | solution.py:344
  203.3 17.2 %collective-permute-start.24 = (bf16[128,768]{1,0:T(8,128)(2,1)S(1)}, bf16[128,768]{1,0:T(8,128)(2,1)S(1)}, u32[]{:S(2)}, u32[]{:S(2)}) collective-permute-start(bf16[128,768]{1,0:T(8,128)(2,1)S(1)} %add_convert_fusion), channel_id=1, source_target_pairs={{0,16},{4,20},{8,24},{12,28},{16,0},{20,4},{24,8},{28,12},{1,17},{... | collective-permute-start | bytes 589832 | tf_op jit(solution)/shard_map/ppermute | solution.py:344
  205.9 14.6 %collective-permute-start.25 = (bf16[128,768]{1,0:T(8,128)(2,1)S(1)}, bf16[128,768]{1,0:T(8,128)(2,1)S(1)}, u32[]{:S(2)}, u32[]{:S(2)}) collective-permute-start(bf16[128,768]{1,0:T(8,128)(2,1)S(1)} %add_convert_fusion), channel_id=1, source_target_pairs={{0,24},{4,28},{8,16},{12,20},{16,8},{20,12},{24,0},{28,4},{1,25},{... | collective-permute-start | bytes 589832 | tf_op jit(solution)/shard_map/ppermute | solution.py:344
  207.9 13.0 %collective-permute-start.13 = (bf16[4,24,768]{2,1,0:T(8,128)(2,1)S(1)}, bf16[4,24,768]{2,1,0:T(8,128)(2,1)S(1)}, u32[]{:S(2)}, u32[]{:S(2)}) collective-permute-start(bf16[4,24,768]{2,1,0:T(8,128)(2,1)S(1)} %get-tuple-element.80), channel_id=1, source_target_pairs={{0,8},{4,12},{8,0},{12,4},{16,24},{20,28},{24,16},{28,20},{1,9},{5... | collective-permute-start | bytes 442376 | tf_op jit(solution)/shard_map/ppermute | solution.py:344
  208.3 25.8 %collective-permute-start.14 = (bf16[4,24,768]{2,1,0:T(8,128)(2,1)S(1)}, bf16[4,24,768]{2,1,0:T(8,128)(2,1)S(1)}, u32[]{:S(2)}, u32[]{:S(2)}) collective-permute-start(bf16[4,24,768]{2,1,0:T(8,128)(2,1)S(1)} %get-tuple-element.82), channel_id=1, source_target_pairs={{0,16},{4,20},{8,24},{12,28},{16,0},{20,4},{24,8},{28,12},{1,17},{... | collective-permute-start | bytes 442376 | tf_op jit(solution)/shard_map/ppermute | solution.py:344
  213.5 20.6 %collective-permute-start.15 = (bf16[4,24,768]{2,1,0:T(8,128)(2,1)S(1)}, bf16[4,24,768]{2,1,0:T(8,128)(2,1)S(1)}, u32[]{:S(2)}, u32[]{:S(2)}) collective-permute-start(bf16[4,24,768]{2,1,0:T(8,128)(2,1)S(1)} %get-tuple-element.81), channel_id=1, source_target_pairs={{0,24},{4,28},{8,16},{12,20},{16,8},{20,12},{24,0},{28,4},{1,25},{... | collective-permute-start | bytes 442376 | tf_op jit(solution)/shard_map/ppermute | solution.py:344
  234.2 5.0 %collective-permute-start.16 = (f32[1,24,768]{2,1,0:T(8,128)S(1)}, f32[1,24,768]{2,1,0:T(8,128)S(1)}, u32[]{:S(2)}, u32[]{:S(2)}) collective-permute-start(f32[1,24,768]{2,1,0:T(8,128)S(1)} %get-tuple-element.83), channel_id=1, source_target_pairs={{0,1},{1,0},{2,3},{3,2},{4,5},{5,4},{6,7},{7,6},{8,9},{9,8},{10,11... | collective-permute-start | bytes 221192 | tf_op jit(solution)/shard_map/ppermute | solution.py:344
  236.0 4.8 %collective-permute-start.17 = (f32[1,24,768]{2,1,0:T(8,128)S(1)}, f32[1,24,768]{2,1,0:T(8,128)S(1)}, u32[]{:S(2)}, u32[]{:S(2)}) collective-permute-start(f32[1,24,768]{2,1,0:T(8,128)S(1)} %get-tuple-element.85), channel_id=1, source_target_pairs={{0,2},{1,3},{2,0},{3,1},{4,6},{5,7},{6,4},{7,5},{8,10},{9,11},{10,... | collective-permute-start | bytes 221192 | tf_op jit(solution)/shard_map/ppermute | solution.py:344
  237.5 5.3 %collective-permute-start.18 = (f32[1,24,768]{2,1,0:T(8,128)S(1)}, f32[1,24,768]{2,1,0:T(8,128)S(1)}, u32[]{:S(2)}, u32[]{:S(2)}) collective-permute-start(f32[1,24,768]{2,1,0:T(8,128)S(1)} %get-tuple-element.84), channel_id=1, source_target_pairs={{0,3},{1,2},{2,1},{3,0},{4,7},{5,6},{6,5},{7,4},{8,11},{9,10},{10,... | collective-permute-start | bytes 221192 | tf_op jit(solution)/shard_map/ppermute | solution.py:344
  242.8 16.7 %collective-permute-start.19 = (f32[1,24,768]{2,1,0:T(8,128)S(1)}, f32[1,24,768]{2,1,0:T(8,128)S(1)}, u32[]{:S(2)}, u32[]{:S(2)}) collective-permute-start(f32[1,24,768]{2,1,0:T(8,128)S(1)} %add_add_fusion), channel_id=1, source_target_pairs={{0,8},{4,12},{8,0},{12,4},{16,24},{20,28},{24,16},{28,20},{1,9},{5... | collective-permute-start | bytes 221192 | tf_op jit(solution)/shard_map/ppermute | solution.py:344
  245.8 13.7 %collective-permute-start.20 = (f32[1,24,768]{2,1,0:T(8,128)S(1)}, f32[1,24,768]{2,1,0:T(8,128)S(1)}, u32[]{:S(2)}, u32[]{:S(2)}) collective-permute-start(f32[1,24,768]{2,1,0:T(8,128)S(1)} %add_add_fusion), channel_id=1, source_target_pairs={{0,16},{4,20},{8,24},{12,28},{16,0},{20,4},{24,8},{28,12},{1,17},{... | collective-permute-start | bytes 221192 | tf_op jit(solution)/shard_map/ppermute | solution.py:344
  246.9 12.6 %collective-permute-start.21 = (f32[1,24,768]{2,1,0:T(8,128)S(1)}, f32[1,24,768]{2,1,0:T(8,128)S(1)}, u32[]{:S(2)}, u32[]{:S(2)}) collective-permute-start(f32[1,24,768]{2,1,0:T(8,128)S(1)} %add_add_fusion), channel_id=1, source_target_pairs={{0,24},{4,28},{8,16},{12,20},{16,8},{20,12},{24,0},{28,4},{1,25},{... | collective-permute-start | bytes 221192 | tf_op jit(solution)/shard_map/ppermute | solution.py:344
  248.4 11.7 %collective-permute-start.26 = (bf16[512,768]{1,0:T(8,128)(2,1)S(1)}, bf16[512,768]{1,0:T(8,128)(2,1)S(1)}, u32[]{:S(2)}, u32[]{:S(2)}) collective-permute-start(bf16[512,768]{1,0:T(8,128)(2,1)S(1)} %bitcast.45), channel_id=1, source_target_pairs={{0,4},{4,0},{8,12},{12,8},{16,20},{20,16},{24,28},{28,24},{1,5},{5... | collective-permute-start | bytes 2359304 | tf_op jit(solution)/shard_map/ppermute | solution.py:344
  248.5 15.2 %all-to-all-start.3 = ((bf16[4,3,2,128,128]{4,3,2,1,0:T(8,128)(2,1)}), bf16[4,3,2,128,128]{4,3,2,1,0:T(8,128)(2,1)S(1)}, u32[]{:S(2)}, u32[]{:S(2)}) async-start(bf16[4,3,2,128,128]{4,3,2,1,0:T(8,128)(2,1)} %get-tuple-element.74), calls=%async_computation.3 | async-start | bytes 1572864 | tf_op jit(solution)/shard_map/all_to_all | solution.py:349
  259.6 2.4 collective-permute-start.22
  263.7 0.9 copy-start.4

commit v2 on v1

--- a/solution.py
+++ b/solution.py
@@ -267,7 +267,8 @@
 
 
 def ending_kernel(devices, count, scale, big, sloped, weights, flat, *refs):
-    pieces, part, total = each(refs[:count], devices), refs[-2], refs[-1]
+    pieces, part, keep, send, total = each(refs[:count], devices), *refs[count:]
+    steps = pl.num_programs(0) * pl.num_programs(1)
     step = pl.program_id(0) * pl.num_programs(1) + pl.program_id(1)
 
     @pl.when(step == 0)
@@ -278,6 +279,16 @@
     grad = (dot(big[0], spread) * sloped[0]).astype(BF16)
     part[0] = dot_last(grad, weights[...].astype(BF16))
     total[...] += dot_first(flat[0], grad) * scale
+
+    @pl.when(step == steps - 1)
+    def _():
+        mine = lax.axis_index("section") % 2
+        rows = keep.shape[1]
+        for q in range(devices):
+            low = pl.multiple_of((2 * q + mine) * rows, rows)
+            other = pl.multiple_of((2 * q + 1 - mine) * rows, rows)
+            keep[q] = total[pl.ds(low, rows), :]
+            send[q] = total[pl.ds(other, rows), :].astype(BF16)
 
 
 def ending(devices, joint, scale, big, sloped, weights, flat, pieces):
@@ -285,17 +296,24 @@
     rows = big.shape[1]
     grid = (parts, batch)
     part = pl.BlockSpec((1, rows, full), lambda g, b: (b, g, 0))
-    whole = pl.BlockSpec((full, full), lambda g, b: (0, 0))
+    half = (devices, full // devices // 2, full)
     return pl.pallas_call(
         functools.partial(ending_kernel, devices, len(pieces), scale),
         grid=grid,
-        in_specs=[pl.BlockSpec((1,) + big.shape[1:], lambda g, b: (g, 0, 0)), part, whole, part]
+        in_specs=[
+            pl.BlockSpec((1,) + big.shape[1:], lambda g, b: (g, 0, 0)),
+            part,
+            pl.BlockSpec((full, full), lambda g, b: (0, 0)),
+            part,
+        ]
         + piece_specs(devices, joint, (1, 1, long, full), lambda g, b: (b, g, 0, 0)),
-        out_specs=[part, whole],
+        out_specs=[part] + [pl.BlockSpec(half, lambda g, b: (0, 0, 0))] * 2,
         out_shape=[
             jax.ShapeDtypeStruct(sloped.shape, F32),
-            jax.ShapeDtypeStruct((full, full), F32),
+            jax.ShapeDtypeStruct(half, F32),
+            jax.ShapeDtypeStruct(half, BF16),
         ],
+        scratch_shapes=[pltpu.VMEM((full, full), F32)],
         compiler_params=params(grid),
         cost_estimate=cost(5e9, 8e6),
     )(big, sloped, weights, flat, *pieces)
@@ -369,8 +387,8 @@
     return keep + swap(send.astype(kind), axis, bit).astype(F32)
 
 
-def double(value, axis, bit, dim):
-    other = swap(value, axis, bit)
+def double(value, axis, bit, dim, other=None):
+    other = swap(value, axis, bit) if other is None else other
     mine = has(axis, bit)
     return jnp.where(
         mine == 0,
@@ -402,9 +420,12 @@
     return total
 
 
-def collect(value, axis, unit, dim):
+def blocks_of(value, axis, unit):
     peers = lax.axis_size(axis) // unit
-    blocks = [value] + [swap(value, axis, r * unit) for r in range(1, peers)]
+    return [value] + [swap(value, axis, r * unit) for r in range(1, peers)]
+
+
+def collect(blocks, axis, unit, dim):
     return by_peer(jnp.concatenate(blocks, axis=dim), dim, axis, unit)
 
 
@@ -454,14 +475,14 @@
     )
     weights = gather_weights(after(gate_weight, firsts), big_li)
     *back_third, sloped = gate(devices, small_qt, weights, flat, upstream)
-    back_spread = exchange(after(back_third, spread))
+    back_spread = exchange(back_third)
     *third, second = middle(
         devices, width, True, True, after(mix_out_left, sloped), big_li, kern, spread
     )
     returned = exchange(after(third, *back_spread))
 
-    sixth = full // 6
-    parts = ((0, 5 * sixth), (5, sixth))
+    third_width = full // 3
+    parts = ((0, 2 * third_width), (2, third_width))
     back_first, totals = [], []
     for c, wide in parts:
         sent, total = back_middle(
@@ -474,17 +495,22 @@
     kernel_grad = halve(kernel_grad, "section", 1, 0, BF16)
     kernel_grad = scatter(kernel_grad, "section", 2, 0, BF16).astype(BF16)
     back_first[0] = after(back_first[0], kernel_grad)
-    gate_part, weight_grad = ending(
+    gate_part, keep, sent = ending(
         devices, True, weight_scale, after(big_qo, kernel_grad), sloped, weights, flat, returned
     )
-    weight_grad = weight_grad.reshape(devices, full // devices, full)
-    weight_grad = halve(weight_grad, "section", 1, 1, BF16)
+    kernel_blocks = blocks_of(kernel_grad, "section", 2)
+    weight_grad = keep + swap(after(sent, *kernel_blocks), "section", 1).astype(F32)
+    kernel_grad = collect(after(kernel_blocks, weight_grad), "section", 2, 0)
+    kernel_other = swap(kernel_grad, "section", 1)
     weight_grad = scatter(weight_grad, "section", 2, 1, BF16)
+    back_return = [exchange([after(back_first[0], *returned)])]
+    back_return.append(
+        exchange([after(back_first[1], *back_return[0], weight_grad, kernel_other)])
+    )
     weight_grad = scatter(weight_grad, "seq", 1, 0, F32)
-    kernel_grad = collect(kernel_grad, "section", 2, 0)
-    kernel_grad = double(kernel_grad, "section", 1, 0)
-    back_return = [exchange([after(back_first[0], *returned)])]
-    back_return.append(exchange([after(back_first[1], *back_return[0], weight_grad)]))
+
+    kernel_other = after(kernel_other, *back_return[0])
+    kernel_grad = double(kernel_grad, "section", 1, 0, kernel_other)
 
     input_grad = None
     halves = []
@@ -493,7 +519,8 @@
             devices, c, wide, True, True, big_rt, gate_part, input_grad, arrived
         )
         halves.append(input_grad)
-    weight_grad = collect(after(weight_grad, *back_return[0]), "section", 2, 1)
+    weight_blocks = blocks_of(after(weight_grad, *back_return[0]), "section", 2)
+    weight_grad = collect(weight_blocks, "section", 2, 1)
     weight_grad = double(after(weight_grad, halves[0]), "section", 1, 1)
     weight_grad = weight_grad.reshape(full // devices, full)
     return (input_grad[None], weight_grad, kernel_grad)

time: 269 us -> 259 us (0.963)
  waiting for transfers between devices: 116 us -> 96.8 us
  other arithmetic: 12 us -> 19 us
    ppermute x27, waiting for transfers between devices: 94.9 us -> 83.2 us  [swap(): return lax.ppermute(value, axis, [(i, i ^ bit) for i in range(size)])]
    all_to_all x4, waiting for transfers between devices: 21.5 us -> 13.6 us  [exchange(): return [lax.all_to_all(pieces[0], 'seq', 0, 0, tiled=True)]]
  transfers between devices with their start and end apart: 31 -> 31, of which waited for: 18 -> 13; matrix products, arithmetic and copies ran while one was open for 5% -> 9% of each run, Pallas kernels for 26% -> 27%
where the time goes in v2:
time: 259 us; the launch traced here: 257 us
  waiting for transfers between devices  96.8 us (37%)
  Pallas kernels  78.4 us (30%)
  starting transfers between devices  52.7 us (20%)
  other arithmetic  19 us (7%)
  local copies, waits for them, and re-layouts  9.12 us (4%)
    ppermute x27, waiting for transfers between devices, swap(): return lax.ppermute(value, axis, [(i, i ^ bit) for i in range(size)])  83.2 us
    ppermute x27, starting transfers between devices, swap(): return lax.ppermute(value, axis, [(i, i ^ bit) for i in range(size)])  34.6 us
    all_to_all x4, starting transfers between devices, exchange(): return [lax.all_to_all(pieces[0], 'seq', 0, 0, tiled=True)]  18.1 us
    pallas_call x1, Pallas kernels, ending(): pl.pallas_call(functools.partial(ending_kernel, devices, len(pieces), sca...  17.4 us
    pallas_call x1, Pallas kernels, gate(): pl.pallas_call(functools.partial(gate_kernel, devices, width), grid=grid,...  16.7 us
    all_to_all x4, waiting for transfers between devices, exchange(): return [lax.all_to_all(pieces[0], 'seq', 0, 0, tiled=True)]  13.6 us
    pallas_call x2, Pallas kernels, back_middle(): pl.pallas_call(functools.partial(back_middle_kernel, devices, len(pieces)...  13.2 us
    pallas_call x1, Pallas kernels, middle(): pl.pallas_call(functools.partial(middle_kernel, devices, len(pieces)), gr...  11.4 us
  transfers between devices with their start and end apart: 31, of which 13 were waited for; matrix products, arithmetic and copies ran while one was open for 9% of the time, Pallas kernels for 27%

profile of v2, /device:TPU:0, one launch (start us, length us, event | category | flops | bytes accessed | tf_op | source)
XLA Modules:
  0.0 257.0 jit_solution(12667203306885358388)
XLA Ops:
  0.7 4.7 %shard_map.103 = bf16[4,3,2,128,768]{4,3,2,1,0:T(8,128)(2,1)} custom-call(bf16[16,64,64]{2,1,0:T(8,128)(2,1)} %right_in.3, bf16[3,16,64,768]{3,2,1,0:T(8,128)(2,1)} %bitcast.30), custom_call_target="tpu_custom_call" | custom-call | flops 1000 | bytes 1000 | tf_op jit(solution)/shard_map/pallas_call | solution.py:118
  5.3 0.9 fusion.1
  6.2 4.0 %collective-permute-start.2 = (f32[48,768]{1,0:T(8,128)S(1)}, f32[48,768]{1,0:T(8,128)S(1)}, u32[]{:S(2)}, u32[]{:S(2)}) collective-permute-start(f32[48,768]{1,0:T(8,128)S(1)} %get-tuple-element.93), channel_id=1, source_target_pairs={{0,3},{1,2},{2,1},{3,0},{4,7},{5,6},{6,5},{7,4},{8,11},{9,10},{10,... | collective-permute-start | bytes 442376 | tf_op jit(solution)/shard_map/ppermute | solution.py:362
  10.2 0.5 collective-permute-start
  10.8 4.9 %all-to-all-start = ((bf16[4,3,2,128,768]{4,3,2,1,0:T(8,128)(2,1)}), bf16[4,3,2,128,768]{4,3,2,1,0:T(8,128)(2,1)}, u32[]{:S(2)}, u32[]{:S(2)}) async-start(bf16[4,3,2,128,768]{4,3,2,1,0:T(8,128)(2,1)} %shard_map.103), calls=%async_computation | async-start | bytes 9437184 | tf_op jit(solution)/shard_map/all_to_all | solution.py:367
  16.2 0.8 copy.13.right_turned
  17.1 0.8 reverse_select_fusion.8
  17.9 4.7 %shard_map.104 = (bf16[2,512,512]{2,1,0:T(8,128)(2,1)}, bf16[2,512,512]{2,1,0:T(8,128)(2,1)}, bf16[2,512,512]{2,1,0:T(8,128)(2,1)}, bf16[2,512,512]{2,1,0:T(8,12...) custom-call(bf16[16,64,64]{2,1,0:T(8,128)(2,1)} %left_in.1, bf16[16,64,64]{2,1,0:T(8,128)(2,1)} %bitcast.51, ...), custom_call_target="tpu_custom_call" | custom-call | flops 1000 | bytes 1000 | tf_op jit(solution)/shard_map/pallas_call | solution.py:80
  22.8 2.0 collective-permute-start.3
  24.8 12.5 %collective-permute-done.3 = f32[4,48,768]{2,1,0:T(8,128)S(1)} collective-permute-done((f32[4,48,768]{2,1,0:T(8,128)S(1)}, f32[4,48,768]{2,1,0:T(8,128)S(1)}, u32[]{:S(2)}, u32[]{:S(2)}) %collective-permute-start.3) | collective-permute-done | bytes 589856 | tf_op jit(solution)/shard_map/ppermute | solution.py:362
  37.6 2.8 %collective-permute-done.4 = f32[4,96,768]{2,1,0:T(8,128)S(1)} collective-permute-done((f32[4,96,768]{2,1,0:T(8,128)S(1)}, f32[4,96,768]{2,1,0:T(8,128)S(1)}, u32[]{:S(2)}, u32[]{:S(2)}) %collective-permute-start.4) | collective-permute-done | bytes 1179680 | tf_op jit(solution)/shard_map/ppermute | solution.py:362
  40.4 1.7 maximum_select_fusion
  42.0 16.7 %shard_map.105 = (bf16[3,2,128,768]{3,2,1,0:T(8,128)(2,1)}, bf16[3,2,128,768]{3,2,1,0:T(8,128)(2,1)}, bf16[3,2,128,768]{3,2,1,0:T(8,128)(2,1)}, bf16[3,2,128,768]{3,2,1,0:T(8,128)(2,1)}, f32[3,1024,768]{2,1,0:T(8,128)}) custom-call(bf16[16,64,64]{2,1,0:T(8,128)(2,1)} %get-tuple-element.48.small, f32[768,768]{1,0:T(8,128)} %bitcast.33, ...), custom_call_target="tpu_custom_call" | custom-call | flops 1000 | bytes 1000 | tf_op jit(solution)/shard_map/pallas_call | solution.py:249
  58.7 1.7 collective-permute-start.5
  60.4 1.5 collective-permute-start.6
  62.2 8.1 %all-to-all-done.refs_0_ = bf16[4,3,2,128,768]{4,3,2,1,0:T(8,128)(2,1)} async-done(((bf16[4,3,2,128,768]{4,3,2,1,0:T(8,128)(2,1)}), bf16[4,3,2,128,768]{4,3,2,1,0:T(8,128)(2,1)}, u32[]{:S(2)}, u32[]{:S(2)}) %all-to-all-start) | async-done | bytes 4718624 | tf_op jit(solution)/shard_map/all_to_all | solution.py:367
  70.2 11.4 %shard_map.106 = (bf16[4,3,2,128,768]{4,3,2,1,0:T(8,128)(2,1)}, f32[3,2,512,768]{3,2,1,0:T(8,128)}) custom-call(bf16[16,64,64]{2,1,0:T(8,128)(2,1)} %small, bf16[2,512,512]{2,1,0:T(8,128)(2,1)} %get-tuple-element.50.big, bf16[2,512,768]{2,1,0:T(8,128)(2,1)} %bitcast.36, bf16[4,3,2,128,768]{4,3,2,1,0:T(8,128)(2,1)} %all-to-all-done.refs_0_), custom_call_target="tpu_custom_call" | custom-call | flops 1000 | bytes 1000 | tf_op jit(solution)/shard_map/pallas_call | solution.py:155
  81.7 13.7 %collective-permute-done.5.refs_1_ = bf16[3,2,128,768]{3,2,1,0:T(8,128)(2,1)S(1)} collective-permute-done((bf16[3,2,128,768]{3,2,1,0:T(8,128)(2,1)}, bf16[3,2,128,768]{3,2,1,0:T(8,128)(2,1)S(1)}, u32[]{:S(2)}, u32[]{:S(2)}) %collective-permute-start.5) | collective-permute-done | bytes 1179680 | tf_op jit(solution)/shard_map/ppermute | solution.py:362
  95.4 24.5 %collective-permute-done.7.refs_3_ = bf16[3,2,128,768]{3,2,1,0:T(8,128)(2,1)S(1)} collective-permute-done((bf16[3,2,128,768]{3,2,1,0:T(8,128)(2,1)}, bf16[3,2,128,768]{3,2,1,0:T(8,128)(2,1)S(1)}, u32[]{:S(2)}, u32[]{:S(2)}) %collective-permute-start.7) | collective-permute-done | bytes 1179680 | tf_op jit(solution)/shard_map/ppermute | solution.py:362
  119.9 1.0 copy-done.3
  120.9 4.9 %all-to-all-start.1 = ((bf16[4,3,2,128,768]{4,3,2,1,0:T(8,128)(2,1)}), bf16[4,3,2,128,768]{4,3,2,1,0:T(8,128)(2,1)}, u32[]{:S(2)}, u32[]{:S(2)}) async-start(bf16[4,3,2,128,768]{4,3,2,1,0:T(8,128)(2,1)} %get-tuple-element.66), calls=%async_computation.1 | async-start | bytes 9437184 | tf_op jit(solution)/shard_map/all_to_all | solution.py:367
  125.9 7.6 %shard_map.107 = (bf16[4,3,2,128,512]{4,3,2,1,0:T(8,128)(2,1)}, f32[2,512,512]{2,1,0:T(8,128)}) custom-call(bf16[16,64,64]{2,1,0:T(8,128)(2,1)} %get-tuple-element.62.small, bf16[2,512,512]{2,1,0:T(8,128)(2,1)} %get-tuple-element.56.big, bf16[2,512,768]{2,1,0:T(8,128)(2,1)} %bitcast.37, f32[3,2,512,768]{3,2,1,0:T(8,128)} %get-tuple-element.54.second, ...), custom_call_target="tpu_custom_call" | custom-call | flops 1000 | bytes 1000 | tf_op jit(solution)/shard_map/pallas_call | solution.py:198
  133.5 5.6 %shard_map.108 = (bf16[4,3,2,128,256]{4,3,2,1,0:T(8,128)(2,1)}, f32[2,512,256]{2,1,0:T(8,128)}) custom-call(bf16[16,64,64]{2,1,0:T(8,128)(2,1)} %get-tuple-element.62.small, bf16[2,512,512]{2,1,0:T(8,128)(2,1)} %get-tuple-element.56.big, bf16[2,512,768]{2,1,0:T(8,128)(2,1)} %bitcast.38, f32[3,2,512,768]{3,2,1,0:T(8,128)} %get-tuple-element.54.second, ...), custom_call_target="tpu_custom_call" | custom-call | flops 1000 | bytes 1000 | tf_op jit(solution)/shard_map/pallas_call | solution.py:198
  139.1 1.6 maximum_multiply_fusion
  140.7 1.0 dynamic-slice_convert_fusion
  141.7 2.6 %collective-permute-done.8 = bf16[512,768]{1,0:T(8,128)(2,1)} collective-permute-done((bf16[512,768]{1,0:T(8,128)(2,1)}, bf16[512,768]{1,0:T(8,128)(2,1)}, u32[]{:S(2)}, u32[]{:S(2)}) %collective-permute-start.8) | collective-permute-done | bytes 786464 | tf_op jit(solution)/shard_map/ppermute | solution.py:362
  144.3 1.3 convert_add_fusion
  145.6 1.1 copy-done.4
  146.8 2.8 %collective-permute-start.10 = (bf16[128,768]{1,0:T(8,128)(2,1)S(1)}, bf16[128,768]{1,0:T(8,128)(2,1)S(1)}, u32[]{:S(2)}, u32[]{:S(2)}) collective-permute-start(bf16[128,768]{1,0:T(8,128)(2,1)S(1)} %get-tuple-element.85), channel_id=1, source_target_pairs={{0,16},{4,20},{8,24},{12,28},{16,0},{20,4},{24,8},{28,12},{1,17},{... | collective-permute-start | bytes 589832 | tf_op jit(solution)/shard_map/ppermute | solution.py:362
  149.6 1.3 collective-permute-start.11
  151.1 12.8 %collective-permute-done.10 = bf16[128,768]{1,0:T(8,128)(2,1)S(1)} collective-permute-done((bf16[128,768]{1,0:T(8,128)(2,1)S(1)}, bf16[128,768]{1,0:T(8,128)(2,1)S(1)}, u32[]{:S(2)}, u32[]{:S(2)}) %collective-permute-start.10) | collective-permute-done | bytes 196640 | tf_op jit(solution)/shard_map/ppermute | solution.py:362
  164.0 0.6 collective-permute-done.9
  164.6 1.1 add_convert_fusion
  165.7 3.7 %collective-permute-start.12 = (bf16[128,768]{1,0:T(8,128)(2,1)S(1)}, bf16[128,768]{1,0:T(8,128)(2,1)S(1)}, u32[]{:S(2)}, u32[]{:S(2)}) collective-permute-start(bf16[128,768]{1,0:T(8,128)(2,1)S(1)} %add_convert_fusion), channel_id=1, source_target_pairs={{0,8},{4,12},{8,0},{12,4},{16,24},{20,28},{24,16},{28,20},{1,9},{5... | collective-permute-start | bytes 589832 | tf_op jit(solution)/shard_map/ppermute | solution.py:362
  169.3 2.0 collective-permute-start.13
  171.3 1.4 collective-permute-start.14
  172.7 5.0 %all-to-all-done.1.refs_0_ = bf16[4,3,2,128,768]{4,3,2,1,0:T(8,128)(2,1)} async-done(((bf16[4,3,2,128,768]{4,3,2,1,0:T(8,128)(2,1)}), bf16[4,3,2,128,768]{4,3,2,1,0:T(8,128)(2,1)}, u32[]{:S(2)}, u32[]{:S(2)}) %all-to-all-start.1) | async-done | bytes 4718624 | tf_op jit(solution)/shard_map/all_to_all | solution.py:367
  177.7 3.9 %all-to-all-start.2 = ((bf16[4,3,2,128,512]{4,3,2,1,0:T(8,128)(2,1)}), bf16[4,3,2,128,512]{4,3,2,1,0:T(8,128)(2,1)S(1)}, u32[]{:S(2)}, u32[]{:S(2)}) async-start(bf16[4,3,2,128,512]{4,3,2,1,0:T(8,128)(2,1)} %get-tuple-element.71), calls=%async_computation.2 | async-start | bytes 6291456 | tf_op jit(solution)/shard_map/all_to_all | solution.py:367
  181.6 17.4 %shard_map.109 = (f32[3,1024,768]{2,1,0:T(8,128)}, f32[4,96,768]{2,1,0:T(8,128)}, bf16[4,96,768]{2,1,0:T(8,128)(2,1)}) custom-call(bf16[2,512,512]{2,1,0:T(8,128)(2,1)} %get-tuple-element.64.big, f32[3,1024,768]{2,1,0:T(8,128)} %get-tuple-element.52.sloped, f32[768,768]{1,0:T(8,128)} %bitcast.34, bf16[3,1024,768]{2,1,0:T(8,128)(2,1)} %bitcast.32, ...), custom_call_target="tpu_custom_call" | custom-call | flops 1000 | bytes 1000 | tf_op jit(solution)/shard_map/pallas_call | solution.py:300
  199.1 2.3 collective-permute-done.15
  201.4 2.5 convert_add_fusion.1
  204.0 1.1 pad_maximum_fusion
  205.2 1.0 reverse_select_fusion
  206.3 1.9 dynamic-slice_convert_fusion.6
  208.2 1.4 collective-permute-start.16
  209.7 2.6 %collective-permute-start.17 = (bf16[4,24,768]{2,1,0:T(8,128)(2,1)}, bf16[4,24,768]{2,1,0:T(8,128)(2,1)S(1)}, u32[]{:S(2)}, u32[]{:S(2)}) collective-permute-start(bf16[4,24,768]{2,1,0:T(8,128)(2,1)} %get-tuple-element.88), channel_id=1, source_target_pairs={{0,16},{4,20},{8,24},{12,28},{16,0},{20,4},{24,8},{28,12},{1,17},{... | collective-permute-start | bytes 442376 | tf_op jit(solution)/shard_map/ppermute | solution.py:362
  212.6 4.6 %collective-permute-done.16 = bf16[4,24,768]{2,1,0:T(8,128)(2,1)S(1)} collective-permute-done((bf16[4,24,768]{2,1,0:T(8,128)(2,1)}, bf16[4,24,768]{2,1,0:T(8,128)(2,1)S(1)}, u32[]{:S(2)}, u32[]{:S(2)}) %collective-permute-start.16) | collective-permute-done | bytes 147488 | tf_op jit(solution)/shard_map/ppermute | solution.py:362
  217.2 6.6 %collective-permute-done.17 = bf16[4,24,768]{2,1,0:T(8,128)(2,1)S(1)} collective-permute-done((bf16[4,24,768]{2,1,0:T(8,128)(2,1)}, bf16[4,24,768]{2,1,0:T(8,128)(2,1)S(1)}, u32[]{:S(2)}, u32[]{:S(2)}) %collective-permute-start.17) | collective-permute-done | bytes 147488 | tf_op jit(solution)/shard_map/ppermute | solution.py:362
  223.8 0.7 copy-done.9
  224.5 1.2 convert_add_fusion.2
  225.8 0.7 constant_dynamic-slice_fusion.2
  226.4 1.8 collective-permute-start.20
  228.2 1.5 collective-permute-start.21
  229.9 1.6 copy-done
  231.6 4.3 %all-to-all-start.3 = ((bf16[4,3,2,128,256]{4,3,2,1,0:T(8,128)(2,1)}), bf16[4,3,2,128,256]{4,3,2,1,0:T(8,128)(2,1)}, u32[]{:S(2)}, u32[]{:S(2)}) async-start(bf16[4,3,2,128,256]{4,3,2,1,0:T(8,128)(2,1)} %get-tuple-element.79), calls=%async_computation.3 | async-start | bytes 3145728 | tf_op jit(solution)/shard_map/all_to_all | solution.py:367
  236.0 1.0 add_add_fusion
  236.9 2.4 collective-permute-start.23
  239.3 1.1 collective-permute-start.24
  240.4 1.4 collective-permute-start.25
  241.8 6.2 %shard_map.110.refs_1_ = bf16[3,1024,768]{2,1,0:T(8,128)(2,1)} custom-call(bf16[2,512,512]{2,1,0:T(8,128)(2,1)} %get-tuple-element.45.big, f32[3,1024,768]{2,1,0:T(8,128)} %get-tuple-element.67.other, bf16[4,3,2,128,512]{4,3,2,1,0:T(8,128)(2,1)} %copy-done), custom_call_target="tpu_custom_call" | custom-call | flops 1000 | bytes 1000 | tf_op jit(solution)/shard_map/pallas_call | solution.py:344
  248.2 3.3 %maximum_select_fusion.1 = bf16[1024,768]{1,0:T(8,128)(2,1)} fusion(bf16[512,768]{1,0:T(8,128)(2,1)} %collective-permute-done.19, bf16[512,768]{1,0:T(8,128)(2,1)} %bitcast.21, pred[]{:T(512)S(6)} %eq.44), kind=kLoop, calls=%fused_computation.2 | loop fusion | flops 7077888 | bytes 3145729 | tf_op jit(solution)/shard_map/jit(_where)/select_n | solution.py:393
  251.5 0.9 maximum_select_fusion.3
  252.4 0.5 all-to-all-done.3.refs_0_
  252.9 4.1 %shard_map.111 = bf16[3,1024,768]{2,1,0:T(8,128)(2,1)} custom-call(bf16[2,512,512]{2,1,0:T(8,128)(2,1)} %get-tuple-element.45.big, f32[3,1024,768]{2,1,0:T(8,128)} %get-tuple-element.67.other, bf16[4,3,2,128,256]{4,3,2,1,0:T(8,128)(2,1)} %all-to-all-done.3.refs_0_, bf16[3,1024,768]{2,1,0:T(8,128)(2,1)} %shard_map.110.refs_1_), custom_call_target="tpu_custom_call", output_to_operand_aliasing={{}: (3, {})} | custom-call | flops 1000 | bytes 1000 | tf_op jit(solution)/shard_map/pallas_call | solution.py:344
  (57 shorter events, 2.6 us)
Async XLA Ops:
  6.2 9.6 %copy-start.6 = (bf16[16,64,64]{2,1,0:T(8,128)(2,1)S(1)}, bf16[16,64,64]{2,1,0:T(8,128)(2,1)}, u32[]{:S(2)}) copy-start(bf16[16,64,64]{2,1,0:T(8,128)(2,1)} %right_out.1) | copy-start | bytes 393220
  6.2 16.4 %collective-permute-start.2 = (f32[48,768]{1,0:T(8,128)S(1)}, f32[48,768]{1,0:T(8,128)S(1)}, u32[]{:S(2)}, u32[]{:S(2)}) collective-permute-start(f32[48,768]{1,0:T(8,128)S(1)} %get-tuple-element.93), channel_id=1, source_target_pairs={{0,3},{1,2},{2,1},{3,0},{4,7},{5,6},{6,5},{7,4},{8,11},{9,10},{10,... | collective-permute-start | bytes 442376 | tf_op jit(solution)/shard_map/ppermute | solution.py:362
  10.2 12.4 %collective-permute-start = (f32[48,768]{1,0:T(8,128)S(1)}, f32[48,768]{1,0:T(8,128)S(1)}, u32[]{:S(2)}, u32[]{:S(2)}) collective-permute-start(f32[48,768]{1,0:T(8,128)S(1)} %get-tuple-element.93), channel_id=1, source_target_pairs={{0,1},{1,0},{2,3},{3,2},{4,5},{5,4},{6,7},{7,6},{8,9},{9,8},{10,11... | collective-permute-start | bytes 442376 | tf_op jit(solution)/shard_map/ppermute | solution.py:362
  10.7 11.9 %collective-permute-start.1 = (f32[48,768]{1,0:T(8,128)S(1)}, f32[48,768]{1,0:T(8,128)S(1)}, u32[]{:S(2)}, u32[]{:S(2)}) collective-permute-start(f32[48,768]{1,0:T(8,128)S(1)} %get-tuple-element.93), channel_id=1, source_target_pairs={{0,2},{1,3},{2,0},{3,1},{4,6},{5,7},{6,4},{7,5},{8,10},{9,11},{10,... | collective-permute-start | bytes 442376 | tf_op jit(solution)/shard_map/ppermute | solution.py:362
  10.8 59.4 %all-to-all-start = ((bf16[4,3,2,128,768]{4,3,2,1,0:T(8,128)(2,1)}), bf16[4,3,2,128,768]{4,3,2,1,0:T(8,128)(2,1)}, u32[]{:S(2)}, u32[]{:S(2)}) async-start(bf16[4,3,2,128,768]{4,3,2,1,0:T(8,128)(2,1)} %shard_map.103), calls=%async_computation | async-start | bytes 9437184 | tf_op jit(solution)/shard_map/all_to_all | solution.py:367
  15.8 1.2 copy-start.7
  22.8 14.6 %collective-permute-start.3 = (f32[4,48,768]{2,1,0:T(8,128)S(1)}, f32[4,48,768]{2,1,0:T(8,128)S(1)}, u32[]{:S(2)}, u32[]{:S(2)}) collective-permute-start(f32[4,48,768]{2,1,0:T(8,128)S(1)} %bitcast.44), channel_id=1, source_target_pairs={{0,8},{4,12},{8,0},{12,4},{16,24},{20,28},{24,16},{28,20},{1,9},{5... | collective-permute-start | bytes 1769480 | tf_op jit(solution)/shard_map/ppermute | solution.py:362
  37.5 2.9 %collective-permute-start.4 = (f32[4,96,768]{2,1,0:T(8,128)S(1)}, f32[4,96,768]{2,1,0:T(8,128)S(1)}, u32[]{:S(2)}, u32[]{:S(2)}) collective-permute-start(f32[4,96,768]{2,1,0:T(8,128)S(1)} %maximum_select_fusion.2), channel_id=1, source_target_pairs={{0,4},{4,0},{8,12},{12,8},{16,20},{20,16},{24,28},{28,24},{1,5},{5... | collective-permute-start | bytes 3538952 | tf_op jit(solution)/shard_map/ppermute | solution.py:362
  58.7 36.7 %collective-permute-start.5 = (bf16[3,2,128,768]{3,2,1,0:T(8,128)(2,1)}, bf16[3,2,128,768]{3,2,1,0:T(8,128)(2,1)S(1)}, u32[]{:S(2)}, u32[]{:S(2)}) collective-permute-start(bf16[3,2,128,768]{3,2,1,0:T(8,128)(2,1)} %get-tuple-element.58), channel_id=1, source_target_pairs={{0,1},{1,0},{2,3},{3,2},{4,5},{5,4},{6,7},{7,6},{8,9},{9,8},{10,11... | collective-permute-start | bytes 3538952 | tf_op jit(solution)/shard_map/ppermute | solution.py:362
  60.4 35.1 %collective-permute-start.6 = (bf16[3,2,128,768]{3,2,1,0:T(8,128)(2,1)}, bf16[3,2,128,768]{3,2,1,0:T(8,128)(2,1)S(1)}, u32[]{:S(2)}, u32[]{:S(2)}) collective-permute-start(bf16[3,2,128,768]{3,2,1,0:T(8,128)(2,1)} %get-tuple-element.59), channel_id=1, source_target_pairs={{0,2},{1,3},{2,0},{3,1},{4,6},{5,7},{6,4},{7,5},{8,10},{9,11},{10,... | collective-permute-start | bytes 3538952 | tf_op jit(solution)/shard_map/ppermute | solution.py:362
  61.8 58.1 %collective-permute-start.7 = (bf16[3,2,128,768]{3,2,1,0:T(8,128)(2,1)}, bf16[3,2,128,768]{3,2,1,0:T(8,128)(2,1)S(1)}, u32[]{:S(2)}, u32[]{:S(2)}) collective-permute-start(bf16[3,2,128,768]{3,2,1,0:T(8,128)(2,1)} %get-tuple-element.60), channel_id=1, source_target_pairs={{0,3},{1,2},{2,1},{3,0},{4,7},{5,6},{6,5},{7,4},{8,11},{9,10},{10,... | collective-permute-start | bytes 3538952 | tf_op jit(solution)/shard_map/ppermute | solution.py:362
  95.4 24.5 %copy-start.1 = (bf16[3,2,128,768]{3,2,1,0:T(8,128)(2,1)}, bf16[3,2,128,768]{3,2,1,0:T(8,128)(2,1)S(1)}, u32[]{:S(2)}) copy-start(bf16[3,2,128,768]{3,2,1,0:T(8,128)(2,1)S(1)} %collective-permute-done.5.refs_1_) | copy-start | bytes 3538948
  95.4 24.5 %copy-start.2 = (bf16[3,2,128,768]{3,2,1,0:T(8,128)(2,1)}, bf16[3,2,128,768]{3,2,1,0:T(8,128)(2,1)S(1)}, u32[]{:S(2)}) copy-start(bf16[3,2,128,768]{3,2,1,0:T(8,128)(2,1)S(1)} %collective-permute-done.6.refs_2_) | copy-start | bytes 3538948
  119.9 1.0 copy-start.3
  120.9 56.8 %all-to-all-start.1 = ((bf16[4,3,2,128,768]{4,3,2,1,0:T(8,128)(2,1)}), bf16[4,3,2,128,768]{4,3,2,1,0:T(8,128)(2,1)}, u32[]{:S(2)}, u32[]{:S(2)}) async-start(bf16[4,3,2,128,768]{4,3,2,1,0:T(8,128)(2,1)} %get-tuple-element.66), calls=%async_computation.1 | async-start | bytes 9437184 | tf_op jit(solution)/shard_map/all_to_all | solution.py:367
  133.5 5.6 %copy-start.5 = (f32[2,512,512]{2,1,0:T(8,128)S(1)}, f32[2,512,512]{2,1,0:T(8,128)}, u32[]{:S(2)}) copy-start(f32[2,512,512]{2,1,0:T(8,128)} %get-tuple-element.61) | copy-start | bytes 6291460
  141.7 2.6 %collective-permute-start.8 = (bf16[512,768]{1,0:T(8,128)(2,1)}, bf16[512,768]{1,0:T(8,128)(2,1)}, u32[]{:S(2)}, u32[]{:S(2)}) collective-permute-start(bf16[512,768]{1,0:T(8,128)(2,1)} %dynamic-slice_convert_fusion), channel_id=1, source_target_pairs={{0,4},{4,0},{8,12},{12,8},{16,20},{20,16},{24,28},{28,24},{1,5},{5... | collective-permute-start | bytes 2359304 | tf_op jit(solution)/shard_map/ppermute | solution.py:362
  145.6 1.1 copy-start.4
  146.8 17.2 %collective-permute-start.10 = (bf16[128,768]{1,0:T(8,128)(2,1)S(1)}, bf16[128,768]{1,0:T(8,128)(2,1)S(1)}, u32[]{:S(2)}, u32[]{:S(2)}) collective-permute-start(bf16[128,768]{1,0:T(8,128)(2,1)S(1)} %get-tuple-element.85), channel_id=1, source_target_pairs={{0,16},{4,20},{8,24},{12,28},{16,0},{20,4},{24,8},{28,12},{1,17},{... | collective-permute-start | bytes 589832 | tf_op jit(solution)/shard_map/ppermute | solution.py:362
  149.6 14.4 %collective-permute-start.11 = (bf16[128,768]{1,0:T(8,128)(2,1)S(1)}, bf16[128,768]{1,0:T(8,128)(2,1)S(1)}, u32[]{:S(2)}, u32[]{:S(2)}) collective-permute-start(bf16[128,768]{1,0:T(8,128)(2,1)S(1)} %get-tuple-element.84), channel_id=1, source_target_pairs={{0,24},{4,28},{8,16},{12,20},{16,8},{20,12},{24,0},{28,4},{1,25},{... | collective-permute-start | bytes 589832 | tf_op jit(solution)/shard_map/ppermute | solution.py:362
  150.9 13.7 %collective-permute-start.9 = (bf16[128,768]{1,0:T(8,128)(2,1)S(1)}, bf16[128,768]{1,0:T(8,128)(2,1)S(1)}, u32[]{:S(2)}, u32[]{:S(2)}) collective-permute-start(bf16[128,768]{1,0:T(8,128)(2,1)S(1)} %get-tuple-element.83), channel_id=1, source_target_pairs={{0,8},{4,12},{8,0},{12,4},{16,24},{20,28},{24,16},{28,20},{1,9},{5... | collective-permute-start | bytes 589832 | tf_op jit(solution)/shard_map/ppermute | solution.py:362
  165.7 33.3 %collective-permute-start.12 = (bf16[128,768]{1,0:T(8,128)(2,1)S(1)}, bf16[128,768]{1,0:T(8,128)(2,1)S(1)}, u32[]{:S(2)}, u32[]{:S(2)}) collective-permute-start(bf16[128,768]{1,0:T(8,128)(2,1)S(1)} %add_convert_fusion), channel_id=1, source_target_pairs={{0,8},{4,12},{8,0},{12,4},{16,24},{20,28},{24,16},{28,20},{1,9},{5... | collective-permute-start | bytes 589832 | tf_op jit(solution)/shard_map/ppermute | solution.py:362
  169.3 29.7 %collective-permute-start.13 = (bf16[128,768]{1,0:T(8,128)(2,1)S(1)}, bf16[128,768]{1,0:T(8,128)(2,1)}, u32[]{:S(2)}, u32[]{:S(2)}) collective-permute-start(bf16[128,768]{1,0:T(8,128)(2,1)S(1)} %add_convert_fusion), channel_id=1, source_target_pairs={{0,16},{4,20},{8,24},{12,28},{16,0},{20,4},{24,8},{28,12},{1,17},{... | collective-permute-start | bytes 589832 | tf_op jit(solution)/shard_map/ppermute | solution.py:362
  171.3 27.7 %collective-permute-start.14 = (bf16[128,768]{1,0:T(8,128)(2,1)S(1)}, bf16[128,768]{1,0:T(8,128)(2,1)}, u32[]{:S(2)}, u32[]{:S(2)}) collective-permute-start(bf16[128,768]{1,0:T(8,128)(2,1)S(1)} %add_convert_fusion), channel_id=1, source_target_pairs={{0,24},{4,28},{8,16},{12,20},{16,8},{20,12},{24,0},{28,4},{1,25},{... | collective-permute-start | bytes 589832 | tf_op jit(solution)/shard_map/ppermute | solution.py:362
  177.7 52.2 %all-to-all-start.2 = ((bf16[4,3,2,128,512]{4,3,2,1,0:T(8,128)(2,1)}), bf16[4,3,2,128,512]{4,3,2,1,0:T(8,128)(2,1)S(1)}, u32[]{:S(2)}, u32[]{:S(2)}) async-start(bf16[4,3,2,128,512]{4,3,2,1,0:T(8,128)(2,1)} %get-tuple-element.71), calls=%async_computation.2 | async-start | bytes 6291456 | tf_op jit(solution)/shard_map/all_to_all | solution.py:367
  199.0 2.4 collective-permute-start.15
  206.2 23.7 %collective-permute-start.19 = (bf16[512,768]{1,0:T(8,128)(2,1)}, bf16[512,768]{1,0:T(8,128)(2,1)}, u32[]{:S(2)}, u32[]{:S(2)}) collective-permute-start(bf16[512,768]{1,0:T(8,128)(2,1)} %bitcast.21), channel_id=1, source_target_pairs={{0,4},{4,0},{8,12},{12,8},{16,20},{20,16},{24,28},{28,24},{1,5},{5... | collective-permute-start | bytes 2359304 | tf_op jit(solution)/shard_map/ppermute | solution.py:362
  208.2 9.0 %collective-permute-start.16 = (bf16[4,24,768]{2,1,0:T(8,128)(2,1)}, bf16[4,24,768]{2,1,0:T(8,128)(2,1)S(1)}, u32[]{:S(2)}, u32[]{:S(2)}) collective-permute-start(bf16[4,24,768]{2,1,0:T(8,128)(2,1)} %get-tuple-element.86), channel_id=1, source_target_pairs={{0,8},{4,12},{8,0},{12,4},{16,24},{20,28},{24,16},{28,20},{1,9},{5... | collective-permute-start | bytes 442376 | tf_op jit(solution)/shard_map/ppermute | solution.py:362
  209.7 14.2 %collective-permute-start.17 = (bf16[4,24,768]{2,1,0:T(8,128)(2,1)}, bf16[4,24,768]{2,1,0:T(8,128)(2,1)S(1)}, u32[]{:S(2)}, u32[]{:S(2)}) collective-permute-start(bf16[4,24,768]{2,1,0:T(8,128)(2,1)} %get-tuple-element.88), channel_id=1, source_target_pairs={{0,16},{4,20},{8,24},{12,28},{16,0},{20,4},{24,8},{28,12},{1,17},{... | collective-permute-start | bytes 442376 | tf_op jit(solution)/shard_map/ppermute | solution.py:362
  212.2 12.3 %collective-permute-start.18 = (bf16[4,24,768]{2,1,0:T(8,128)(2,1)}, bf16[4,24,768]{2,1,0:T(8,128)(2,1)}, u32[]{:S(2)}, u32[]{:S(2)}) collective-permute-start(bf16[4,24,768]{2,1,0:T(8,128)(2,1)} %get-tuple-element.87), channel_id=1, source_target_pairs={{0,24},{4,28},{8,16},{12,20},{16,8},{20,12},{24,0},{28,4},{1,25},{... | collective-permute-start | bytes 442376 | tf_op jit(solution)/shard_map/ppermute | solution.py:362
  217.2 6.6 %copy-start.8 = (bf16[4,24,768]{2,1,0:T(8,128)(2,1)}, bf16[4,24,768]{2,1,0:T(8,128)(2,1)S(1)}, u32[]{:S(2)}) copy-start(bf16[4,24,768]{2,1,0:T(8,128)(2,1)S(1)} %collective-permute-done.16) | copy-start | bytes 442372
  223.8 0.7 copy-start.9
  226.4 9.5 %collective-permute-start.20 = (f32[1,24,768]{2,1,0:T(8,128)}, f32[1,24,768]{2,1,0:T(8,128)}, u32[]{:S(2)}, u32[]{:S(2)}) collective-permute-start(f32[1,24,768]{2,1,0:T(8,128)} %get-tuple-element.89), channel_id=1, source_target_pairs={{0,1},{1,0},{2,3},{3,2},{4,5},{5,4},{6,7},{7,6},{8,9},{9,8},{10,11... | collective-permute-start | bytes 221192 | tf_op jit(solution)/shard_map/ppermute | solution.py:362
  228.2 7.7 %collective-permute-start.21 = (f32[1,24,768]{2,1,0:T(8,128)}, f32[1,24,768]{2,1,0:T(8,128)}, u32[]{:S(2)}, u32[]{:S(2)}) collective-permute-start(f32[1,24,768]{2,1,0:T(8,128)} %get-tuple-element.91), channel_id=1, source_target_pairs={{0,2},{1,3},{2,0},{3,1},{4,6},{5,7},{6,4},{7,5},{8,10},{9,11},{10,... | collective-permute-start | bytes 221192 | tf_op jit(solution)/shard_map/ppermute | solution.py:362
  229.7 6.3 %collective-permute-start.22 = (f32[1,24,768]{2,1,0:T(8,128)S(1)}, f32[1,24,768]{2,1,0:T(8,128)}, u32[]{:S(2)}, u32[]{:S(2)}) collective-permute-start(f32[1,24,768]{2,1,0:T(8,128)S(1)} %get-tuple-element.90), channel_id=1, source_target_pairs={{0,3},{1,2},{2,1},{3,0},{4,7},{5,6},{6,5},{7,4},{8,11},{9,10},{10,... | collective-permute-start | bytes 221192 | tf_op jit(solution)/shard_map/ppermute | solution.py:362
  229.9 1.6 copy-start
  231.6 21.3 %all-to-all-start.3 = ((bf16[4,3,2,128,256]{4,3,2,1,0:T(8,128)(2,1)}), bf16[4,3,2,128,256]{4,3,2,1,0:T(8,128)(2,1)}, u32[]{:S(2)}, u32[]{:S(2)}) async-start(bf16[4,3,2,128,256]{4,3,2,1,0:T(8,128)(2,1)} %get-tuple-element.79), calls=%async_computation.3 | async-start | bytes 3145728 | tf_op jit(solution)/shard_map/all_to_all | solution.py:367
  236.9 11.0 %collective-permute-start.23 = (f32[1,24,768]{2,1,0:T(8,128)S(1)}, f32[1,24,768]{2,1,0:T(8,128)S(1)}, u32[]{:S(2)}, u32[]{:S(2)}) collective-permute-start(f32[1,24,768]{2,1,0:T(8,128)S(1)} %add_add_fusion), channel_id=1, source_target_pairs={{0,8},{4,12},{8,0},{12,4},{16,24},{20,28},{24,16},{28,20},{1,9},{5... | collective-permute-start | bytes 221192 | tf_op jit(solution)/shard_map/ppermute | solution.py:362
  239.3 8.7 %collective-permute-start.24 = (f32[1,24,768]{2,1,0:T(8,128)S(1)}, f32[1,24,768]{2,1,0:T(8,128)S(1)}, u32[]{:S(2)}, u32[]{:S(2)}) collective-permute-start(f32[1,24,768]{2,1,0:T(8,128)S(1)} %add_add_fusion), channel_id=1, source_target_pairs={{0,16},{4,20},{8,24},{12,28},{16,0},{20,4},{24,8},{28,12},{1,17},{... | collective-permute-start | bytes 221192 | tf_op jit(solution)/shard_map/ppermute | solution.py:362
  240.4 7.6 %collective-permute-start.25 = (f32[1,24,768]{2,1,0:T(8,128)S(1)}, f32[1,24,768]{2,1,0:T(8,128)S(1)}, u32[]{:S(2)}, u32[]{:S(2)}) collective-permute-start(f32[1,24,768]{2,1,0:T(8,128)S(1)} %add_add_fusion), channel_id=1, source_target_pairs={{0,24},{4,28},{8,16},{12,20},{16,8},{20,12},{24,0},{28,4},{1,25},{... | collective-permute-start | bytes 221192 | tf_op jit(solution)/shard_map/ppermute | solution.py:362
  248.1 3.4 %collective-permute-start.26 = (f32[1,96,768]{2,1,0:T(8,128)S(1)}, f32[1,96,768]{2,1,0:T(8,128)S(1)}, u32[]{:S(2)}, u32[]{:S(2)}) collective-permute-start(f32[1,96,768]{2,1,0:T(8,128)S(1)} %bitcast.49), channel_id=1, source_target_pairs={{0,4},{4,0},{8,12},{12,8},{16,20},{20,16},{24,28},{28,24},{1,5},{5... | collective-permute-start | bytes 884744 | tf_op jit(solution)/shard_map/ppermute | solution.py:362

commit v3 on v2

--- a/solution.py
+++ b/solution.py
@@ -409,14 +409,15 @@
     return value
 
 
-def scatter(value, axis, unit, dim, kind):
+def scatter(value, axis, unit, dim, kind, earlier=()):
     peers = lax.axis_size(axis) // unit
     block = value.shape[dim] // peers
     me = lax.axis_index(axis) // unit
     total = lax.dynamic_slice_in_dim(value, me * block, block, dim)
     for r in range(1, peers):
         part = lax.dynamic_slice_in_dim(value, jnp.bitwise_xor(me, r) * block, block, dim)
-        total = total + swap(part.astype(kind), axis, r * unit).astype(F32)
+        moved = swap(part.astype(kind), axis, r * unit)
+        total = total + (after(moved, *earlier) if earlier else moved).astype(F32)
     return total
 
 
@@ -499,18 +500,16 @@
         devices, True, weight_scale, after(big_qo, kernel_grad), sloped, weights, flat, returned
     )
     kernel_blocks = blocks_of(kernel_grad, "section", 2)
-    weight_grad = keep + swap(after(sent, *kernel_blocks), "section", 1).astype(F32)
-    kernel_grad = collect(after(kernel_blocks, weight_grad), "section", 2, 0)
-    kernel_other = swap(kernel_grad, "section", 1)
-    weight_grad = scatter(weight_grad, "section", 2, 1, BF16)
+    kernel_grad = collect(after(kernel_blocks, sent), "section", 2, 0)
+    moved = swap(after(sent, *kernel_blocks), "section", 1)
+    weight_grad = keep + after(moved, kernel_grad).astype(F32)
+    kernel_grad = double(kernel_grad, "section", 1, 0)
+    weight_grad = scatter(weight_grad, "section", 2, 1, BF16, [kernel_grad])
     back_return = [exchange([after(back_first[0], *returned)])]
     back_return.append(
-        exchange([after(back_first[1], *back_return[0], weight_grad, kernel_other)])
+        exchange([after(back_first[1], *back_return[0], weight_grad, kernel_grad)])
     )
     weight_grad = scatter(weight_grad, "seq", 1, 0, F32)
-
-    kernel_other = after(kernel_other, *back_return[0])
-    kernel_grad = double(kernel_grad, "section", 1, 0, kernel_other)
 
     input_grad = None
     halves = []

time: 259 us -> 256 us (0.988)
  waiting for transfers between devices: 96.8 us -> 101 us
    all_to_all x4, waiting for transfers between devices: 13.6 us -> 22.3 us  [exchange(): return [lax.all_to_all(pieces[0], 'seq', 0, 0, tiled=True)]]
    ppermute x27, waiting for transfers between devices: 83.2 us -> 78.6 us  [swap(): return lax.ppermute(value, axis, [(i, i ^ bit) for i in range(size)])]
  transfers between devices with their start and end apart: 31 -> 31, of which waited for: 13 -> 13; matrix products, arithmetic and copies ran while one was open for 9% -> 7% of each run, Pallas kernels for 27% -> 27%
where the time goes in v3:
time: 256 us; the launch traced here: 254 us
  waiting for transfers between devices  101 us (39%)
  Pallas kernels  78.2 us (31%)
  starting transfers between devices  51 us (20%)
  other arithmetic  16.8 us (7%)
  local copies, waits for them, and re-layouts  6.59 us (3%)
    ppermute x27, waiting for transfers between devices, swap(): return lax.ppermute(value, axis, [(i, i ^ bit) for i in range(size)])  78.6 us
    ppermute x27, starting transfers between devices, swap(): return lax.ppermute(value, axis, [(i, i ^ bit) for i in range(size)])  32.9 us
    all_to_all x4, waiting for transfers between devices, exchange(): return [lax.all_to_all(pieces[0], 'seq', 0, 0, tiled=True)]  22.3 us
    all_to_all x4, starting transfers between devices, exchange(): return [lax.all_to_all(pieces[0], 'seq', 0, 0, tiled=True)]  18.1 us
    pallas_call x1, Pallas kernels, ending(): pl.pallas_call(functools.partial(ending_kernel, devices, len(pieces), sca...  17.3 us
    pallas_call x1, Pallas kernels, gate(): pl.pallas_call(functools.partial(gate_kernel, devices, width), grid=grid,...  16.7 us
    pallas_call x2, Pallas kernels, back_middle(): pl.pallas_call(functools.partial(back_middle_kernel, devices, len(pieces)...  13.2 us
    pallas_call x1, Pallas kernels, middle(): pl.pallas_call(functools.partial(middle_kernel, devices, len(pieces)), gr...  11.3 us
  transfers between devices with their start and end apart: 31, of which 13 were waited for; matrix products, arithmetic and copies ran while one was open for 7% of the time, Pallas kernels for 27%

profile of v3, /device:TPU:0, one launch (start us, length us, event | category | flops | bytes accessed | tf_op | source)
XLA Modules:
  0.0 254.5 jit_solution(3881622690888581527)
XLA Ops:
  0.7 4.7 %shard_map.103 = bf16[4,3,2,128,768]{4,3,2,1,0:T(8,128)(2,1)} custom-call(bf16[16,64,64]{2,1,0:T(8,128)(2,1)} %right_in.3, bf16[3,16,64,768]{3,2,1,0:T(8,128)(2,1)} %bitcast.30), custom_call_target="tpu_custom_call" | custom-call | flops 1000 | bytes 1000 | tf_op jit(solution)/shard_map/pallas_call | solution.py:118
  5.3 0.9 fusion.1
  6.2 4.0 %collective-permute-start.2 = (f32[48,768]{1,0:T(8,128)S(1)}, f32[48,768]{1,0:T(8,128)S(1)}, u32[]{:S(2)}, u32[]{:S(2)}) collective-permute-start(f32[48,768]{1,0:T(8,128)S(1)} %get-tuple-element.99), channel_id=1, source_target_pairs={{0,3},{1,2},{2,1},{3,0},{4,7},{5,6},{6,5},{7,4},{8,11},{9,10},{10,... | collective-permute-start | bytes 442376 | tf_op jit(solution)/shard_map/ppermute | solution.py:362
  10.2 0.5 collective-permute-start
  10.8 4.9 %all-to-all-start = ((bf16[4,3,2,128,768]{4,3,2,1,0:T(8,128)(2,1)}), bf16[4,3,2,128,768]{4,3,2,1,0:T(8,128)(2,1)}, u32[]{:S(2)}, u32[]{:S(2)}) async-start(bf16[4,3,2,128,768]{4,3,2,1,0:T(8,128)(2,1)} %shard_map.103), calls=%async_computation | async-start | bytes 9437184 | tf_op jit(solution)/shard_map/all_to_all | solution.py:367
  16.2 0.8 copy.13.right_turned
  17.1 0.8 reverse_select_fusion.8
  17.9 4.7 %shard_map.104 = (bf16[2,512,512]{2,1,0:T(8,128)(2,1)}, bf16[2,512,512]{2,1,0:T(8,128)(2,1)}, bf16[2,512,512]{2,1,0:T(8,128)(2,1)}, bf16[2,512,512]{2,1,0:T(8,12...) custom-call(bf16[16,64,64]{2,1,0:T(8,128)(2,1)} %left_in.1, bf16[16,64,64]{2,1,0:T(8,128)(2,1)} %bitcast.51, ...), custom_call_target="tpu_custom_call" | custom-call | flops 1000 | bytes 1000 | tf_op jit(solution)/shard_map/pallas_call | solution.py:80
  22.8 2.0 collective-permute-start.3
  24.8 12.5 %collective-permute-done.3 = f32[4,48,768]{2,1,0:T(8,128)S(1)} collective-permute-done((f32[4,48,768]{2,1,0:T(8,128)S(1)}, f32[4,48,768]{2,1,0:T(8,128)S(1)}, u32[]{:S(2)}, u32[]{:S(2)}) %collective-permute-start.3) | collective-permute-done | bytes 589856 | tf_op jit(solution)/shard_map/ppermute | solution.py:362
  37.6 2.8 %collective-permute-done.4 = f32[4,96,768]{2,1,0:T(8,128)S(1)} collective-permute-done((f32[4,96,768]{2,1,0:T(8,128)S(1)}, f32[4,96,768]{2,1,0:T(8,128)S(1)}, u32[]{:S(2)}, u32[]{:S(2)}) %collective-permute-start.4) | collective-permute-done | bytes 1179680 | tf_op jit(solution)/shard_map/ppermute | solution.py:362
  40.4 1.7 maximum_select_fusion
  42.0 16.7 %shard_map.105 = (bf16[3,2,128,768]{3,2,1,0:T(8,128)(2,1)}, bf16[3,2,128,768]{3,2,1,0:T(8,128)(2,1)}, bf16[3,2,128,768]{3,2,1,0:T(8,128)(2,1)}, bf16[3,2,128,768]{3,2,1,0:T(8,128)(2,1)}, f32[3,1024,768]{2,1,0:T(8,128)}) custom-call(bf16[16,64,64]{2,1,0:T(8,128)(2,1)} %get-tuple-element.51.small, f32[768,768]{1,0:T(8,128)} %bitcast.33, ...), custom_call_target="tpu_custom_call" | custom-call | flops 1000 | bytes 1000 | tf_op jit(solution)/shard_map/pallas_call | solution.py:249
  58.7 1.6 collective-permute-start.5
  60.4 1.5 collective-permute-start.6
  61.8 0.4 collective-permute-start.7
  62.2 8.0 %all-to-all-done.refs_0_ = bf16[4,3,2,128,768]{4,3,2,1,0:T(8,128)(2,1)} async-done(((bf16[4,3,2,128,768]{4,3,2,1,0:T(8,128)(2,1)}), bf16[4,3,2,128,768]{4,3,2,1,0:T(8,128)(2,1)}, u32[]{:S(2)}, u32[]{:S(2)}) %all-to-all-start) | async-done | bytes 4718624 | tf_op jit(solution)/shard_map/all_to_all | solution.py:367
  70.2 11.3 %shard_map.106 = (bf16[4,3,2,128,768]{4,3,2,1,0:T(8,128)(2,1)}, f32[3,2,512,768]{3,2,1,0:T(8,128)}) custom-call(bf16[16,64,64]{2,1,0:T(8,128)(2,1)} %small, bf16[2,512,512]{2,1,0:T(8,128)(2,1)} %get-tuple-element.53.big, bf16[2,512,768]{2,1,0:T(8,128)(2,1)} %bitcast.36, bf16[4,3,2,128,768]{4,3,2,1,0:T(8,128)(2,1)} %all-to-all-done.refs_0_), custom_call_target="tpu_custom_call" | custom-call | flops 1000 | bytes 1000 | tf_op jit(solution)/shard_map/pallas_call | solution.py:155
  81.6 13.9 %collective-permute-done.5.refs_1_ = bf16[3,2,128,768]{3,2,1,0:T(8,128)(2,1)S(1)} collective-permute-done((bf16[3,2,128,768]{3,2,1,0:T(8,128)(2,1)}, bf16[3,2,128,768]{3,2,1,0:T(8,128)(2,1)S(1)}, u32[]{:S(2)}, u32[]{:S(2)}) %collective-permute-start.5) | collective-permute-done | bytes 1179680 | tf_op jit(solution)/shard_map/ppermute | solution.py:362
  95.4 24.5 %collective-permute-done.7.refs_3_ = bf16[3,2,128,768]{3,2,1,0:T(8,128)(2,1)S(1)} collective-permute-done((bf16[3,2,128,768]{3,2,1,0:T(8,128)(2,1)}, bf16[3,2,128,768]{3,2,1,0:T(8,128)(2,1)S(1)}, u32[]{:S(2)}, u32[]{:S(2)}) %collective-permute-start.7) | collective-permute-done | bytes 1179680 | tf_op jit(solution)/shard_map/ppermute | solution.py:362
  119.9 1.0 copy-done.3
  120.9 4.9 %all-to-all-start.1 = ((bf16[4,3,2,128,768]{4,3,2,1,0:T(8,128)(2,1)}), bf16[4,3,2,128,768]{4,3,2,1,0:T(8,128)(2,1)}, u32[]{:S(2)}, u32[]{:S(2)}) async-start(bf16[4,3,2,128,768]{4,3,2,1,0:T(8,128)(2,1)} %get-tuple-element.69), calls=%async_computation.1 | async-start | bytes 9437184 | tf_op jit(solution)/shard_map/all_to_all | solution.py:367
  125.9 7.6 %shard_map.107 = (bf16[4,3,2,128,512]{4,3,2,1,0:T(8,128)(2,1)}, f32[2,512,512]{2,1,0:T(8,128)}) custom-call(bf16[16,64,64]{2,1,0:T(8,128)(2,1)} %get-tuple-element.65.small, bf16[2,512,512]{2,1,0:T(8,128)(2,1)} %get-tuple-element.59.big, bf16[2,512,768]{2,1,0:T(8,128)(2,1)} %bitcast.37, f32[3,2,512,768]{3,2,1,0:T(8,128)} %get-tuple-element.57.second, ...), custom_call_target="tpu_custom_call" | custom-call | flops 1000 | bytes 1000 | tf_op jit(solution)/shard_map/pallas_call | solution.py:198
  133.5 5.6 %shard_map.108 = (bf16[4,3,2,128,256]{4,3,2,1,0:T(8,128)(2,1)}, f32[2,512,256]{2,1,0:T(8,128)}) custom-call(bf16[16,64,64]{2,1,0:T(8,128)(2,1)} %get-tuple-element.65.small, bf16[2,512,512]{2,1,0:T(8,128)(2,1)} %get-tuple-element.59.big, bf16[2,512,768]{2,1,0:T(8,128)(2,1)} %bitcast.38, f32[3,2,512,768]{3,2,1,0:T(8,128)} %get-tuple-element.57.second, ...), custom_call_target="tpu_custom_call" | custom-call | flops 1000 | bytes 1000 | tf_op jit(solution)/shard_map/pallas_call | solution.py:198
  139.1 1.6 maximum_multiply_fusion
  140.6 1.0 dynamic-slice_convert_fusion
  141.6 2.6 %collective-permute-done.8 = bf16[512,768]{1,0:T(8,128)(2,1)} collective-permute-done((bf16[512,768]{1,0:T(8,128)(2,1)}, bf16[512,768]{1,0:T(8,128)(2,1)}, u32[]{:S(2)}, u32[]{:S(2)}) %collective-permute-start.8) | collective-permute-done | bytes 786464 | tf_op jit(solution)/shard_map/ppermute | solution.py:362
  144.2 1.3 convert_add_fusion
  145.5 1.1 copy-done.4
  146.7 2.8 %collective-permute-start.10 = (bf16[128,768]{1,0:T(8,128)(2,1)S(1)}, bf16[128,768]{1,0:T(8,128)(2,1)S(1)}, u32[]{:S(2)}, u32[]{:S(2)}) collective-permute-start(bf16[128,768]{1,0:T(8,128)(2,1)S(1)} %get-tuple-element.91), channel_id=1, source_target_pairs={{0,16},{4,20},{8,24},{12,28},{16,0},{20,4},{24,8},{28,12},{1,17},{... | collective-permute-start | bytes 589832 | tf_op jit(solution)/shard_map/ppermute | solution.py:362
  149.5 1.3 collective-permute-start.11
  151.1 12.8 %collective-permute-done.10 = bf16[128,768]{1,0:T(8,128)(2,1)S(1)} collective-permute-done((bf16[128,768]{1,0:T(8,128)(2,1)S(1)}, bf16[128,768]{1,0:T(8,128)(2,1)S(1)}, u32[]{:S(2)}, u32[]{:S(2)}) %collective-permute-start.10) | collective-permute-done | bytes 196640 | tf_op jit(solution)/shard_map/ppermute | solution.py:362
  163.9 0.6 collective-permute-done.9
  164.5 1.1 add_convert_fusion
  165.6 12.1 %all-to-all-done.1.refs_0_ = bf16[4,3,2,128,768]{4,3,2,1,0:T(8,128)(2,1)} async-done(((bf16[4,3,2,128,768]{4,3,2,1,0:T(8,128)(2,1)}), bf16[4,3,2,128,768]{4,3,2,1,0:T(8,128)(2,1)}, u32[]{:S(2)}, u32[]{:S(2)}) %all-to-all-start.1) | async-done | bytes 4718624 | tf_op jit(solution)/shard_map/all_to_all | solution.py:367
  177.7 3.9 %all-to-all-start.2 = ((bf16[4,3,2,128,512]{4,3,2,1,0:T(8,128)(2,1)}), bf16[4,3,2,128,512]{4,3,2,1,0:T(8,128)(2,1)S(1)}, u32[]{:S(2)}, u32[]{:S(2)}) async-start(bf16[4,3,2,128,512]{4,3,2,1,0:T(8,128)(2,1)} %get-tuple-element.74), calls=%async_computation.2 | async-start | bytes 6291456 | tf_op jit(solution)/shard_map/all_to_all | solution.py:367
  181.6 1.5 collective-permute-start.12
  183.1 2.6 %collective-permute-start.13 = (bf16[128,768]{1,0:T(8,128)(2,1)S(1)}, bf16[128,768]{1,0:T(8,128)(2,1)}, u32[]{:S(2)}, u32[]{:S(2)}) collective-permute-start(bf16[128,768]{1,0:T(8,128)(2,1)S(1)} %add_convert_fusion), channel_id=1, source_target_pairs={{0,16},{4,20},{8,24},{12,28},{16,0},{20,4},{24,8},{28,12},{1,17},{... | collective-permute-start | bytes 589832 | tf_op jit(solution)/shard_map/ppermute | solution.py:362
  185.7 0.4 collective-permute-start.14
  186.1 17.3 %shard_map.109 = (f32[3,1024,768]{2,1,0:T(8,128)}, f32[4,96,768]{2,1,0:T(8,128)}, bf16[4,96,768]{2,1,0:T(8,128)(2,1)}) custom-call(bf16[2,512,512]{2,1,0:T(8,128)(2,1)} %get-tuple-element.67.big, f32[3,1024,768]{2,1,0:T(8,128)} %get-tuple-element.55.sloped, f32[768,768]{1,0:T(8,128)} %bitcast.34, bf16[3,1024,768]{2,1,0:T(8,128)(2,1)} %bitcast.32, ...), custom_call_target="tpu_custom_call" | custom-call | flops 1000 | bytes 1000 | tf_op jit(solution)/shard_map/pallas_call | solution.py:300
  203.5 1.1 pad_maximum_fusion
  204.7 1.0 reverse_select_fusion
  205.7 0.5 collective-permute-start.17
  206.2 1.5 convert_add_fusion.1
  207.8 0.6 collective-permute-start.16
  208.4 3.5 %collective-permute-start.18 = (bf16[4,24,768]{2,1,0:T(8,128)(2,1)S(1)}, bf16[4,24,768]{2,1,0:T(8,128)(2,1)S(1)}, u32[]{:S(2)}, u32[]{:S(2)}) collective-permute-start(bf16[4,24,768]{2,1,0:T(8,128)(2,1)S(1)} %get-tuple-element.94), channel_id=1, source_target_pairs={{0,16},{4,20},{8,24},{12,28},{16,0},{20,4},{24,8},{28,12},{1,17},{... | collective-permute-start | bytes 442376 | tf_op jit(solution)/shard_map/ppermute | solution.py:362
  211.9 0.4 collective-permute-start.19
  212.3 3.4 %maximum_select_fusion.1 = bf16[1024,768]{1,0:T(8,128)(2,1)} fusion(bf16[512,768]{1,0:T(8,128)(2,1)} %collective-permute-done.17, bf16[512,768]{1,0:T(8,128)(2,1)} %bitcast.21, pred[]{:T(512)S(6)} %eq.44), kind=kLoop, calls=%fused_computation.2 | loop fusion | flops 7077888 | bytes 3145729 | tf_op jit(solution)/shard_map/jit(_where)/select_n | solution.py:393
  215.7 0.6 collective-permute-done.16
  216.2 6.7 %collective-permute-done.18 = bf16[4,24,768]{2,1,0:T(8,128)(2,1)S(1)} collective-permute-done((bf16[4,24,768]{2,1,0:T(8,128)(2,1)S(1)}, bf16[4,24,768]{2,1,0:T(8,128)(2,1)S(1)}, u32[]{:S(2)}, u32[]{:S(2)}) %collective-permute-start.18) | collective-permute-done | bytes 147488 | tf_op jit(solution)/shard_map/ppermute | solution.py:362
  223.0 0.7 constant_dynamic-slice_fusion.2
  223.7 1.7 collective-permute-start.20
  225.4 1.5 collective-permute-start.21
  227.2 1.6 copy-done
  228.8 4.3 %all-to-all-start.3 = ((bf16[4,3,2,128,256]{4,3,2,1,0:T(8,128)(2,1)}), bf16[4,3,2,128,256]{4,3,2,1,0:T(8,128)(2,1)}, u32[]{:S(2)}, u32[]{:S(2)}) async-start(bf16[4,3,2,128,256]{4,3,2,1,0:T(8,128)(2,1)} %get-tuple-element.86), calls=%async_computation.3 | async-start | bytes 3145728 | tf_op jit(solution)/shard_map/all_to_all | solution.py:367
  233.2 1.0 add_add_fusion
  234.2 2.9 %collective-permute-start.23 = (f32[1,24,768]{2,1,0:T(8,128)S(1)}, f32[1,24,768]{2,1,0:T(8,128)S(1)}, u32[]{:S(2)}, u32[]{:S(2)}) collective-permute-start(f32[1,24,768]{2,1,0:T(8,128)S(1)} %add_add_fusion), channel_id=1, source_target_pairs={{0,8},{4,12},{8,0},{12,4},{16,24},{20,28},{24,16},{28,20},{1,9},{5... | collective-permute-start | bytes 221192 | tf_op jit(solution)/shard_map/ppermute | solution.py:362
  237.0 1.0 collective-permute-start.24
  238.1 1.4 collective-permute-start.25
  239.5 6.2 %shard_map.110.refs_1_ = bf16[3,1024,768]{2,1,0:T(8,128)(2,1)} custom-call(bf16[2,512,512]{2,1,0:T(8,128)(2,1)} %get-tuple-element.48.big, f32[3,1024,768]{2,1,0:T(8,128)} %get-tuple-element.70.other, bf16[4,3,2,128,512]{4,3,2,1,0:T(8,128)(2,1)} %copy-done), custom_call_target="tpu_custom_call" | custom-call | flops 1000 | bytes 1000 | tf_op jit(solution)/shard_map/pallas_call | solution.py:344
  245.9 1.6 collective-permute-done.26
  247.4 0.9 maximum_select_fusion.3
  248.3 2.1 all-to-all-done.3.refs_0_
  250.4 4.1 %shard_map.111 = bf16[3,1024,768]{2,1,0:T(8,128)(2,1)} custom-call(bf16[2,512,512]{2,1,0:T(8,128)(2,1)} %get-tuple-element.48.big, f32[3,1024,768]{2,1,0:T(8,128)} %get-tuple-element.70.other, bf16[4,3,2,128,256]{4,3,2,1,0:T(8,128)(2,1)} %all-to-all-done.3.refs_0_, bf16[3,1024,768]{2,1,0:T(8,128)(2,1)} %shard_map.110.refs_1_), custom_call_target="tpu_custom_call", output_to_operand_aliasing={{}: (3, {})} | custom-call | flops 1000 | bytes 1000 | tf_op jit(solution)/shard_map/pallas_call | solution.py:344
  (53 shorter events, 1.9 us)
Async XLA Ops:
  6.2 9.6 %copy-start.6 = (bf16[16,64,64]{2,1,0:T(8,128)(2,1)S(1)}, bf16[16,64,64]{2,1,0:T(8,128)(2,1)}, u32[]{:S(2)}) copy-start(bf16[16,64,64]{2,1,0:T(8,128)(2,1)} %right_out.1) | copy-start | bytes 393220
  6.2 16.4 %collective-permute-start.2 = (f32[48,768]{1,0:T(8,128)S(1)}, f32[48,768]{1,0:T(8,128)S(1)}, u32[]{:S(2)}, u32[]{:S(2)}) collective-permute-start(f32[48,768]{1,0:T(8,128)S(1)} %get-tuple-element.99), channel_id=1, source_target_pairs={{0,3},{1,2},{2,1},{3,0},{4,7},{5,6},{6,5},{7,4},{8,11},{9,10},{10,... | collective-permute-start | bytes 442376 | tf_op jit(solution)/shard_map/ppermute | solution.py:362
  10.2 12.4 %collective-permute-start = (f32[48,768]{1,0:T(8,128)S(1)}, f32[48,768]{1,0:T(8,128)S(1)}, u32[]{:S(2)}, u32[]{:S(2)}) collective-permute-start(f32[48,768]{1,0:T(8,128)S(1)} %get-tuple-element.99), channel_id=1, source_target_pairs={{0,1},{1,0},{2,3},{3,2},{4,5},{5,4},{6,7},{7,6},{8,9},{9,8},{10,11... | collective-permute-start | bytes 442376 | tf_op jit(solution)/shard_map/ppermute | solution.py:362
  10.7 11.9 %collective-permute-start.1 = (f32[48,768]{1,0:T(8,128)S(1)}, f32[48,768]{1,0:T(8,128)S(1)}, u32[]{:S(2)}, u32[]{:S(2)}) collective-permute-start(f32[48,768]{1,0:T(8,128)S(1)} %get-tuple-element.99), channel_id=1, source_target_pairs={{0,2},{1,3},{2,0},{3,1},{4,6},{5,7},{6,4},{7,5},{8,10},{9,11},{10,... | collective-permute-start | bytes 442376 | tf_op jit(solution)/shard_map/ppermute | solution.py:362
  10.8 59.4 %all-to-all-start = ((bf16[4,3,2,128,768]{4,3,2,1,0:T(8,128)(2,1)}), bf16[4,3,2,128,768]{4,3,2,1,0:T(8,128)(2,1)}, u32[]{:S(2)}, u32[]{:S(2)}) async-start(bf16[4,3,2,128,768]{4,3,2,1,0:T(8,128)(2,1)} %shard_map.103), calls=%async_computation | async-start | bytes 9437184 | tf_op jit(solution)/shard_map/all_to_all | solution.py:367
  15.8 1.2 copy-start.7
  22.8 14.6 %collective-permute-start.3 = (f32[4,48,768]{2,1,0:T(8,128)S(1)}, f32[4,48,768]{2,1,0:T(8,128)S(1)}, u32[]{:S(2)}, u32[]{:S(2)}) collective-permute-start(f32[4,48,768]{2,1,0:T(8,128)S(1)} %bitcast.44), channel_id=1, source_target_pairs={{0,8},{4,12},{8,0},{12,4},{16,24},{20,28},{24,16},{28,20},{1,9},{5... | collective-permute-start | bytes 1769480 | tf_op jit(solution)/shard_map/ppermute | solution.py:362
  37.5 2.9 %collective-permute-start.4 = (f32[4,96,768]{2,1,0:T(8,128)S(1)}, f32[4,96,768]{2,1,0:T(8,128)S(1)}, u32[]{:S(2)}, u32[]{:S(2)}) collective-permute-start(f32[4,96,768]{2,1,0:T(8,128)S(1)} %maximum_select_fusion.2), channel_id=1, source_target_pairs={{0,4},{4,0},{8,12},{12,8},{16,20},{20,16},{24,28},{28,24},{1,5},{5... | collective-permute-start | bytes 3538952 | tf_op jit(solution)/shard_map/ppermute | solution.py:362
  58.7 36.7 %collective-permute-start.5 = (bf16[3,2,128,768]{3,2,1,0:T(8,128)(2,1)}, bf16[3,2,128,768]{3,2,1,0:T(8,128)(2,1)S(1)}, u32[]{:S(2)}, u32[]{:S(2)}) collective-permute-start(bf16[3,2,128,768]{3,2,1,0:T(8,128)(2,1)} %get-tuple-element.61), channel_id=1, source_target_pairs={{0,1},{1,0},{2,3},{3,2},{4,5},{5,4},{6,7},{7,6},{8,9},{9,8},{10,11... | collective-permute-start | bytes 3538952 | tf_op jit(solution)/shard_map/ppermute | solution.py:362
  60.4 35.1 %collective-permute-start.6 = (bf16[3,2,128,768]{3,2,1,0:T(8,128)(2,1)}, bf16[3,2,128,768]{3,2,1,0:T(8,128)(2,1)S(1)}, u32[]{:S(2)}, u32[]{:S(2)}) collective-permute-start(bf16[3,2,128,768]{3,2,1,0:T(8,128)(2,1)} %get-tuple-element.62), channel_id=1, source_target_pairs={{0,2},{1,3},{2,0},{3,1},{4,6},{5,7},{6,4},{7,5},{8,10},{9,11},{10,... | collective-permute-start | bytes 3538952 | tf_op jit(solution)/shard_map/ppermute | solution.py:362
  61.8 58.1 %collective-permute-start.7 = (bf16[3,2,128,768]{3,2,1,0:T(8,128)(2,1)}, bf16[3,2,128,768]{3,2,1,0:T(8,128)(2,1)S(1)}, u32[]{:S(2)}, u32[]{:S(2)}) collective-permute-start(bf16[3,2,128,768]{3,2,1,0:T(8,128)(2,1)} %get-tuple-element.63), channel_id=1, source_target_pairs={{0,3},{1,2},{2,1},{3,0},{4,7},{5,6},{6,5},{7,4},{8,11},{9,10},{10,... | collective-permute-start | bytes 3538952 | tf_op jit(solution)/shard_map/ppermute | solution.py:362
  95.4 24.5 %copy-start.1 = (bf16[3,2,128,768]{3,2,1,0:T(8,128)(2,1)}, bf16[3,2,128,768]{3,2,1,0:T(8,128)(2,1)S(1)}, u32[]{:S(2)}) copy-start(bf16[3,2,128,768]{3,2,1,0:T(8,128)(2,1)S(1)} %collective-permute-done.5.refs_1_) | copy-start | bytes 3538948
  95.4 24.5 %copy-start.2 = (bf16[3,2,128,768]{3,2,1,0:T(8,128)(2,1)}, bf16[3,2,128,768]{3,2,1,0:T(8,128)(2,1)S(1)}, u32[]{:S(2)}) copy-start(bf16[3,2,128,768]{3,2,1,0:T(8,128)(2,1)S(1)} %collective-permute-done.6.refs_2_) | copy-start | bytes 3538948
  119.9 1.0 copy-start.3
  120.9 56.8 %all-to-all-start.1 = ((bf16[4,3,2,128,768]{4,3,2,1,0:T(8,128)(2,1)}), bf16[4,3,2,128,768]{4,3,2,1,0:T(8,128)(2,1)}, u32[]{:S(2)}, u32[]{:S(2)}) async-start(bf16[4,3,2,128,768]{4,3,2,1,0:T(8,128)(2,1)} %get-tuple-element.69), calls=%async_computation.1 | async-start | bytes 9437184 | tf_op jit(solution)/shard_map/all_to_all | solution.py:367
  133.5 5.6 %copy-start.5 = (f32[2,512,512]{2,1,0:T(8,128)S(1)}, f32[2,512,512]{2,1,0:T(8,128)}, u32[]{:S(2)}) copy-start(f32[2,512,512]{2,1,0:T(8,128)} %get-tuple-element.64) | copy-start | bytes 6291460
  141.6 2.6 %collective-permute-start.8 = (bf16[512,768]{1,0:T(8,128)(2,1)}, bf16[512,768]{1,0:T(8,128)(2,1)}, u32[]{:S(2)}, u32[]{:S(2)}) collective-permute-start(bf16[512,768]{1,0:T(8,128)(2,1)} %dynamic-slice_convert_fusion), channel_id=1, source_target_pairs={{0,4},{4,0},{8,12},{12,8},{16,20},{20,16},{24,28},{28,24},{1,5},{5... | collective-permute-start | bytes 2359304 | tf_op jit(solution)/shard_map/ppermute | solution.py:362
  145.5 1.1 copy-start.4
  146.7 17.2 %collective-permute-start.10 = (bf16[128,768]{1,0:T(8,128)(2,1)S(1)}, bf16[128,768]{1,0:T(8,128)(2,1)S(1)}, u32[]{:S(2)}, u32[]{:S(2)}) collective-permute-start(bf16[128,768]{1,0:T(8,128)(2,1)S(1)} %get-tuple-element.91), channel_id=1, source_target_pairs={{0,16},{4,20},{8,24},{12,28},{16,0},{20,4},{24,8},{28,12},{1,17},{... | collective-permute-start | bytes 589832 | tf_op jit(solution)/shard_map/ppermute | solution.py:362
  149.5 14.4 %collective-permute-start.11 = (bf16[128,768]{1,0:T(8,128)(2,1)S(1)}, bf16[128,768]{1,0:T(8,128)(2,1)S(1)}, u32[]{:S(2)}, u32[]{:S(2)}) collective-permute-start(bf16[128,768]{1,0:T(8,128)(2,1)S(1)} %get-tuple-element.90), channel_id=1, source_target_pairs={{0,24},{4,28},{8,16},{12,20},{16,8},{20,12},{24,0},{28,4},{1,25},{... | collective-permute-start | bytes 589832 | tf_op jit(solution)/shard_map/ppermute | solution.py:362
  150.8 13.7 %collective-permute-start.9 = (bf16[128,768]{1,0:T(8,128)(2,1)S(1)}, bf16[128,768]{1,0:T(8,128)(2,1)S(1)}, u32[]{:S(2)}, u32[]{:S(2)}) collective-permute-start(bf16[128,768]{1,0:T(8,128)(2,1)S(1)} %get-tuple-element.89), channel_id=1, source_target_pairs={{0,8},{4,12},{8,0},{12,4},{16,24},{20,28},{24,16},{28,20},{1,9},{5... | collective-permute-start | bytes 589832 | tf_op jit(solution)/shard_map/ppermute | solution.py:362
  177.7 49.4 %all-to-all-start.2 = ((bf16[4,3,2,128,512]{4,3,2,1,0:T(8,128)(2,1)}), bf16[4,3,2,128,512]{4,3,2,1,0:T(8,128)(2,1)S(1)}, u32[]{:S(2)}, u32[]{:S(2)}) async-start(bf16[4,3,2,128,512]{4,3,2,1,0:T(8,128)(2,1)} %get-tuple-element.74), calls=%async_computation.2 | async-start | bytes 6291456 | tf_op jit(solution)/shard_map/all_to_all | solution.py:367
  181.6 21.8 %collective-permute-start.12 = (bf16[128,768]{1,0:T(8,128)(2,1)S(1)}, bf16[128,768]{1,0:T(8,128)(2,1)S(1)}, u32[]{:S(2)}, u32[]{:S(2)}) collective-permute-start(bf16[128,768]{1,0:T(8,128)(2,1)S(1)} %add_convert_fusion), channel_id=1, source_target_pairs={{0,8},{4,12},{8,0},{12,4},{16,24},{20,28},{24,16},{28,20},{1,9},{5... | collective-permute-start | bytes 589832 | tf_op jit(solution)/shard_map/ppermute | solution.py:362
  183.1 20.3 %collective-permute-start.13 = (bf16[128,768]{1,0:T(8,128)(2,1)S(1)}, bf16[128,768]{1,0:T(8,128)(2,1)}, u32[]{:S(2)}, u32[]{:S(2)}) collective-permute-start(bf16[128,768]{1,0:T(8,128)(2,1)S(1)} %add_convert_fusion), channel_id=1, source_target_pairs={{0,16},{4,20},{8,24},{12,28},{16,0},{20,4},{24,8},{28,12},{1,17},{... | collective-permute-start | bytes 589832 | tf_op jit(solution)/shard_map/ppermute | solution.py:362
  185.7 17.7 %collective-permute-start.14 = (bf16[128,768]{1,0:T(8,128)(2,1)S(1)}, bf16[128,768]{1,0:T(8,128)(2,1)}, u32[]{:S(2)}, u32[]{:S(2)}) collective-permute-start(bf16[128,768]{1,0:T(8,128)(2,1)S(1)} %add_convert_fusion), channel_id=1, source_target_pairs={{0,24},{4,28},{8,16},{12,20},{16,8},{20,12},{24,0},{28,4},{1,25},{... | collective-permute-start | bytes 589832 | tf_op jit(solution)/shard_map/ppermute | solution.py:362
  203.4 2.8 %collective-permute-start.15 = (bf16[4,96,768]{2,1,0:T(8,128)(2,1)}, bf16[4,96,768]{2,1,0:T(8,128)(2,1)}, u32[]{:S(2)}, u32[]{:S(2)}) collective-permute-start(bf16[4,96,768]{2,1,0:T(8,128)(2,1)} %get-tuple-element.77), channel_id=1, source_target_pairs={{0,4},{4,0},{8,12},{12,8},{16,20},{20,16},{24,28},{28,24},{1,5},{5... | collective-permute-start | bytes 1769480 | tf_op jit(solution)/shard_map/ppermute | solution.py:362
  205.7 6.5 %collective-permute-start.17 = (bf16[512,768]{1,0:T(8,128)(2,1)}, bf16[512,768]{1,0:T(8,128)(2,1)}, u32[]{:S(2)}, u32[]{:S(2)}) collective-permute-start(bf16[512,768]{1,0:T(8,128)(2,1)} %bitcast.21), channel_id=1, source_target_pairs={{0,4},{4,0},{8,12},{12,8},{16,20},{20,16},{24,28},{28,24},{1,5},{5... | collective-permute-start | bytes 2359304 | tf_op jit(solution)/shard_map/ppermute | solution.py:362
  207.8 8.4 %collective-permute-start.16 = (bf16[4,24,768]{2,1,0:T(8,128)(2,1)S(1)}, bf16[4,24,768]{2,1,0:T(8,128)(2,1)S(1)}, u32[]{:S(2)}, u32[]{:S(2)}) collective-permute-start(bf16[4,24,768]{2,1,0:T(8,128)(2,1)S(1)} %get-tuple-element.92), channel_id=1, source_target_pairs={{0,8},{4,12},{8,0},{12,4},{16,24},{20,28},{24,16},{28,20},{1,9},{5... | collective-permute-start | bytes 442376 | tf_op jit(solution)/shard_map/ppermute | solution.py:362
  208.4 14.5 %collective-permute-start.18 = (bf16[4,24,768]{2,1,0:T(8,128)(2,1)S(1)}, bf16[4,24,768]{2,1,0:T(8,128)(2,1)S(1)}, u32[]{:S(2)}, u32[]{:S(2)}) collective-permute-start(bf16[4,24,768]{2,1,0:T(8,128)(2,1)S(1)} %get-tuple-element.94), channel_id=1, source_target_pairs={{0,16},{4,20},{8,24},{12,28},{16,0},{20,4},{24,8},{28,12},{1,17},{... | collective-permute-start | bytes 442376 | tf_op jit(solution)/shard_map/ppermute | solution.py:362
  211.9 11.1 %collective-permute-start.19 = (bf16[4,24,768]{2,1,0:T(8,128)(2,1)S(1)}, bf16[4,24,768]{2,1,0:T(8,128)(2,1)S(1)}, u32[]{:S(2)}, u32[]{:S(2)}) collective-permute-start(bf16[4,24,768]{2,1,0:T(8,128)(2,1)S(1)} %get-tuple-element.93), channel_id=1, source_target_pairs={{0,24},{4,28},{8,16},{12,20},{16,8},{20,12},{24,0},{28,4},{1,25},{... | collective-permute-start | bytes 442376 | tf_op jit(solution)/shard_map/ppermute | solution.py:362
  223.7 9.5 %collective-permute-start.20 = (f32[1,24,768]{2,1,0:T(8,128)}, f32[1,24,768]{2,1,0:T(8,128)}, u32[]{:S(2)}, u32[]{:S(2)}) collective-permute-start(f32[1,24,768]{2,1,0:T(8,128)} %get-tuple-element.95), channel_id=1, source_target_pairs={{0,1},{1,0},{2,3},{3,2},{4,5},{5,4},{6,7},{7,6},{8,9},{9,8},{10,11... | collective-permute-start | bytes 221192 | tf_op jit(solution)/shard_map/ppermute | solution.py:362
  225.4 7.7 %collective-permute-start.21 = (f32[1,24,768]{2,1,0:T(8,128)}, f32[1,24,768]{2,1,0:T(8,128)}, u32[]{:S(2)}, u32[]{:S(2)}) collective-permute-start(f32[1,24,768]{2,1,0:T(8,128)} %get-tuple-element.97), channel_id=1, source_target_pairs={{0,2},{1,3},{2,0},{3,1},{4,6},{5,7},{6,4},{7,5},{8,10},{9,11},{10,... | collective-permute-start | bytes 221192 | tf_op jit(solution)/shard_map/ppermute | solution.py:362
  226.9 6.3 %collective-permute-start.22 = (f32[1,24,768]{2,1,0:T(8,128)S(1)}, f32[1,24,768]{2,1,0:T(8,128)}, u32[]{:S(2)}, u32[]{:S(2)}) collective-permute-start(f32[1,24,768]{2,1,0:T(8,128)S(1)} %get-tuple-element.96), channel_id=1, source_target_pairs={{0,3},{1,2},{2,1},{3,0},{4,7},{5,6},{6,5},{7,4},{8,11},{9,10},{10,... | collective-permute-start | bytes 221192 | tf_op jit(solution)/shard_map/ppermute | solution.py:362
  227.2 1.6 copy-start
  228.8 21.6 %all-to-all-start.3 = ((bf16[4,3,2,128,256]{4,3,2,1,0:T(8,128)(2,1)}), bf16[4,3,2,128,256]{4,3,2,1,0:T(8,128)(2,1)}, u32[]{:S(2)}, u32[]{:S(2)}) async-start(bf16[4,3,2,128,256]{4,3,2,1,0:T(8,128)(2,1)} %get-tuple-element.86), calls=%async_computation.3 | async-start | bytes 3145728 | tf_op jit(solution)/shard_map/all_to_all | solution.py:367
  234.2 11.5 %collective-permute-start.23 = (f32[1,24,768]{2,1,0:T(8,128)S(1)}, f32[1,24,768]{2,1,0:T(8,128)S(1)}, u32[]{:S(2)}, u32[]{:S(2)}) collective-permute-start(f32[1,24,768]{2,1,0:T(8,128)S(1)} %add_add_fusion), channel_id=1, source_target_pairs={{0,8},{4,12},{8,0},{12,4},{16,24},{20,28},{24,16},{28,20},{1,9},{5... | collective-permute-start | bytes 221192 | tf_op jit(solution)/shard_map/ppermute | solution.py:362
  237.0 8.7 %collective-permute-start.24 = (f32[1,24,768]{2,1,0:T(8,128)S(1)}, f32[1,24,768]{2,1,0:T(8,128)S(1)}, u32[]{:S(2)}, u32[]{:S(2)}) collective-permute-start(f32[1,24,768]{2,1,0:T(8,128)S(1)} %add_add_fusion), channel_id=1, source_target_pairs={{0,16},{4,20},{8,24},{12,28},{16,0},{20,4},{24,8},{28,12},{1,17},{... | collective-permute-start | bytes 221192 | tf_op jit(solution)/shard_map/ppermute | solution.py:362
  238.1 7.6 %collective-permute-start.25 = (f32[1,24,768]{2,1,0:T(8,128)S(1)}, f32[1,24,768]{2,1,0:T(8,128)S(1)}, u32[]{:S(2)}, u32[]{:S(2)}) collective-permute-start(f32[1,24,768]{2,1,0:T(8,128)S(1)} %add_add_fusion), channel_id=1, source_target_pairs={{0,24},{4,28},{8,16},{12,20},{16,8},{20,12},{24,0},{28,4},{1,25},{... | collective-permute-start | bytes 221192 | tf_op jit(solution)/shard_map/ppermute | solution.py:362
  245.8 1.6 collective-permute-start.26

commit v4 on v3

--- a/solution.py
+++ b/solution.py
@@ -482,8 +482,8 @@
     )
     returned = exchange(after(third, *back_spread))
 
-    third_width = full // 3
-    parts = ((0, 2 * third_width), (2, third_width))
+    sixth = full // 6
+    parts = ((0, 5 * sixth), (5, sixth))
     back_first, totals = [], []
     for c, wide in parts:
         sent, total = back_middle(

time: 256 us -> 255 us (level)
  other arithmetic: 16.8 us -> 10.7 us
  waiting for transfers between devices: 101 us -> 105 us
    ppermute x27, waiting for transfers between devices: 78.6 us -> 86.4 us  [swap(): return lax.ppermute(value, axis, [(i, i ^ bit) for i in range(size)])]
    all_to_all x4, waiting for transfers between devices: 22.3 us -> 19 us  [exchange(): return [lax.all_to_all(pieces[0], 'seq', 0, 0, tiled=True)]]
  transfers between devices with their start and end apart: 31 -> 31, of which waited for: 13 -> 15; matrix products, arithmetic and copies ran while one was open for 7% -> 5% of each run, Pallas kernels for 27% -> 28%
where the time goes in v4:
time: 255 us; the launch traced here: 254 us
  waiting for transfers between devices  105 us (41%)
  Pallas kernels  80.1 us (31%)
  starting transfers between devices  51.5 us (20%)
  other arithmetic  10.7 us (4%)
  local copies, waits for them, and re-layouts  5.19 us (2%)
    ppermute x27, waiting for transfers between devices, swap(): return lax.ppermute(value, axis, [(i, i ^ bit) for i in range(size)])  86.4 us
    ppermute x27, starting transfers between devices, swap(): return lax.ppermute(value, axis, [(i, i ^ bit) for i in range(size)])  33.1 us
    all_to_all x4, waiting for transfers between devices, exchange(): return [lax.all_to_all(pieces[0], 'seq', 0, 0, tiled=True)]  19 us
    all_to_all x4, starting transfers between devices, exchange(): return [lax.all_to_all(pieces[0], 'seq', 0, 0, tiled=True)]  18.4 us
    pallas_call x1, Pallas kernels, ending(): pl.pallas_call(functools.partial(ending_kernel, devices, len(pieces), sca...  17.3 us
    pallas_call x1, Pallas kernels, gate(): pl.pallas_call(functools.partial(gate_kernel, devices, width), grid=grid,...  16.6 us
    pallas_call x2, Pallas kernels, back_middle(): pl.pallas_call(functools.partial(back_middle_kernel, devices, len(pieces)...  14.7 us
    pallas_call x1, Pallas kernels, middle(): pl.pallas_call(functools.partial(middle_kernel, devices, len(pieces)), gr...  11.3 us
  transfers between devices with their start and end apart: 31, of which 15 were waited for; matrix products, arithmetic and copies ran while one was open for 5% of the time, Pallas kernels for 28%

profile of v4, /device:TPU:0, one launch (start us, length us, event | category | flops | bytes accessed | tf_op | source)
XLA Modules:
  0.0 254.0 jit_solution(6520243175817221424)
XLA Ops:
  0.7 4.7 %shard_map.103 = bf16[4,3,2,128,768]{4,3,2,1,0:T(8,128)(2,1)} custom-call(bf16[16,64,64]{2,1,0:T(8,128)(2,1)} %right_in.3, bf16[3,16,64,768]{3,2,1,0:T(8,128)(2,1)} %bitcast.30), custom_call_target="tpu_custom_call" | custom-call | flops 1000 | bytes 1000 | tf_op jit(solution)/shard_map/pallas_call | solution.py:118
  5.3 0.9 fusion.1
  6.2 4.0 %collective-permute-start.2 = (f32[48,768]{1,0:T(8,128)S(1)}, f32[48,768]{1,0:T(8,128)S(1)}, u32[]{:S(2)}, u32[]{:S(2)}) collective-permute-start(f32[48,768]{1,0:T(8,128)S(1)} %get-tuple-element.99), channel_id=1, source_target_pairs={{0,3},{1,2},{2,1},{3,0},{4,7},{5,6},{6,5},{7,4},{8,11},{9,10},{10,... | collective-permute-start | bytes 442376 | tf_op jit(solution)/shard_map/ppermute | solution.py:362
  10.2 0.5 collective-permute-start
  10.8 4.9 %all-to-all-start = ((bf16[4,3,2,128,768]{4,3,2,1,0:T(8,128)(2,1)}), bf16[4,3,2,128,768]{4,3,2,1,0:T(8,128)(2,1)}, u32[]{:S(2)}, u32[]{:S(2)}) async-start(bf16[4,3,2,128,768]{4,3,2,1,0:T(8,128)(2,1)} %shard_map.103), calls=%async_computation | async-start | bytes 9437184 | tf_op jit(solution)/shard_map/all_to_all | solution.py:367
  15.9 0.2 copy.12
  16.2 0.8 copy.13.right_turned
  17.1 0.8 reverse_select_fusion.8
  17.9 4.8 %shard_map.104 = (bf16[2,512,512]{2,1,0:T(8,128)(2,1)}, bf16[2,512,512]{2,1,0:T(8,128)(2,1)}, bf16[2,512,512]{2,1,0:T(8,128)(2,1)}, bf16[2,512,512]{2,1,0:T(8,12...) custom-call(bf16[16,64,64]{2,1,0:T(8,128)(2,1)} %left_in.1, bf16[16,64,64]{2,1,0:T(8,128)(2,1)} %bitcast.53, ...), custom_call_target="tpu_custom_call" | custom-call | flops 1000 | bytes 1000 | tf_op jit(solution)/shard_map/pallas_call | solution.py:80
  22.9 2.1 collective-permute-start.3
  24.9 12.5 %collective-permute-done.3 = f32[4,48,768]{2,1,0:T(8,128)S(1)} collective-permute-done((f32[4,48,768]{2,1,0:T(8,128)S(1)}, f32[4,48,768]{2,1,0:T(8,128)S(1)}, u32[]{:S(2)}, u32[]{:S(2)}) %collective-permute-start.3) | collective-permute-done | bytes 589856 | tf_op jit(solution)/shard_map/ppermute | solution.py:362
  37.6 2.8 %collective-permute-done.4 = f32[4,96,768]{2,1,0:T(8,128)S(1)} collective-permute-done((f32[4,96,768]{2,1,0:T(8,128)S(1)}, f32[4,96,768]{2,1,0:T(8,128)S(1)}, u32[]{:S(2)}, u32[]{:S(2)}) %collective-permute-start.4) | collective-permute-done | bytes 1179680 | tf_op jit(solution)/shard_map/ppermute | solution.py:362
  40.5 1.6 maximum_select_fusion
  42.1 16.6 %shard_map.105 = (bf16[3,2,128,768]{3,2,1,0:T(8,128)(2,1)}, bf16[3,2,128,768]{3,2,1,0:T(8,128)(2,1)}, bf16[3,2,128,768]{3,2,1,0:T(8,128)(2,1)}, bf16[3,2,128,768]{3,2,1,0:T(8,128)(2,1)}, f32[3,1024,768]{2,1,0:T(8,128)}) custom-call(bf16[16,64,64]{2,1,0:T(8,128)(2,1)} %get-tuple-element.51.small, f32[768,768]{1,0:T(8,128)} %bitcast.33, ...), custom_call_target="tpu_custom_call" | custom-call | flops 1000 | bytes 1000 | tf_op jit(solution)/shard_map/pallas_call | solution.py:249
  58.7 1.6 collective-permute-start.5
  60.3 1.5 collective-permute-start.6
  61.8 0.4 collective-permute-start.7
  62.2 8.1 %all-to-all-done.refs_0_ = bf16[4,3,2,128,768]{4,3,2,1,0:T(8,128)(2,1)} async-done(((bf16[4,3,2,128,768]{4,3,2,1,0:T(8,128)(2,1)}), bf16[4,3,2,128,768]{4,3,2,1,0:T(8,128)(2,1)}, u32[]{:S(2)}, u32[]{:S(2)}) %all-to-all-start) | async-done | bytes 4718624 | tf_op jit(solution)/shard_map/all_to_all | solution.py:367
  70.3 11.3 %shard_map.106 = (bf16[4,3,2,128,768]{4,3,2,1,0:T(8,128)(2,1)}, f32[3,2,512,768]{3,2,1,0:T(8,128)}) custom-call(bf16[16,64,64]{2,1,0:T(8,128)(2,1)} %small, bf16[2,512,512]{2,1,0:T(8,128)(2,1)} %get-tuple-element.53.big, bf16[2,512,768]{2,1,0:T(8,128)(2,1)} %bitcast.36, bf16[4,3,2,128,768]{4,3,2,1,0:T(8,128)(2,1)} %all-to-all-done.refs_0_), custom_call_target="tpu_custom_call" | custom-call | flops 1000 | bytes 1000 | tf_op jit(solution)/shard_map/pallas_call | solution.py:155
  81.5 13.9 %collective-permute-done.5.refs_1_ = bf16[3,2,128,768]{3,2,1,0:T(8,128)(2,1)S(1)} collective-permute-done((bf16[3,2,128,768]{3,2,1,0:T(8,128)(2,1)}, bf16[3,2,128,768]{3,2,1,0:T(8,128)(2,1)S(1)}, u32[]{:S(2)}, u32[]{:S(2)}) %collective-permute-start.5) | collective-permute-done | bytes 1179680 | tf_op jit(solution)/shard_map/ppermute | solution.py:362
  95.4 24.5 %collective-permute-done.7.refs_3_ = bf16[3,2,128,768]{3,2,1,0:T(8,128)(2,1)S(1)} collective-permute-done((bf16[3,2,128,768]{3,2,1,0:T(8,128)(2,1)}, bf16[3,2,128,768]{3,2,1,0:T(8,128)(2,1)S(1)}, u32[]{:S(2)}, u32[]{:S(2)}) %collective-permute-start.7) | collective-permute-done | bytes 1179680 | tf_op jit(solution)/shard_map/ppermute | solution.py:362
  119.9 1.0 copy-done.2
  120.9 4.9 %all-to-all-start.1 = ((bf16[4,3,2,128,768]{4,3,2,1,0:T(8,128)(2,1)}), bf16[4,3,2,128,768]{4,3,2,1,0:T(8,128)(2,1)}, u32[]{:S(2)}, u32[]{:S(2)}) async-start(bf16[4,3,2,128,768]{4,3,2,1,0:T(8,128)(2,1)} %get-tuple-element.69), calls=%async_computation.1 | async-start | bytes 9437184 | tf_op jit(solution)/shard_map/all_to_all | solution.py:367
  125.9 9.9 %shard_map.107 = (bf16[4,3,2,128,640]{4,3,2,1,0:T(8,128)(2,1)}, f32[2,512,640]{2,1,0:T(8,128)}) custom-call(bf16[16,64,64]{2,1,0:T(8,128)(2,1)} %get-tuple-element.65.small, bf16[2,512,512]{2,1,0:T(8,128)(2,1)} %get-tuple-element.59.big, bf16[2,512,768]{2,1,0:T(8,128)(2,1)} %bitcast.37, f32[3,2,512,768]{3,2,1,0:T(8,128)} %get-tuple-element.57.second, ...), custom_call_target="tpu_custom_call" | custom-call | flops 1000 | bytes 1000 | tf_op jit(solution)/shard_map/pallas_call | solution.py:198
  135.7 4.8 %shard_map.108 = (bf16[4,3,2,128,128]{4,3,2,1,0:T(8,128)(2,1)}, f32[2,512,128]{2,1,0:T(8,128)}) custom-call(bf16[16,64,64]{2,1,0:T(8,128)(2,1)} %get-tuple-element.65.small, bf16[2,512,512]{2,1,0:T(8,128)(2,1)} %get-tuple-element.59.big, bf16[2,512,768]{2,1,0:T(8,128)(2,1)} %bitcast.38, f32[3,2,512,768]{3,2,1,0:T(8,128)} %get-tuple-element.57.second, ...), custom_call_target="tpu_custom_call" | custom-call | flops 1000 | bytes 1000 | tf_op jit(solution)/shard_map/pallas_call | solution.py:198
  140.6 1.3 maximum_multiply_fusion
  141.9 1.0 dynamic-slice_convert_fusion
  142.9 2.6 %collective-permute-done.8 = bf16[512,768]{1,0:T(8,128)(2,1)} collective-permute-done((bf16[512,768]{1,0:T(8,128)(2,1)}, bf16[512,768]{1,0:T(8,128)(2,1)}, u32[]{:S(2)}, u32[]{:S(2)}) %collective-permute-start.8) | collective-permute-done | bytes 786464 | tf_op jit(solution)/shard_map/ppermute | solution.py:362
  145.5 1.3 convert_add_fusion
  146.8 1.1 copy-done.3
  148.0 2.8 %collective-permute-start.10 = (bf16[128,768]{1,0:T(8,128)(2,1)S(1)}, bf16[128,768]{1,0:T(8,128)(2,1)S(1)}, u32[]{:S(2)}, u32[]{:S(2)}) collective-permute-start(bf16[128,768]{1,0:T(8,128)(2,1)S(1)} %get-tuple-element.91), channel_id=1, source_target_pairs={{0,16},{4,20},{8,24},{12,28},{16,0},{20,4},{24,8},{28,12},{1,17},{... | collective-permute-start | bytes 589832 | tf_op jit(solution)/shard_map/ppermute | solution.py:362
  150.8 1.3 collective-permute-start.11
  152.1 0.2 collective-permute-start.9
  152.3 12.8 %collective-permute-done.10 = bf16[128,768]{1,0:T(8,128)(2,1)S(1)} collective-permute-done((bf16[128,768]{1,0:T(8,128)(2,1)S(1)}, bf16[128,768]{1,0:T(8,128)(2,1)S(1)}, u32[]{:S(2)}, u32[]{:S(2)}) %collective-permute-start.10) | collective-permute-done | bytes 196640 | tf_op jit(solution)/shard_map/ppermute | solution.py:362
  165.2 0.6 collective-permute-done.9
  165.8 1.1 add_convert_fusion
  166.9 10.9 %all-to-all-done.1.refs_0_ = bf16[4,3,2,128,768]{4,3,2,1,0:T(8,128)(2,1)} async-done(((bf16[4,3,2,128,768]{4,3,2,1,0:T(8,128)(2,1)}), bf16[4,3,2,128,768]{4,3,2,1,0:T(8,128)(2,1)}, u32[]{:S(2)}, u32[]{:S(2)}) %all-to-all-start.1) | async-done | bytes 4718624 | tf_op jit(solution)/shard_map/all_to_all | solution.py:367
  177.7 5.0 %all-to-all-start.2 = ((bf16[4,3,2,128,640]{4,3,2,1,0:T(8,128)(2,1)}), bf16[4,3,2,128,640]{4,3,2,1,0:T(8,128)(2,1)}, u32[]{:S(2)}, u32[]{:S(2)}) async-start(bf16[4,3,2,128,640]{4,3,2,1,0:T(8,128)(2,1)} %get-tuple-element.74), calls=%async_computation.2 | async-start | bytes 7864320 | tf_op jit(solution)/shard_map/all_to_all | solution.py:367
  182.7 1.5 collective-permute-start.12
  184.2 2.6 %collective-permute-start.13 = (bf16[128,768]{1,0:T(8,128)(2,1)S(1)}, bf16[128,768]{1,0:T(8,128)(2,1)S(1)}, u32[]{:S(2)}, u32[]{:S(2)}) collective-permute-start(bf16[128,768]{1,0:T(8,128)(2,1)S(1)} %add_convert_fusion), channel_id=1, source_target_pairs={{0,16},{4,20},{8,24},{12,28},{16,0},{20,4},{24,8},{28,12},{1,17},{... | collective-permute-start | bytes 589832 | tf_op jit(solution)/shard_map/ppermute | solution.py:362
  186.8 0.4 collective-permute-start.14
  187.2 17.3 %shard_map.109 = (f32[3,1024,768]{2,1,0:T(8,128)}, f32[4,96,768]{2,1,0:T(8,128)}, bf16[4,96,768]{2,1,0:T(8,128)(2,1)}) custom-call(bf16[2,512,512]{2,1,0:T(8,128)(2,1)} %get-tuple-element.67.big, f32[3,1024,768]{2,1,0:T(8,128)} %get-tuple-element.55.sloped, f32[768,768]{1,0:T(8,128)} %bitcast.34, bf16[3,1024,768]{2,1,0:T(8,128)(2,1)} %bitcast.32, ...), custom_call_target="tpu_custom_call" | custom-call | flops 1000 | bytes 1000 | tf_op jit(solution)/shard_map/pallas_call | solution.py:300
  205.0 0.6 collective-permute-start.17
  205.5 1.3 collective-permute-done.15
  207.0 0.6 collective-permute-start.16
  207.6 3.5 %collective-permute-start.18 = (bf16[4,24,768]{2,1,0:T(8,128)(2,1)S(1)}, bf16[4,24,768]{2,1,0:T(8,128)(2,1)S(1)}, u32[]{:S(2)}, u32[]{:S(2)}) collective-permute-start(bf16[4,24,768]{2,1,0:T(8,128)(2,1)S(1)} %get-tuple-element.94), channel_id=1, source_target_pairs={{0,16},{4,20},{8,24},{12,28},{16,0},{20,4},{24,8},{28,12},{1,17},{... | collective-permute-start | bytes 442376 | tf_op jit(solution)/shard_map/ppermute | solution.py:362
  211.0 0.4 collective-permute-start.19
  211.4 1.8 maximum_select_fusion.1
  213.3 2.3 collective-permute-done.16
  215.6 6.5 %collective-permute-done.18 = bf16[4,24,768]{2,1,0:T(8,128)(2,1)S(1)} collective-permute-done((bf16[4,24,768]{2,1,0:T(8,128)(2,1)S(1)}, bf16[4,24,768]{2,1,0:T(8,128)(2,1)S(1)}, u32[]{:S(2)}, u32[]{:S(2)}) %collective-permute-start.18) | collective-permute-done | bytes 147488 | tf_op jit(solution)/shard_map/ppermute | solution.py:362
  222.2 1.8 collective-permute-start.20
  224.0 1.5 collective-permute-start.21
  225.5 0.3 collective-permute-start.22
  225.7 3.1 %collective-permute-done.20 = f32[1,24,768]{2,1,0:T(8,128)S(1)} collective-permute-done((f32[1,24,768]{2,1,0:T(8,128)S(1)}, f32[1,24,768]{2,1,0:T(8,128)S(1)}, u32[]{:S(2)}, u32[]{:S(2)}) %collective-permute-start.20) | collective-permute-done | bytes 73760 | tf_op jit(solution)/shard_map/ppermute | solution.py:362
  228.8 1.9 collective-permute-done.22
  230.7 3.0 %collective-permute-start.23 = (f32[1,24,768]{2,1,0:T(8,128)S(1)}, f32[1,24,768]{2,1,0:T(8,128)S(1)}, u32[]{:S(2)}, u32[]{:S(2)}) collective-permute-start(f32[1,24,768]{2,1,0:T(8,128)S(1)} %add_add_fusion), channel_id=1, source_target_pairs={{0,8},{4,12},{8,0},{12,4},{16,24},{20,28},{24,16},{28,20},{1,9},{5... | collective-permute-start | bytes 221192 | tf_op jit(solution)/shard_map/ppermute | solution.py:362
  233.7 1.1 collective-permute-start.24
  234.8 1.4 collective-permute-start.25
  236.2 3.5 %all-to-all-start.3 = ((bf16[4,3,2,128,128]{4,3,2,1,0:T(8,128)(2,1)}), bf16[4,3,2,128,128]{4,3,2,1,0:T(8,128)(2,1)S(1)}, u32[]{:S(2)}, u32[]{:S(2)}) async-start(bf16[4,3,2,128,128]{4,3,2,1,0:T(8,128)(2,1)} %get-tuple-element.86), calls=%async_computation.3 | async-start | bytes 1572864 | tf_op jit(solution)/shard_map/all_to_all | solution.py:367
  239.7 7.5 %shard_map.110.refs_1_ = bf16[3,1024,768]{2,1,0:T(8,128)(2,1)} custom-call(bf16[2,512,512]{2,1,0:T(8,128)(2,1)} %get-tuple-element.48.big, f32[3,1024,768]{2,1,0:T(8,128)} %get-tuple-element.70.other, bf16[4,3,2,128,640]{4,3,2,1,0:T(8,128)(2,1)} %all-to-all-done.2.refs_0_), custom_call_target="tpu_custom_call" | custom-call | flops 1000 | bytes 1000 | tf_op jit(solution)/shard_map/pallas_call | solution.py:344
  247.3 1.6 collective-permute-done.26
  248.9 0.9 maximum_select_fusion.3
  249.8 0.9 copy-done.4
  250.6 3.4 %shard_map.111 = bf16[3,1024,768]{2,1,0:T(8,128)(2,1)} custom-call(bf16[2,512,512]{2,1,0:T(8,128)(2,1)} %get-tuple-element.48.big, f32[3,1024,768]{2,1,0:T(8,128)} %get-tuple-element.70.other, bf16[4,3,2,128,128]{4,3,2,1,0:T(8,128)(2,1)} %copy-done.4, bf16[3,1024,768]{2,1,0:T(8,128)(2,1)} %shard_map.110.refs_1_), custom_call_target="tpu_custom_call", output_to_operand_aliasing={{}: (3, {})} | custom-call | flops 1000 | bytes 1000 | tf_op jit(solution)/shard_map/pallas_call | solution.py:344
  (55 shorter events, 1.6 us)
Async XLA Ops:
  6.2 9.6 %copy-start.7 = (bf16[16,64,64]{2,1,0:T(8,128)(2,1)S(1)}, bf16[16,64,64]{2,1,0:T(8,128)(2,1)}, u32[]{:S(2)}) copy-start(bf16[16,64,64]{2,1,0:T(8,128)(2,1)} %right_out.1) | copy-start | bytes 393220
  6.2 16.4 %collective-permute-start.2 = (f32[48,768]{1,0:T(8,128)S(1)}, f32[48,768]{1,0:T(8,128)S(1)}, u32[]{:S(2)}, u32[]{:S(2)}) collective-permute-start(f32[48,768]{1,0:T(8,128)S(1)} %get-tuple-element.99), channel_id=1, source_target_pairs={{0,3},{1,2},{2,1},{3,0},{4,7},{5,6},{6,5},{7,4},{8,11},{9,10},{10,... | collective-permute-start | bytes 442376 | tf_op jit(solution)/shard_map/ppermute | solution.py:362
  10.2 12.5 %collective-permute-start = (f32[48,768]{1,0:T(8,128)S(1)}, f32[48,768]{1,0:T(8,128)S(1)}, u32[]{:S(2)}, u32[]{:S(2)}) collective-permute-start(f32[48,768]{1,0:T(8,128)S(1)} %get-tuple-element.99), channel_id=1, source_target_pairs={{0,1},{1,0},{2,3},{3,2},{4,5},{5,4},{6,7},{7,6},{8,9},{9,8},{10,11... | collective-permute-start | bytes 442376 | tf_op jit(solution)/shard_map/ppermute | solution.py:362
  10.7 11.9 %collective-permute-start.1 = (f32[48,768]{1,0:T(8,128)S(1)}, f32[48,768]{1,0:T(8,128)S(1)}, u32[]{:S(2)}, u32[]{:S(2)}) collective-permute-start(f32[48,768]{1,0:T(8,128)S(1)} %get-tuple-element.99), channel_id=1, source_target_pairs={{0,2},{1,3},{2,0},{3,1},{4,6},{5,7},{6,4},{7,5},{8,10},{9,11},{10,... | collective-permute-start | bytes 442376 | tf_op jit(solution)/shard_map/ppermute | solution.py:362
  10.8 59.4 %all-to-all-start = ((bf16[4,3,2,128,768]{4,3,2,1,0:T(8,128)(2,1)}), bf16[4,3,2,128,768]{4,3,2,1,0:T(8,128)(2,1)}, u32[]{:S(2)}, u32[]{:S(2)}) async-start(bf16[4,3,2,128,768]{4,3,2,1,0:T(8,128)(2,1)} %shard_map.103), calls=%async_computation | async-start | bytes 9437184 | tf_op jit(solution)/shard_map/all_to_all | solution.py:367
  15.8 1.2 copy-start.8
  22.9 14.6 %collective-permute-start.3 = (f32[4,48,768]{2,1,0:T(8,128)S(1)}, f32[4,48,768]{2,1,0:T(8,128)S(1)}, u32[]{:S(2)}, u32[]{:S(2)}) collective-permute-start(f32[4,48,768]{2,1,0:T(8,128)S(1)} %bitcast.46), channel_id=1, source_target_pairs={{0,8},{4,12},{8,0},{12,4},{16,24},{20,28},{24,16},{28,20},{1,9},{5... | collective-permute-start | bytes 1769480 | tf_op jit(solution)/shard_map/ppermute | solution.py:362
  37.5 2.9 %collective-permute-start.4 = (f32[4,96,768]{2,1,0:T(8,128)S(1)}, f32[4,96,768]{2,1,0:T(8,128)S(1)}, u32[]{:S(2)}, u32[]{:S(2)}) collective-permute-start(f32[4,96,768]{2,1,0:T(8,128)S(1)} %maximum_select_fusion.2), channel_id=1, source_target_pairs={{0,4},{4,0},{8,12},{12,8},{16,20},{20,16},{24,28},{28,24},{1,5},{5... | collective-permute-start | bytes 3538952 | tf_op jit(solution)/shard_map/ppermute | solution.py:362
  58.7 36.7 %collective-permute-start.5 = (bf16[3,2,128,768]{3,2,1,0:T(8,128)(2,1)}, bf16[3,2,128,768]{3,2,1,0:T(8,128)(2,1)S(1)}, u32[]{:S(2)}, u32[]{:S(2)}) collective-permute-start(bf16[3,2,128,768]{3,2,1,0:T(8,128)(2,1)} %get-tuple-element.61), channel_id=1, source_target_pairs={{0,1},{1,0},{2,3},{3,2},{4,5},{5,4},{6,7},{7,6},{8,9},{9,8},{10,11... | collective-permute-start | bytes 3538952 | tf_op jit(solution)/shard_map/ppermute | solution.py:362
  60.3 35.1 %collective-permute-start.6 = (bf16[3,2,128,768]{3,2,1,0:T(8,128)(2,1)}, bf16[3,2,128,768]{3,2,1,0:T(8,128)(2,1)S(1)}, u32[]{:S(2)}, u32[]{:S(2)}) collective-permute-start(bf16[3,2,128,768]{3,2,1,0:T(8,128)(2,1)} %get-tuple-element.62), channel_id=1, source_target_pairs={{0,2},{1,3},{2,0},{3,1},{4,6},{5,7},{6,4},{7,5},{8,10},{9,11},{10,... | collective-permute-start | bytes 3538952 | tf_op jit(solution)/shard_map/ppermute | solution.py:362
  61.8 58.1 %collective-permute-start.7 = (bf16[3,2,128,768]{3,2,1,0:T(8,128)(2,1)}, bf16[3,2,128,768]{3,2,1,0:T(8,128)(2,1)S(1)}, u32[]{:S(2)}, u32[]{:S(2)}) collective-permute-start(bf16[3,2,128,768]{3,2,1,0:T(8,128)(2,1)} %get-tuple-element.63), channel_id=1, source_target_pairs={{0,3},{1,2},{2,1},{3,0},{4,7},{5,6},{6,5},{7,4},{8,11},{9,10},{10,... | collective-permute-start | bytes 3538952 | tf_op jit(solution)/shard_map/ppermute | solution.py:362
  95.4 24.5 %copy-start = (bf16[3,2,128,768]{3,2,1,0:T(8,128)(2,1)}, bf16[3,2,128,768]{3,2,1,0:T(8,128)(2,1)S(1)}, u32[]{:S(2)}) copy-start(bf16[3,2,128,768]{3,2,1,0:T(8,128)(2,1)S(1)} %collective-permute-done.5.refs_1_) | copy-start | bytes 3538948
  95.4 24.5 %copy-start.1 = (bf16[3,2,128,768]{3,2,1,0:T(8,128)(2,1)}, bf16[3,2,128,768]{3,2,1,0:T(8,128)(2,1)S(1)}, u32[]{:S(2)}) copy-start(bf16[3,2,128,768]{3,2,1,0:T(8,128)(2,1)S(1)} %collective-permute-done.6.refs_2_) | copy-start | bytes 3538948
  119.9 1.0 copy-start.2
  120.9 56.8 %all-to-all-start.1 = ((bf16[4,3,2,128,768]{4,3,2,1,0:T(8,128)(2,1)}), bf16[4,3,2,128,768]{4,3,2,1,0:T(8,128)(2,1)}, u32[]{:S(2)}, u32[]{:S(2)}) async-start(bf16[4,3,2,128,768]{4,3,2,1,0:T(8,128)(2,1)} %get-tuple-element.69), calls=%async_computation.1 | async-start | bytes 9437184 | tf_op jit(solution)/shard_map/all_to_all | solution.py:367
  135.7 4.8 %copy-start.5 = (f32[2,512,640]{2,1,0:T(8,128)S(1)}, f32[2,512,640]{2,1,0:T(8,128)}, u32[]{:S(2)}) copy-start(f32[2,512,640]{2,1,0:T(8,128)} %get-tuple-element.64) | copy-start | bytes 7864324
  142.9 2.6 %collective-permute-start.8 = (bf16[512,768]{1,0:T(8,128)(2,1)}, bf16[512,768]{1,0:T(8,128)(2,1)}, u32[]{:S(2)}, u32[]{:S(2)}) collective-permute-start(bf16[512,768]{1,0:T(8,128)(2,1)} %dynamic-slice_convert_fusion), channel_id=1, source_target_pairs={{0,4},{4,0},{8,12},{12,8},{16,20},{20,16},{24,28},{28,24},{1,5},{5... | collective-permute-start | bytes 2359304 | tf_op jit(solution)/shard_map/ppermute | solution.py:362
  146.8 1.1 copy-start.3
  148.0 17.2 %collective-permute-start.10 = (bf16[128,768]{1,0:T(8,128)(2,1)S(1)}, bf16[128,768]{1,0:T(8,128)(2,1)S(1)}, u32[]{:S(2)}, u32[]{:S(2)}) collective-permute-start(bf16[128,768]{1,0:T(8,128)(2,1)S(1)} %get-tuple-element.91), channel_id=1, source_target_pairs={{0,16},{4,20},{8,24},{12,28},{16,0},{20,4},{24,8},{28,12},{1,17},{... | collective-permute-start | bytes 589832 | tf_op jit(solution)/shard_map/ppermute | solution.py:362
  150.8 14.4 %collective-permute-start.11 = (bf16[128,768]{1,0:T(8,128)(2,1)S(1)}, bf16[128,768]{1,0:T(8,128)(2,1)S(1)}, u32[]{:S(2)}, u32[]{:S(2)}) collective-permute-start(bf16[128,768]{1,0:T(8,128)(2,1)S(1)} %get-tuple-element.90), channel_id=1, source_target_pairs={{0,24},{4,28},{8,16},{12,20},{16,8},{20,12},{24,0},{28,4},{1,25},{... | collective-permute-start | bytes 589832 | tf_op jit(solution)/shard_map/ppermute | solution.py:362
  152.1 13.7 %collective-permute-start.9 = (bf16[128,768]{1,0:T(8,128)(2,1)S(1)}, bf16[128,768]{1,0:T(8,128)(2,1)S(1)}, u32[]{:S(2)}, u32[]{:S(2)}) collective-permute-start(bf16[128,768]{1,0:T(8,128)(2,1)S(1)} %get-tuple-element.89), channel_id=1, source_target_pairs={{0,8},{4,12},{8,0},{12,4},{16,24},{20,28},{24,16},{28,20},{1,9},{5... | collective-permute-start | bytes 589832 | tf_op jit(solution)/shard_map/ppermute | solution.py:362
  177.7 53.0 %all-to-all-start.2 = ((bf16[4,3,2,128,640]{4,3,2,1,0:T(8,128)(2,1)}), bf16[4,3,2,128,640]{4,3,2,1,0:T(8,128)(2,1)}, u32[]{:S(2)}, u32[]{:S(2)}) async-start(bf16[4,3,2,128,640]{4,3,2,1,0:T(8,128)(2,1)} %get-tuple-element.74), calls=%async_computation.2 | async-start | bytes 7864320 | tf_op jit(solution)/shard_map/all_to_all | solution.py:367
  182.7 21.8 %collective-permute-start.12 = (bf16[128,768]{1,0:T(8,128)(2,1)S(1)}, bf16[128,768]{1,0:T(8,128)(2,1)S(1)}, u32[]{:S(2)}, u32[]{:S(2)}) collective-permute-start(bf16[128,768]{1,0:T(8,128)(2,1)S(1)} %add_convert_fusion), channel_id=1, source_target_pairs={{0,8},{4,12},{8,0},{12,4},{16,24},{20,28},{24,16},{28,20},{1,9},{5... | collective-permute-start | bytes 589832 | tf_op jit(solution)/shard_map/ppermute | solution.py:362
  184.2 20.3 %collective-permute-start.13 = (bf16[128,768]{1,0:T(8,128)(2,1)S(1)}, bf16[128,768]{1,0:T(8,128)(2,1)S(1)}, u32[]{:S(2)}, u32[]{:S(2)}) collective-permute-start(bf16[128,768]{1,0:T(8,128)(2,1)S(1)} %add_convert_fusion), channel_id=1, source_target_pairs={{0,16},{4,20},{8,24},{12,28},{16,0},{20,4},{24,8},{28,12},{1,17},{... | collective-permute-start | bytes 589832 | tf_op jit(solution)/shard_map/ppermute | solution.py:362
  186.8 17.7 %collective-permute-start.14 = (bf16[128,768]{1,0:T(8,128)(2,1)S(1)}, bf16[128,768]{1,0:T(8,128)(2,1)S(1)}, u32[]{:S(2)}, u32[]{:S(2)}) collective-permute-start(bf16[128,768]{1,0:T(8,128)(2,1)S(1)} %add_convert_fusion), channel_id=1, source_target_pairs={{0,24},{4,28},{8,16},{12,20},{16,8},{20,12},{24,0},{28,4},{1,25},{... | collective-permute-start | bytes 589832 | tf_op jit(solution)/shard_map/ppermute | solution.py:362
  204.5 2.3 collective-permute-start.15
  204.7 2.1 copy-start.6
  205.0 6.5 %collective-permute-start.17 = (bf16[512,768]{1,0:T(8,128)(2,1)S(1)}, bf16[512,768]{1,0:T(8,128)(2,1)S(1)}, u32[]{:S(2)}, u32[]{:S(2)}) collective-permute-start(bf16[512,768]{1,0:T(8,128)(2,1)S(1)} %bitcast.44), channel_id=1, source_target_pairs={{0,4},{4,0},{8,12},{12,8},{16,20},{20,16},{24,28},{28,24},{1,5},{5... | collective-permute-start | bytes 2359304 | tf_op jit(solution)/shard_map/ppermute | solution.py:362
  207.0 8.6 %collective-permute-start.16 = (bf16[4,24,768]{2,1,0:T(8,128)(2,1)S(1)}, bf16[4,24,768]{2,1,0:T(8,128)(2,1)S(1)}, u32[]{:S(2)}, u32[]{:S(2)}) collective-permute-start(bf16[4,24,768]{2,1,0:T(8,128)(2,1)S(1)} %get-tuple-element.92), channel_id=1, source_target_pairs={{0,8},{4,12},{8,0},{12,4},{16,24},{20,28},{24,16},{28,20},{1,9},{5... | collective-permute-start | bytes 442376 | tf_op jit(solution)/shard_map/ppermute | solution.py:362
  207.6 14.5 %collective-permute-start.18 = (bf16[4,24,768]{2,1,0:T(8,128)(2,1)S(1)}, bf16[4,24,768]{2,1,0:T(8,128)(2,1)S(1)}, u32[]{:S(2)}, u32[]{:S(2)}) collective-permute-start(bf16[4,24,768]{2,1,0:T(8,128)(2,1)S(1)} %get-tuple-element.94), channel_id=1, source_target_pairs={{0,16},{4,20},{8,24},{12,28},{16,0},{20,4},{24,8},{28,12},{1,17},{... | collective-permute-start | bytes 442376 | tf_op jit(solution)/shard_map/ppermute | solution.py:362
  211.0 11.0 %collective-permute-start.19 = (bf16[4,24,768]{2,1,0:T(8,128)(2,1)S(1)}, bf16[4,24,768]{2,1,0:T(8,128)(2,1)S(1)}, u32[]{:S(2)}, u32[]{:S(2)}) collective-permute-start(bf16[4,24,768]{2,1,0:T(8,128)(2,1)S(1)} %get-tuple-element.93), channel_id=1, source_target_pairs={{0,24},{4,28},{8,16},{12,20},{16,8},{20,12},{24,0},{28,4},{1,25},{... | collective-permute-start | bytes 442376 | tf_op jit(solution)/shard_map/ppermute | solution.py:362
  222.2 6.7 %collective-permute-start.20 = (f32[1,24,768]{2,1,0:T(8,128)S(1)}, f32[1,24,768]{2,1,0:T(8,128)S(1)}, u32[]{:S(2)}, u32[]{:S(2)}) collective-permute-start(f32[1,24,768]{2,1,0:T(8,128)S(1)} %get-tuple-element.95), channel_id=1, source_target_pairs={{0,1},{1,0},{2,3},{3,2},{4,5},{5,4},{6,7},{7,6},{8,9},{9,8},{10,11... | collective-permute-start | bytes 221192 | tf_op jit(solution)/shard_map/ppermute | solution.py:362
  224.0 4.9 %collective-permute-start.21 = (f32[1,24,768]{2,1,0:T(8,128)S(1)}, f32[1,24,768]{2,1,0:T(8,128)S(1)}, u32[]{:S(2)}, u32[]{:S(2)}) collective-permute-start(f32[1,24,768]{2,1,0:T(8,128)S(1)} %get-tuple-element.97), channel_id=1, source_target_pairs={{0,2},{1,3},{2,0},{3,1},{4,6},{5,7},{6,4},{7,5},{8,10},{9,11},{10,... | collective-permute-start | bytes 221192 | tf_op jit(solution)/shard_map/ppermute | solution.py:362
  225.5 5.3 %collective-permute-start.22 = (f32[1,24,768]{2,1,0:T(8,128)S(1)}, f32[1,24,768]{2,1,0:T(8,128)S(1)}, u32[]{:S(2)}, u32[]{:S(2)}) collective-permute-start(f32[1,24,768]{2,1,0:T(8,128)S(1)} %get-tuple-element.96), channel_id=1, source_target_pairs={{0,3},{1,2},{2,1},{3,0},{4,7},{5,6},{6,5},{7,4},{8,11},{9,10},{10,... | collective-permute-start | bytes 221192 | tf_op jit(solution)/shard_map/ppermute | solution.py:362
  230.7 16.4 %collective-permute-start.23 = (f32[1,24,768]{2,1,0:T(8,128)S(1)}, f32[1,24,768]{2,1,0:T(8,128)S(1)}, u32[]{:S(2)}, u32[]{:S(2)}) collective-permute-start(f32[1,24,768]{2,1,0:T(8,128)S(1)} %add_add_fusion), channel_id=1, source_target_pairs={{0,8},{4,12},{8,0},{12,4},{16,24},{20,28},{24,16},{28,20},{1,9},{5... | collective-permute-start | bytes 221192 | tf_op jit(solution)/shard_map/ppermute | solution.py:362
  233.7 13.4 %collective-permute-start.24 = (f32[1,24,768]{2,1,0:T(8,128)S(1)}, f32[1,24,768]{2,1,0:T(8,128)S(1)}, u32[]{:S(2)}, u32[]{:S(2)}) collective-permute-start(f32[1,24,768]{2,1,0:T(8,128)S(1)} %add_add_fusion), channel_id=1, source_target_pairs={{0,16},{4,20},{8,24},{12,28},{16,0},{20,4},{24,8},{28,12},{1,17},{... | collective-permute-start | bytes 221192 | tf_op jit(solution)/shard_map/ppermute | solution.py:362
  234.8 12.4 %collective-permute-start.25 = (f32[1,24,768]{2,1,0:T(8,128)S(1)}, f32[1,24,768]{2,1,0:T(8,128)S(1)}, u32[]{:S(2)}, u32[]{:S(2)}) collective-permute-start(f32[1,24,768]{2,1,0:T(8,128)S(1)} %add_add_fusion), channel_id=1, source_target_pairs={{0,24},{4,28},{8,16},{12,20},{16,8},{20,12},{24,0},{28,4},{1,25},{... | collective-permute-start | bytes 221192 | tf_op jit(solution)/shard_map/ppermute | solution.py:362
  236.2 13.6 %all-to-all-start.3 = ((bf16[4,3,2,128,128]{4,3,2,1,0:T(8,128)(2,1)}), bf16[4,3,2,128,128]{4,3,2,1,0:T(8,128)(2,1)S(1)}, u32[]{:S(2)}, u32[]{:S(2)}) async-start(bf16[4,3,2,128,128]{4,3,2,1,0:T(8,128)(2,1)} %get-tuple-element.86), calls=%async_computation.3 | async-start | bytes 1572864 | tf_op jit(solution)/shard_map/all_to_all | solution.py:367
  247.2 1.6 collective-permute-start.26
  249.8 0.9 copy-start.4
